TPU v7x, 256 devices: a whole 4x4x8 slice. The times are simulated.
256 devices in a mesh: fsdp: 64 (over z, y, core), tensor: 4 (over x).
Axes of the slice: x: 4, y: 4, z: 8, core: 2. Of those that a mesh axis runs over, the one named last changes fastest.
Arguments:
- momentum: bfloat16 [16384, 26624], P('fsdp', 'tensor'), may hold values from -6 to 6
- q_basis: float32 [256, 26624], P('fsdp', 'tensor'), may hold values from -0.0390625 to 0.0390625
Outputs:
- new_momentum: bfloat16 [16384, 26624], P('fsdp', 'tensor')
- update: bfloat16 [16384, 26624], P('fsdp', 'tensor')
- q_next: float32 [256, 26624], P('fsdp', 'tensor')
All inputs are finite; a program needn't handle non-finite values.
Results may differ from a plain program's by a relative error of at most 0.0073.
Values may be sent and summed in bfloat16 or wider, within the bound.
No kernel may reach another device: no remote copies, remote signals or barrier semaphores. Data moves between devices by JAX's collectives and lax.ppermute only.
A program may use at most 64 MiB of HBM per device.

v0:
```python
import math

import jax
import jax.numpy as jnp
from jax import lax
from jax.experimental import pallas as pl
from jax.experimental.pallas import tpu as pltpu
from jax.sharding import Mesh
from jax.sharding import PartitionSpec as P

momentum_decay = 0.95
f32, bf16 = jnp.float32, jnp.bfloat16
HIGHEST = lax.Precision.HIGHEST
VMEM = pl.BlockSpec(memory_space=pltpu.VMEM)
SMEM = pl.BlockSpec(memory_space=pltpu.SMEM)
ANY = pl.BlockSpec(memory_space=pl.ANY)
BOTH_LAST = (((1,), (1,)), ((), ()))
BOTH_FIRST = (((0,), (0,)), ((), ()))
MIB = 2**20
NZ, NY, NX = 8, 4, 4
PIVOTS = 8
RING_FROM = (0, 1, 3, 2, 2)
AT_Y, AT_CORE, AT_X, FIRST_RANK = range(4)


def ahead(index, by, parts):
    return lax.rem(index + by, parts)


def inverse_factor_kernel(at_ref, own_ref, next_ref, across_ref, last_ref, inverse_ref, work_ref, half_ref, done_ref):
    rank = work_ref.shape[0]
    part = rank // (NX * 2)
    for by, ref in enumerate((own_ref, next_ref, across_ref, last_ref)):
        base = ahead(at_ref[AT_X], by, NX) * 2
        for other in range(2):
            at_core = (at_ref[AT_CORE] + other) % 2
            start = pl.multiple_of((base + at_core) * part, part)
            work_ref[pl.ds(start, part), :] = ref[other * part : (other + 1) * part, :]
    gram = work_ref[...]
    diagonal = lax.broadcasted_iota(jnp.int32, gram.shape, 0) == lax.broadcasted_iota(
        jnp.int32, gram.shape, 1
    )
    ridge = 0.001 * jnp.sum(jnp.where(diagonal, gram, 0.0)) / rank
    work_ref[...] = jnp.where(diagonal, gram + ridge, gram)
    lane = lax.broadcasted_iota(jnp.int32, (1, rank), 1)
    per_y, per_half = NZ * PIVOTS, NZ * PIVOTS // 2
    half = rank // 2
    order = (lane % per_y) // PIVOTS * (NY * PIVOTS) + lane // per_y * PIVOTS + lane % PIVOTS

    def of_half(array, second):
        starts = [y * per_y + second * per_half for y in range(NY)]
        return jnp.concatenate([array[start : start + per_half] for start in starts], axis=0)

    half_ref[...] = of_half(work_ref[...], 0)

    def wide(value):
        return jnp.concatenate([value] * (rank // 128), axis=1)

    steps = range(PIVOTS)

    def eliminate(second, carry):
        for group in range(half // PIVOTS):
            at_z, at_y = divmod(group, NY)
            first_row = at_y * per_half + at_z * PIVOTS
            at = at_y * per_y + at_z * PIVOTS
            block = half_ref[first_row : first_row + PIVOTS, :]
            spread = [jnp.broadcast_to(block[:, at + t : at + t + 1], (PIVOTS, 128)) for t in steps]
            core = [[spread[t][s : s + 1, :] for t in range(s + 1)] for s in steps]
            inside = (lane >= at) & (lane < at + PIVOTS)
            row = [jnp.where(inside, (lane == at + s).astype(f32), block[s : s + 1, :]) for s in steps]
            inverse = [None] * PIVOTS
            ratio = [[None] * PIVOTS for _ in steps]
            for t in steps:
                inverse[t] = 1.0 / core[t][t]
                for s in range(t + 1, PIVOTS):
                    ratio[s][t] = core[s][t] * inverse[t]
                for s in range(t + 1, PIVOTS):
                    for u in range(t + 1, s + 1):
                        core[s][u] = core[s][u] - ratio[s][t] * core[u][t]
                    row[s] = row[s] - wide(ratio[s][t]) * row[t]
            for s in steps:
                done_ref[group * PIVOTS + s : group * PIVOTS + s + 1, :] = row[s] * wide(
                    lax.rsqrt(core[s][s])
                )
            solved = [row[s] * wide(inverse[s]) for s in steps]
            for s in reversed(steps):
                for t in range(s):
                    solved[t] = solved[t] - wide(ratio[s][t]) * solved[s]
            for y in range(NY):
                next_z = at_z + (0 if y > at_y else 1)
                if next_z == NZ // 2:
                    continue
                rows = slice(y * per_half + next_z * PIVOTS, (y + 1) * per_half)
                below = half_ref[rows, :]
                rest = jnp.where(inside, 0.0, below)
                for t in steps:
                    rest = rest - below[:, at + t : at + t + 1] * solved[t]
                half_ref[rows, :] = rest

        @pl.when(second == 0)
        def _():
            done = done_ref[...]
            lower = order <= lax.broadcasted_iota(jnp.int32, (half, rank), 0)
            inverse_ref[:half, :] = jnp.where(lower, done, 0.0)
            done = jnp.where(lower | (order >= half), done, 0.0)
            product = lax.dot_general(
                done, done, BOTH_FIRST, preferred_element_type=f32, precision=HIGHEST
            )
            rest = jnp.where(order < half, 0.0, of_half(work_ref[...], 1)) - of_half(product, 1)
            half_ref[...] = pltpu.roll(rest, rank - per_half, 1)

        @pl.when(second == 1)
        def _():
            inverse_ref[half:, :] = jnp.where(
                order <= lax.broadcasted_iota(jnp.int32, (half, rank), 0) + half,
                pltpu.roll(done_ref[...], per_half, 1),
                0.0,
            )

        return carry

    lax.fori_loop(0, 2, eliminate, 0)


def inverse_factor(at, pieces):
    rank = pieces[0].shape[1]
    return pl.pallas_call(
        inverse_factor_kernel,
        out_shape=jax.ShapeDtypeStruct((rank, rank), f32),
        in_specs=[SMEM] + [VMEM] * 4,
        out_specs=VMEM,
        scratch_shapes=[pltpu.VMEM((rows, rank), f32) for rows in (rank, rank // 2, rank // 2)],
        compiler_params=pltpu.CompilerParams(vmem_limit_bytes=8 * MIB),
    )(at, *pieces)


def project_kernel(at_ref, mine_ref, other_ref, *refs):
    pieces, (out_mine_ref, out_other_ref, basis_ref) = refs[:5], refs[5:]
    per_y = pieces[0].shape[0]
    for n, ref in enumerate(pieces):
        size = ref.shape[0]
        start = ahead(at_ref[AT_Y], RING_FROM[n], NY) * per_y + (size if n == 4 else 0)
        basis_ref[pl.ds(pl.multiple_of(start, size), size), :] = ref[...]
    width = mine_ref.shape[1] // 2
    out_mine_ref[...] = jnp.zeros_like(out_mine_ref)
    out_other_ref[...] = jnp.zeros_like(out_other_ref)

    def add(step, carry):
        columns = pl.ds(pl.multiple_of(step * width, 128), width)
        basis = basis_ref[:, columns]
        for ref, out_ref in ((mine_ref, out_mine_ref), (other_ref, out_other_ref)):
            out_ref[...] += lax.dot_general(
                ref[:, columns], basis, BOTH_LAST, preferred_element_type=f32
            )
        return carry

    lax.fori_loop(0, 2, add, 0)


def project(at, mine, other, pieces):
    rows, cols = mine.shape
    rank = pieces[0].shape[0] * NY
    return pl.pallas_call(
        project_kernel,
        out_shape=[jax.ShapeDtypeStruct((rows, rank), f32)] * 2,
        in_specs=[SMEM] + [VMEM] * 7,
        out_specs=[VMEM, VMEM],
        scratch_shapes=[pltpu.VMEM((rank, cols), bf16)],
        compiler_params=pltpu.CompilerParams(vmem_limit_bytes=12 * MIB),
        cost_estimate=pl.CostEstimate(
            flops=4 * rows * cols * rank, bytes_accessed=6 * rows * cols, transcendentals=0
        ),
    )(at, mine, other, *pieces)


def cross_kernel(at_ref, mine_ref, other_ref, left_mine_ref, left_other_ref, *refs):
    pieces, (terms_ref, whole_ref) = refs[:NY], refs[NY:]
    rows, rank = left_mine_ref.shape
    for n, ref in enumerate((left_mine_ref, left_other_ref)):
        left = ref[...]
        for t in range(3):
            term = left.astype(bf16)
            terms_ref[n * rows : (n + 1) * rows, t * rank : (t + 1) * rank] = term
            left = left - term.astype(f32)
    width = mine_ref.shape[1] // 2

    def multiply(step, carry):
        columns = pl.ds(pl.multiple_of(step * width, 128), width)
        momentum = jnp.concatenate([mine_ref[:, columns], other_ref[:, columns]], axis=0)
        product = lax.dot_general(momentum, terms_ref[...], BOTH_FIRST, preferred_element_type=f32)
        total = (product[:, 2 * rank :] + product[:, rank : 2 * rank]) + product[:, :rank]
        whole_ref[columns, :] = total
        return carry

    lax.fori_loop(0, 2, multiply, 0)
    size = pieces[0].shape[0]
    for by, ref in enumerate(pieces):
        start = pl.multiple_of(ahead(at_ref[AT_Y], by, NY) * size, size)
        ref[...] = whole_ref[pl.ds(start, size), :]


def cross(at, mine, other, left_mine, left_other):
    rows, cols = mine.shape
    rank = left_mine.shape[1]
    return pl.pallas_call(
        cross_kernel,
        out_shape=[jax.ShapeDtypeStruct((cols // NY, rank), f32)] * NY,
        in_specs=[SMEM] + [VMEM] * 4,
        out_specs=[VMEM] * NY,
        scratch_shapes=[pltpu.VMEM((2 * rows, 3 * rank), bf16), pltpu.VMEM((cols, rank), f32)],
        compiler_params=pltpu.CompilerParams(vmem_limit_bytes=16 * MIB),
        cost_estimate=pl.CostEstimate(
            flops=12 * rows * cols * rank, bytes_accessed=4 * rows * cols + 8 * cols * rank, transcendentals=0
        ),
    )(at, mine, other, left_mine, left_other)


def finish_kernel(scaling, at_ref, momentum_ref, solved_ref, squares_ref, *refs):
    pieces = refs[:10]
    new_momentum_ref, update_ref, q_next_ref, right_ref, left_ref, inverse_ref, semaphores = refs[10:]
    rows, rank = solved_ref.shape
    step = pl.program_id(0)
    width = momentum_ref.shape[1]
    shard_rank = q_next_ref.shape[0]
    size = pieces[0].shape[0]

    @pl.when(step == 0)
    def _():
        copies = []
        for n, ref in enumerate(pieces):
            side = at_ref[AT_CORE] if n < 5 else 1 - at_ref[AT_CORE]
            start = (side * NY + ahead(at_ref[AT_Y], RING_FROM[n % 5], NY)) * size
            start = pl.multiple_of(start + (ref.shape[0] if n % 5 == 4 else 0), 16)
            copy = pltpu.make_async_copy(
                ref, right_ref.at[pl.ds(start, ref.shape[0]), :], semaphores.at[n]
            )
            copy.start()
            copies.append(copy)
        solved = solved_ref[...]
        squares = jnp.sum(squares_ref[...], axis=0, keepdims=True)
        inverse_lengths = lax.rsqrt(squares + 1e-06)
        left_ref[:rows, :] = solved.astype(bf16)
        left_ref[rows : 2 * rows, :] = (solved * (scaling * inverse_lengths)).astype(bf16)
        wanted = lax.broadcasted_iota(jnp.int32, (16, rank), 0) + at_ref[FIRST_RANK]
        picked = jnp.where(wanted == lax.broadcasted_iota(jnp.int32, (16, rank), 1), 1.0, 0.0)
        left_ref[2 * rows :, :] = picked.astype(bf16)
        own = jnp.sum(picked * inverse_lengths, axis=1, keepdims=True)
        inverse_ref[...] = jnp.broadcast_to(own, inverse_ref.shape)
        for copy in copies:
            copy.wait()

    right = right_ref[pl.ds(pl.multiple_of(step * width, width), width), :]
    product = lax.dot_general(left_ref[...], right, BOTH_LAST, preferred_element_type=f32)
    momentum = momentum_ref[...].astype(f32)
    new_momentum_ref[...] = (momentum - (1.0 - momentum_decay) * product[:rows]).astype(bf16)
    update_ref[...] = product[rows : 2 * rows].astype(bf16)
    q_next_ref[...] = (
        product[2 * rows : 2 * rows + shard_rank] * inverse_ref[:shard_rank, :1]
    )


def finish(at, momentum, solved, squares, pieces, scaling, shard_rank):
    rows, cols = momentum.shape
    rank = solved.shape[1]
    width = cols // 4
    columns = pl.BlockSpec((rows, width), lambda i: (0, i))
    out = jax.ShapeDtypeStruct((rows, cols), bf16)
    return pl.pallas_call(
        lambda *refs: finish_kernel(scaling, *refs),
        out_shape=[out, out, jax.ShapeDtypeStruct((shard_rank, cols), f32)],
        grid=(4,),
        in_specs=[
            SMEM,
            columns,
            pl.BlockSpec(solved.shape, lambda i: (0, 0)),
            pl.BlockSpec(squares.shape, lambda i: (0, 0)),
        ]
        + [ANY] * 10,
        out_specs=[columns, columns, pl.BlockSpec((shard_rank, width), lambda i: (0, i))],
        scratch_shapes=[
            pltpu.VMEM((cols, rank), bf16),
            pltpu.VMEM((2 * rows + 16, rank), bf16),
            pltpu.VMEM((16, 128), f32),
            pltpu.SemaphoreType.DMA((10,)),
        ],
        compiler_params=pltpu.CompilerParams(vmem_limit_bytes=20 * MIB),
        cost_estimate=pl.CostEstimate(
            flops=4 * rows * cols * rank, bytes_accessed=8 * rows * cols, transcendentals=0
        ),
    )(at, momentum, solved, squares, *pieces)


def swap_cores(block):
    return lax.ppermute(block, "c", [(0, 1), (1, 0)])


def from_ahead(block, axis, by, parts=4):
    return lax.ppermute(block, axis, [((i + by) % parts, i) for i in range(parts)])


def sum_four(block, axis):
    one, two, three = (from_ahead(block, axis, by) for by in (1, 2, 3))
    return (block + two) + (one + three)


def ring_of_four(block, axis, beside=None):
    middle = block.shape[0] // 2
    one, three = from_ahead(block, axis, 1), from_ahead(block, axis, 3)
    one, three, beside = lax.optimization_barrier((one, three, beside))
    across = (from_ahead(three[:middle], axis, 3), from_ahead(one[middle:], axis, 1))
    return (block, one, three) + across, beside


def gather(block, axes, parts):
    copies = jnp.broadcast_to(block[None], (parts,) + block.shape)
    return lax.all_to_all(copies, axes, 0, 0)


def scatter_sum(block, axes, parts):
    pieces = block.reshape((parts, block.shape[0] // parts) + block.shape[1:])
    return jnp.sum(lax.all_to_all(pieces, axes, 0, 0).astype(f32), axis=0)


def per_device(momentum, q_basis):
    rows, cols = momentum.shape
    half = cols // 2
    shard_rank = q_basis.shape[0]
    rank = shard_rank * NZ * NY * 2
    core, at_x, at_y = lax.axis_index("c"), lax.axis_index("x"), lax.axis_index("y")
    position = (lax.axis_index("z") * NY + at_y) * 2 + core
    at = jnp.stack([at_y, core, at_x, position * shard_rank]).astype(jnp.int32)

    def columns(array, of_core):
        return lax.dynamic_slice_in_dim(array, of_core * half, half, 1)

    basis_half = q_basis.astype(bf16)
    basis_own = columns(basis_half, core)
    basis_other = swap_cores(columns(basis_half, 1 - core))
    basis_chip = jnp.concatenate(
        [jnp.where(core == 0, basis_own, basis_other), jnp.where(core == 0, basis_other, basis_own)]
    )
    later, basis_chip = lax.optimization_barrier((momentum, basis_chip))
    mine = columns(later, core)
    other = swap_cores(columns(later, 1 - core))

    basis_z = gather(basis_chip, "z", NZ).reshape(rank // NY, half)
    basis, other = ring_of_four(basis_z, "y", other)
    proj_mine, proj_other = project(at, mine, other, basis)
    projected = sum_four(proj_mine + swap_cores(proj_other), "x")

    gram_own = jnp.dot(projected.T, projected, preferred_element_type=f32, precision=HIGHEST)
    part = rank // (NX * 2)

    def gram_part(of_core):
        return lax.dynamic_slice_in_dim(gram_own, (at_x * 2 + of_core) * part, part, 0)

    gram_rows = sum_four(gram_part(core) + swap_cores(gram_part(1 - core)), "y")
    gram_rows = jnp.sum(gather(gram_rows, "z", NZ), axis=0)
    gram_chip = jnp.concatenate([gram_rows, swap_cores(gram_rows)])
    inverse = inverse_factor(
        at, [gram_chip] + [from_ahead(gram_chip, "x", by) for by in (1, 2, 3)]
    )

    crossed = cross(at, mine, other, projected, swap_cores(projected))
    right = crossed[0] + sum(from_ahead(crossed[by], "y", NY - by) for by in (1, 2, 3))

    def whiten(array):
        return lax.dot_general(
            array, inverse, BOTH_LAST, preferred_element_type=f32, precision=HIGHEST
        )

    solved = whiten(projected)
    right = scatter_sum(whiten(right).astype(bf16), "z", NZ).astype(bf16)
    right = gather(right, "z", NZ).reshape(half // NY, rank)
    squares = jnp.sum(jnp.square(right.astype(f32)), axis=0, keepdims=True)
    squares = gather(squares, ("y", "c", "x"), NY * 2 * NX).reshape(NY * 2 * NX, rank)
    pieces, squares = ring_of_four(right, "y", squares)
    pieces = pieces + tuple(swap_cores(piece) for piece in pieces)

    total_rows = rows * NZ * NY * 2
    total_cols = cols * NX
    scaling = math.sqrt(total_rows * total_cols / rank)
    return tuple(finish(at, momentum, solved, squares, pieces, scaling, shard_rank))


def solution(mesh):
    split = Mesh(mesh.devices.reshape(NZ, NY, 2, NX), ("z", "y", "c", "x"))
    spec = P(("z", "y", "c"), "x")
    return jax.shard_map(
        per_device,
        mesh=split,
        in_specs=(spec, spec),
        out_specs=(spec, spec, spec),
        check_vma=False,
    )
```

profile of v0, /device:TPU:1, one launch (start us, length us, event | category | flops | bytes accessed | tf_op | source)
XLA Modules:
  0.0 203.7 jit_solution(11525763836602733401)
XLA Ops:
  0.6 0.9 convert_element_type.12
  1.6 3.3 %collective-permute-start = (bf16[4,3328]{1,0:T(4,128)(2,1)S(1)}, bf16[4,3328]{1,0:T(4,128)(2,1)S(1)}, u32[]{:S(2)}, u32[]{:S(2)}) collective-permute-start(bf16[4,3328]{1,0:T(4,128)(2,1)S(1)} %constant_dynamic-slice_fusion.3), channel_id=1, source_target_pairs={{0,4},{4,0},{1,5},{5,1},{2,6},{6,2},{3,7},{7,3},{8,12},{12,8},{9,1... | collective-permute-start | bytes 79880 | tf_op jit(solution)/shard_map/ppermute | solution.py:294
  5.8 2.2 %constant_dynamic-slice_fusion.1 = (bf16[256,3328]{1,0:T(8,128)(2,1)S(1)}, bf16[256,3328]{1,0:T(8,128)(2,1)S(1)}) fusion(bf16[256,6656]{1,0:T(8,128)(2,1)} %refs_1_.1, s32[]{:T(128)S(6)} %select_n.28, s32[]{:T(128)S(6)} %select_n.27), kind=kLoop, calls=%fused_computation.14 | loop fusion | bytes 6815752 | tf_op jit(solution)/shard_map/dynamic_slice | solution.py:334
  8.5 22.0 %all_to_all.25 = bf16[8,8,3328]{2,1,0:T(8,128)(2,1)S(1)} all-to-all(bf16[8,8,3328]{2,1,0:T(8,128)(2,1)S(1)} %broadcast_in_dim.8), channel_id=1, replica_groups=mesh['z'=8,'y'=4,'c'=2,'x'=4] {'z'}, dimensions={0} | all-to-all | bytes 851968 | tf_op jit(solution)/shard_map/all_to_all | solution.py:316
  30.5 1.3 collective-permute-start.2
  31.8 1.4 collective-permute-start.1
  34.0 8.7 %collective-permute-done.2.refs_2_ = bf16[64,3328]{1,0:T(8,128)(2,1)S(1)} collective-permute-done((bf16[64,3328]{1,0:T(8,128)(2,1)S(1)}, bf16[64,3328]{1,0:T(8,128)(2,1)S(1)}, u32[]{:S(2)}, u32[]{:S(2)}) %collective-permute-start.2) | collective-permute-done | bytes 426016 | tf_op jit(solution)/shard_map/ppermute | solution.py:298
  45.1 1.9 collective-permute-start.5
  47.0 4.2 %collective-permute-done.4.refs_3_ = bf16[32,3328]{1,0:T(8,128)(2,1)} collective-permute-done((bf16[32,3328]{1,0:T(8,128)(2,1)}, bf16[32,3328]{1,0:T(8,128)(2,1)}, u32[]{:S(2)}, u32[]{:S(2)}) %collective-permute-start.4) | collective-permute-done | bytes 213024 | tf_op jit(solution)/shard_map/ppermute | solution.py:298
  51.2 1.0 copy-done.4
  52.2 1.0 copy-done.6
  53.2 1.0 copy-done.8
  54.2 2.5 %shard_map.49 = (f32[256,256]{1,0:T(8,128)S(1)}, f32[256,256]{1,0:T(8,128)S(1)}) custom-call(s32[4]{0:T(128)S(1)} %pad_add_fusion.at_ref.refs_0_, bf16[256,3328]{1,0:T(8,128)(2,1)S(1)} %get-tuple-element.32.mine_ref, bf16[256,3328]{1,0:T(8,128)(2,1)S(1)} %collective-permute-done.3.other_ref, bf16[64,3328]{1,0:T(8,128)(2,1)S(1)} %bitcast.21, ...), custom_call_target="tpu_custom_call" | custom-call | flops 872415232 | bytes 5111808 | tf_op jit(solution)/shard_map/pallas_call | solution.py:163
  56.8 2.4 %collective-permute-start.6 = (f32[256,256]{1,0:T(8,128)S(1)}, f32[256,256]{1,0:T(8,128)S(1)}, u32[]{:S(2)}, u32[]{:S(2)}) collective-permute-start(f32[256,256]{1,0:T(8,128)S(1)} %get-tuple-element.23), channel_id=1, source_target_pairs={{0,4},{4,0},{1,5},{5,1},{2,6},{6,2},{3,7},{7,3},{8,12},{12,8},{9,1... | collective-permute-start | bytes 786440 | tf_op jit(solution)/shard_map/ppermute | solution.py:294
  59.1 1.2 collective-permute-done.6
  60.3 1.3 collective-permute-start.9
  61.6 1.5 collective-permute-start.8
  63.1 1.5 collective-permute-start.7
  64.6 4.5 %collective-permute-done.9 = f32[256,256]{1,0:T(8,128)S(1)} collective-permute-done((f32[256,256]{1,0:T(8,128)S(1)}, f32[256,256]{1,0:T(8,128)S(1)}, u32[]{:S(2)}, u32[]{:S(2)}) %collective-permute-start.9) | collective-permute-done | bytes 262176 | tf_op jit(solution)/shard_map/ppermute | solution.py:298
  69.2 6.6 %collective-permute-done.7 = f32[256,256]{1,0:T(8,128)S(1)} collective-permute-done((f32[256,256]{1,0:T(8,128)S(1)}, f32[256,256]{1,0:T(8,128)S(1)}, u32[]{:S(2)}, u32[]{:S(2)}) %collective-permute-start.7) | collective-permute-done | bytes 262176 | tf_op jit(solution)/shard_map/ppermute | solution.py:298
  76.4 1.3 collective-permute-start.18
  77.8 1.1 collective-permute-done.10
  79.7 2.0 collective-permute-start.12
  81.7 1.1 collective-permute-start.11
  82.8 1.5 copy-done.2
  84.3 5.4 %shard_map.51 = (f32[832,256]{1,0:T(8,128)S(1)}, f32[832,256]{1,0:T(8,128)}, f32[832,256]{1,0:T(8,128)}, f32[832,256]{1,0:T(8,128)}) custom-call(s32[4]{0:T(128)S(1)} %pad_add_fusion.at_ref.refs_0_, bf16[256,3328]{1,0:T(8,128)(2,1)S(1)} %get-tuple-element.32.mine_ref, bf16[256,3328]{1,0:T(8,128)(2,1)S(1)} %copy-done.2, ...), custom_call_target="tpu_custom_call" | custom-call | flops 2617245696 | bytes 10223616 | tf_op jit(solution)/shard_map/pallas_call | solution.py:205
  90.5 1.1 collective-permute-start.20
  91.6 2.0 collective-permute-start.21
  93.7 11.6 %all_to_all.26 = f32[8,32,256]{2,1,0:T(8,128)S(1)} all-to-all(f32[8,32,256]{2,1,0:T(8,128)S(1)} %broadcast_in_dim.9), channel_id=1, replica_groups=mesh['z'=8,'y'=4,'c'=2,'x'=4] {'z'}, dimensions={0} | all-to-all | bytes 524288 | tf_op jit(solution)/shard_map/all_to_all | solution.py:316
  105.3 3.7 %collective-permute-start.14 = (f32[32,256]{1,0:T(8,128)S(1)}, f32[32,256]{1,0:T(8,128)S(1)}, u32[]{:S(2)}, u32[]{:S(2)}) collective-permute-start(f32[32,256]{1,0:T(8,128)S(1)} %reduce_sum.30), channel_id=1, source_target_pairs={{0,4},{4,0},{1,5},{5,1},{2,6},{6,2},{3,7},{7,3},{8,12},{12,8},{9,1... | collective-permute-start | bytes 98312 | tf_op jit(solution)/shard_map/ppermute | solution.py:294
  109.0 0.9 collective-permute-done.14
  110.7 2.0 collective-permute-start.16
  112.7 1.8 collective-permute-done.17.last_ref
  115.1 1.4 collective-permute-done.16.across_ref
  116.4 1.7 collective-permute-done.15.next_ref
  118.1 9.9 %shard_map.50 = f32[256,256]{1,0:T(8,128)S(1)} custom-call(s32[4]{0:T(128)S(1)} %pad_add_fusion.at_ref.refs_0_, f32[64,256]{1,0:T(8,128)S(1)} %pad_maximum_fusion.own_ref, f32[64,256]{1,0:T(8,128)S(1)} %collective-permute-done.15.next_ref, f32[64,256]{1,0:T(8,128)S(1)} %collective-permute-done.16.across_ref, f32[64,256]{1,0:T(8,128)S(1)} %collective-permute-done.17.last_ref), custom_call_target="tpu_custom_call" | custom-call | tf_op jit(solution)/shard_map/pallas_call | solution.py:127
  128.1 1.8 collective-permute-done.21
  129.9 2.3 %convolution_convert_fusion = bf16[832,256]{1,0:T(8,128)(2,1)S(1)} fusion(f32[256,256]{1,0:T(8,128)S(1)} %shard_map.50, f32[832,256]{1,0:T(8,128)S(1)} %get-tuple-element.24, f32[832,256]{1,0:T(8,128)} %collective-permute-done.21, f32[832,256]{1,0:T(8,128)S(1)} %collective-permute-done.19, f32[832,256]{1,0:T(8,128)} %collective-permute-done.20), kind=kOutput, calls=%fused_computation | convolution fusion | flops 655163392 | bytes 4096000 | tf_op jit(solution)/shard_map/dot_general | solution.py:368
  132.2 16.1 %all_to_all.27 = bf16[8,104,256]{2,1,0:T(8,128)(2,1)S(1)} all-to-all(bf16[8,104,256]{2,1,0:T(8,128)(2,1)S(1)} %bitcast.23), channel_id=1, replica_groups=mesh['z'=8,'y'=4,'c'=2,'x'=4] {'z'}, dimensions={0} | all-to-all | bytes 851968 | tf_op jit(solution)/shard_map/all_to_all | solution.py:321
  148.3 14.9 %all_to_all.28 = bf16[8,104,256]{2,1,0:T(8,128)(2,1)S(1)} all-to-all(bf16[8,104,256]{2,1,0:T(8,128)(2,1)S(1)} %broadcast_in_dim.10), channel_id=1, replica_groups=mesh['z'=8,'y'=4,'c'=2,'x'=4] {'z'}, dimensions={0} | all-to-all | bytes 851968 | tf_op jit(solution)/shard_map/all_to_all | solution.py:316
  163.2 6.9 %collective-permute-start.23 = (bf16[832,256]{1,0:T(8,128)(2,1)S(1)}, bf16[832,256]{1,0:T(8,128)(2,1)S(1)}, u32[]{:S(2)}, u32[]{:S(2)}) collective-permute-start(bf16[832,256]{1,0:T(8,128)(2,1)S(1)} %bitcast.15), channel_id=1, source_target_pairs={{24,0},{0,8},{8,16},{16,24},{25,1},{1,9},{9,17},{17,25},{26,2},{2,... | collective-permute-start | bytes 1277960 | tf_op jit(solution)/shard_map/ppermute | solution.py:298
  170.1 1.1 collective-permute-start.22
  171.4 13.8 %all_to_all.29 = f32[32,1,256]{2,1,0:T(1,128)S(1)} all-to-all(f32[32,1,256]{2,1,0:T(1,128)S(1)} %broadcast_in_dim.11), channel_id=1, replica_groups=mesh['z'=8,'y'=4,'c'=2,'x'=4] {'y','c','x'}, dimensions={0} | all-to-all | bytes 65536 | tf_op jit(solution)/shard_map/all_to_all | solution.py:316
  185.6 2.4 %collective-permute-start.25 = (bf16[416,256]{1,0:T(8,128)(2,1)S(1)}, bf16[416,256]{1,0:T(8,128)(2,1)S(1)}, u32[]{:S(2)}, u32[]{:S(2)}) collective-permute-start(bf16[416,256]{1,0:T(8,128)(2,1)S(1)} %slice.15), channel_id=1, source_target_pairs={{8,0},{16,8},{24,16},{0,24},{9,1},{17,9},{25,17},{1,25},{10,2},{18... | collective-permute-start | bytes 638984 | tf_op jit(solution)/shard_map/ppermute | solution.py:298
  188.0 1.0 collective-permute-start.26
  189.5 3.4 %collective-permute-done.24.refs_7_ = bf16[416,256]{1,0:T(8,128)(2,1)S(1)} collective-permute-done((bf16[416,256]{1,0:T(8,128)(2,1)S(1)}, bf16[416,256]{1,0:T(8,128)(2,1)S(1)}, u32[]{:S(2)}, u32[]{:S(2)}) %collective-permute-start.24) | collective-permute-done | bytes 213024 | tf_op jit(solution)/shard_map/ppermute | solution.py:298
  192.9 1.2 collective-permute-start.29
  195.6 7.9 %shard_map.52 = (bf16[256,6656]{1,0:T(8,128)(2,1)}, bf16[256,6656]{1,0:T(8,128)(2,1)}, f32[4,6656]{1,0:T(4,128)}) custom-call(s32[4]{0:T(128)S(1)} %pad_add_fusion.at_ref.refs_0_, bf16[256,6656]{1,0:T(8,128)(2,1)S(1)} %copy-done, f32[256,256]{1,0:T(8,128)S(1)} %fusion.4.refs_2_, f32[32,256]{1,0:T(8,128)S(1)} %bitcast.22, bf16[832,256]{1,0:T(8,128)(2,1)S(1)} %bitcast.18, ...), custom_call_target="tpu_custom_call" | custom-call | flops 1744830464 | bytes 13631488 | tf_op jit(solution)/shard_map/pallas_call | solution.py:268
  (68 shorter events, 11.2 us)
Async XLA Ops:
  1.6 4.2 %collective-permute-start = (bf16[4,3328]{1,0:T(4,128)(2,1)S(1)}, bf16[4,3328]{1,0:T(4,128)(2,1)S(1)}, u32[]{:S(2)}, u32[]{:S(2)}) collective-permute-start(bf16[4,3328]{1,0:T(4,128)(2,1)S(1)} %constant_dynamic-slice_fusion.3), channel_id=1, source_target_pairs={{0,4},{4,0},{1,5},{5,1},{2,6},{6,2},{3,7},{7,3},{8,12},{12,8},{9,1... | collective-permute-start | bytes 79880 | tf_op jit(solution)/shard_map/ppermute | solution.py:294
  8.0 34.7 %collective-permute-start.3 = (bf16[256,3328]{1,0:T(8,128)(2,1)S(1)}, bf16[256,3328]{1,0:T(8,128)(2,1)S(1)}, u32[]{:S(2)}, u32[]{:S(2)}) collective-permute-start(bf16[256,3328]{1,0:T(8,128)(2,1)S(1)} %get-tuple-element.31), channel_id=1, source_target_pairs={{0,4},{4,0},{1,5},{5,1},{2,6},{6,2},{3,7},{7,3},{8,12},{12,8},{9,1... | collective-permute-start | bytes 5111816 | tf_op jit(solution)/shard_map/ppermute | solution.py:294
  30.5 12.1 %collective-permute-start.2 = (bf16[64,3328]{1,0:T(8,128)(2,1)S(1)}, bf16[64,3328]{1,0:T(8,128)(2,1)S(1)}, u32[]{:S(2)}, u32[]{:S(2)}) collective-permute-start(bf16[64,3328]{1,0:T(8,128)(2,1)S(1)} %bitcast.19), channel_id=1, source_target_pairs={{24,0},{0,8},{8,16},{16,24},{25,1},{1,9},{9,17},{17,25},{26,2},{2,... | collective-permute-start | bytes 1277960 | tf_op jit(solution)/shard_map/ppermute | solution.py:298
  31.8 10.9 %collective-permute-start.1 = (bf16[64,3328]{1,0:T(8,128)(2,1)S(1)}, bf16[64,3328]{1,0:T(8,128)(2,1)S(1)}, u32[]{:S(2)}, u32[]{:S(2)}) collective-permute-start(bf16[64,3328]{1,0:T(8,128)(2,1)S(1)} %bitcast.20), channel_id=1, source_target_pairs={{8,0},{16,8},{24,16},{0,24},{9,1},{17,9},{25,17},{1,25},{10,2},{18... | collective-permute-start | bytes 1277960 | tf_op jit(solution)/shard_map/ppermute | solution.py:298
  33.3 0.8 copy-start.3
  42.7 0.9 copy-start.5
  42.7 1.6 copy-start.7
  42.7 14.1 %copy-start.1 = (bf16[256,3328]{1,0:T(8,128)(2,1)}, bf16[256,3328]{1,0:T(8,128)(2,1)S(1)}, u32[]{:S(2)}) copy-start(bf16[256,3328]{1,0:T(8,128)(2,1)S(1)} %collective-permute-done.3.other_ref) | copy-start | bytes 5111812
  44.3 6.9 %collective-permute-start.4 = (bf16[32,3328]{1,0:T(8,128)(2,1)}, bf16[32,3328]{1,0:T(8,128)(2,1)}, u32[]{:S(2)}, u32[]{:S(2)}) collective-permute-start(bf16[32,3328]{1,0:T(8,128)(2,1)} %slice.12), channel_id=1, source_target_pairs={{24,0},{0,8},{8,16},{16,24},{25,1},{1,9},{9,17},{17,25},{26,2},{2,... | collective-permute-start | bytes 638984 | tf_op jit(solution)/shard_map/ppermute | solution.py:298
  45.1 6.1 %collective-permute-start.5 = (bf16[32,3328]{1,0:T(8,128)(2,1)}, bf16[32,3328]{1,0:T(8,128)(2,1)}, u32[]{:S(2)}, u32[]{:S(2)}) collective-permute-start(bf16[32,3328]{1,0:T(8,128)(2,1)} %slice.13), channel_id=1, source_target_pairs={{8,0},{16,8},{24,16},{0,24},{9,1},{17,9},{25,17},{1,25},{10,2},{18... | collective-permute-start | bytes 638984 | tf_op jit(solution)/shard_map/ppermute | solution.py:298
  51.2 1.0 copy-start.4
  52.2 1.0 copy-start.6
  53.2 1.0 copy-start.8
  56.8 3.5 %collective-permute-start.6 = (f32[256,256]{1,0:T(8,128)S(1)}, f32[256,256]{1,0:T(8,128)S(1)}, u32[]{:S(2)}, u32[]{:S(2)}) collective-permute-start(f32[256,256]{1,0:T(8,128)S(1)} %get-tuple-element.23), channel_id=1, source_target_pairs={{0,4},{4,0},{1,5},{5,1},{2,6},{6,2},{3,7},{7,3},{8,12},{12,8},{9,1... | collective-permute-start | bytes 786440 | tf_op jit(solution)/shard_map/ppermute | solution.py:294
  60.3 8.8 %collective-permute-start.9 = (f32[256,256]{1,0:T(8,128)S(1)}, f32[256,256]{1,0:T(8,128)S(1)}, u32[]{:S(2)}, u32[]{:S(2)}) collective-permute-start(f32[256,256]{1,0:T(8,128)S(1)} %add.63), channel_id=1, source_target_pairs={{3,0},{0,1},{1,2},{2,3},{7,4},{4,5},{5,6},{6,7},{11,8},{8,9},{9,10... | collective-permute-start | bytes 786440 | tf_op jit(solution)/shard_map/ppermute | solution.py:298
  61.6 7.5 %collective-permute-start.8 = (f32[256,256]{1,0:T(8,128)S(1)}, f32[256,256]{1,0:T(8,128)S(1)}, u32[]{:S(2)}, u32[]{:S(2)}) collective-permute-start(f32[256,256]{1,0:T(8,128)S(1)} %add.63), channel_id=1, source_target_pairs={{1,0},{2,1},{3,2},{0,3},{5,4},{6,5},{7,6},{4,7},{9,8},{10,9},{11,1... | collective-permute-start | bytes 786440 | tf_op jit(solution)/shard_map/ppermute | solution.py:298
  63.1 12.7 %collective-permute-start.7 = (f32[256,256]{1,0:T(8,128)S(1)}, f32[256,256]{1,0:T(8,128)S(1)}, u32[]{:S(2)}, u32[]{:S(2)}) collective-permute-start(f32[256,256]{1,0:T(8,128)S(1)} %add.63), channel_id=1, source_target_pairs={{2,0},{3,1},{0,2},{1,3},{6,4},{7,5},{4,6},{5,7},{10,8},{11,9},{8,1... | collective-permute-start | bytes 786440 | tf_op jit(solution)/shard_map/ppermute | solution.py:298
  76.4 6.4 %collective-permute-start.18 = (f32[256,256]{1,0:T(8,128)S(1)}, f32[256,256]{1,0:T(8,128)S(1)}, u32[]{:S(2)}, u32[]{:S(2)}) collective-permute-start(f32[256,256]{1,0:T(8,128)S(1)} %add_add_fusion.left_mine_ref), channel_id=1, source_target_pairs={{0,4},{4,0},{1,5},{5,1},{2,6},{6,2},{3,7},{7,3},{8,12},{12,8},{9,1... | collective-permute-start | bytes 786440 | tf_op jit(solution)/shard_map/ppermute | solution.py:294
  77.7 1.2 collective-permute-start.10
  78.9 12.7 %collective-permute-start.13 = (f32[32,256]{1,0:T(8,128)S(1)}, f32[32,256]{1,0:T(8,128)S(1)}, u32[]{:S(2)}, u32[]{:S(2)}) collective-permute-start(f32[32,256]{1,0:T(8,128)S(1)} %dynamic-slice_add_fusion), channel_id=1, source_target_pairs={{24,0},{0,8},{8,16},{16,24},{25,1},{1,9},{9,17},{17,25},{26,2},{2,... | collective-permute-start | bytes 98312 | tf_op jit(solution)/shard_map/ppermute | solution.py:298
  79.7 13.9 %collective-permute-start.12 = (f32[32,256]{1,0:T(8,128)S(1)}, f32[32,256]{1,0:T(8,128)S(1)}, u32[]{:S(2)}, u32[]{:S(2)}) collective-permute-start(f32[32,256]{1,0:T(8,128)S(1)} %dynamic-slice_add_fusion), channel_id=1, source_target_pairs={{8,0},{16,8},{24,16},{0,24},{9,1},{17,9},{25,17},{1,25},{10,2},{18... | collective-permute-start | bytes 98312 | tf_op jit(solution)/shard_map/ppermute | solution.py:298
  81.7 11.9 %collective-permute-start.11 = (f32[32,256]{1,0:T(8,128)S(1)}, f32[32,256]{1,0:T(8,128)S(1)}, u32[]{:S(2)}, u32[]{:S(2)}) collective-permute-start(f32[32,256]{1,0:T(8,128)S(1)} %dynamic-slice_add_fusion), channel_id=1, source_target_pairs={{16,0},{24,8},{0,16},{8,24},{17,1},{25,9},{1,17},{9,25},{18,2},{26... | collective-permute-start | bytes 98312 | tf_op jit(solution)/shard_map/ppermute | solution.py:298
  82.8 1.5 copy-start.2
  89.7 38.4 %collective-permute-start.19 = (f32[832,256]{1,0:T(8,128)}, f32[832,256]{1,0:T(8,128)S(1)}, u32[]{:S(2)}, u32[]{:S(2)}) collective-permute-start(f32[832,256]{1,0:T(8,128)} %get-tuple-element.25), channel_id=1, source_target_pairs={{24,0},{0,8},{8,16},{16,24},{25,1},{1,9},{9,17},{17,25},{26,2},{2,... | collective-permute-start | bytes 2555912 | tf_op jit(solution)/shard_map/ppermute | solution.py:298
  90.5 37.5 %collective-permute-start.20 = (f32[832,256]{1,0:T(8,128)}, f32[832,256]{1,0:T(8,128)}, u32[]{:S(2)}, u32[]{:S(2)}) collective-permute-start(f32[832,256]{1,0:T(8,128)} %get-tuple-element.26), channel_id=1, source_target_pairs={{16,0},{24,8},{0,16},{8,24},{17,1},{25,9},{1,17},{9,25},{18,2},{26... | collective-permute-start | bytes 2555912 | tf_op jit(solution)/shard_map/ppermute | solution.py:298
  91.6 38.2 %collective-permute-start.21 = (f32[832,256]{1,0:T(8,128)}, f32[832,256]{1,0:T(8,128)}, u32[]{:S(2)}, u32[]{:S(2)}) collective-permute-start(f32[832,256]{1,0:T(8,128)} %get-tuple-element.27), channel_id=1, source_target_pairs={{8,0},{16,8},{24,16},{0,24},{9,1},{17,9},{25,17},{1,25},{10,2},{18... | collective-permute-start | bytes 2555912 | tf_op jit(solution)/shard_map/ppermute | solution.py:298
  105.3 4.6 %collective-permute-start.14 = (f32[32,256]{1,0:T(8,128)S(1)}, f32[32,256]{1,0:T(8,128)S(1)}, u32[]{:S(2)}, u32[]{:S(2)}) collective-permute-start(f32[32,256]{1,0:T(8,128)S(1)} %reduce_sum.30), channel_id=1, source_target_pairs={{0,4},{4,0},{1,5},{5,1},{2,6},{6,2},{3,7},{7,3},{8,12},{12,8},{9,1... | collective-permute-start | bytes 98312 | tf_op jit(solution)/shard_map/ppermute | solution.py:294
  109.9 4.7 %collective-permute-start.17 = (f32[64,256]{1,0:T(8,128)S(1)}, f32[64,256]{1,0:T(8,128)S(1)}, u32[]{:S(2)}, u32[]{:S(2)}) collective-permute-start(f32[64,256]{1,0:T(8,128)S(1)} %pad_maximum_fusion.own_ref), channel_id=1, source_target_pairs={{3,0},{0,1},{1,2},{2,3},{7,4},{4,5},{5,6},{6,7},{11,8},{8,9},{9,10... | collective-permute-start | bytes 196616 | tf_op jit(solution)/shard_map/ppermute | solution.py:298
  110.7 5.7 %collective-permute-start.16 = (f32[64,256]{1,0:T(8,128)S(1)}, f32[64,256]{1,0:T(8,128)S(1)}, u32[]{:S(2)}, u32[]{:S(2)}) collective-permute-start(f32[64,256]{1,0:T(8,128)S(1)} %pad_maximum_fusion.own_ref), channel_id=1, source_target_pairs={{2,0},{3,1},{0,2},{1,3},{6,4},{7,5},{4,6},{5,7},{10,8},{11,9},{8,1... | collective-permute-start | bytes 196616 | tf_op jit(solution)/shard_map/ppermute | solution.py:298
  114.6 3.5 %collective-permute-start.15 = (f32[64,256]{1,0:T(8,128)S(1)}, f32[64,256]{1,0:T(8,128)S(1)}, u32[]{:S(2)}, u32[]{:S(2)}) collective-permute-start(f32[64,256]{1,0:T(8,128)S(1)} %pad_maximum_fusion.own_ref), channel_id=1, source_target_pairs={{1,0},{2,1},{3,2},{0,3},{5,4},{6,5},{7,6},{4,7},{9,8},{10,9},{11,1... | collective-permute-start | bytes 196616 | tf_op jit(solution)/shard_map/ppermute | solution.py:298
  148.3 47.3 %copy-start = (bf16[256,6656]{1,0:T(8,128)(2,1)S(1)}, bf16[256,6656]{1,0:T(8,128)(2,1)}, u32[]{:S(2)}) copy-start(bf16[256,6656]{1,0:T(8,128)(2,1)} %refs_1_.1) | copy-start | bytes 10223620
  163.2 21.9 %collective-permute-start.23 = (bf16[832,256]{1,0:T(8,128)(2,1)S(1)}, bf16[832,256]{1,0:T(8,128)(2,1)S(1)}, u32[]{:S(2)}, u32[]{:S(2)}) collective-permute-start(bf16[832,256]{1,0:T(8,128)(2,1)S(1)} %bitcast.15), channel_id=1, source_target_pairs={{24,0},{0,8},{8,16},{16,24},{25,1},{1,9},{9,17},{17,25},{26,2},{2,... | collective-permute-start | bytes 1277960 | tf_op jit(solution)/shard_map/ppermute | solution.py:298
  170.1 15.1 %collective-permute-start.22 = (bf16[832,256]{1,0:T(8,128)(2,1)S(1)}, bf16[832,256]{1,0:T(8,128)(2,1)S(1)}, u32[]{:S(2)}, u32[]{:S(2)}) collective-permute-start(bf16[832,256]{1,0:T(8,128)(2,1)S(1)} %bitcast.16), channel_id=1, source_target_pairs={{8,0},{16,8},{24,16},{0,24},{9,1},{17,9},{25,17},{1,25},{10,2},{18... | collective-permute-start | bytes 1277960 | tf_op jit(solution)/shard_map/ppermute | solution.py:298
  185.2 7.7 %collective-permute-start.24 = (bf16[416,256]{1,0:T(8,128)(2,1)S(1)}, bf16[416,256]{1,0:T(8,128)(2,1)S(1)}, u32[]{:S(2)}, u32[]{:S(2)}) collective-permute-start(bf16[416,256]{1,0:T(8,128)(2,1)S(1)} %slice.14), channel_id=1, source_target_pairs={{24,0},{0,8},{8,16},{16,24},{25,1},{1,9},{9,17},{17,25},{26,2},{2,... | collective-permute-start | bytes 638984 | tf_op jit(solution)/shard_map/ppermute | solution.py:298
  185.6 8.5 %collective-permute-start.25 = (bf16[416,256]{1,0:T(8,128)(2,1)S(1)}, bf16[416,256]{1,0:T(8,128)(2,1)S(1)}, u32[]{:S(2)}, u32[]{:S(2)}) collective-permute-start(bf16[416,256]{1,0:T(8,128)(2,1)S(1)} %slice.15), channel_id=1, source_target_pairs={{8,0},{16,8},{24,16},{0,24},{9,1},{17,9},{25,17},{1,25},{10,2},{18... | collective-permute-start | bytes 638984 | tf_op jit(solution)/shard_map/ppermute | solution.py:298
  188.0 6.5 %collective-permute-start.26 = (bf16[832,256]{1,0:T(8,128)(2,1)S(1)}, bf16[832,256]{1,0:T(8,128)(2,1)S(1)}, u32[]{:S(2)}, u32[]{:S(2)}) collective-permute-start(bf16[832,256]{1,0:T(8,128)(2,1)S(1)} %bitcast.17), channel_id=1, source_target_pairs={{0,4},{4,0},{1,5},{5,1},{2,6},{6,2},{3,7},{7,3},{8,12},{12,8},{9,1... | collective-permute-start | bytes 1277960 | tf_op jit(solution)/shard_map/ppermute | solution.py:294
  189.0 6.6 %collective-permute-start.27 = (bf16[832,256]{1,0:T(8,128)(2,1)S(1)}, bf16[832,256]{1,0:T(8,128)(2,1)S(1)}, u32[]{:S(2)}, u32[]{:S(2)}) collective-permute-start(bf16[832,256]{1,0:T(8,128)(2,1)S(1)} %collective-permute-done.22.refs_5_), channel_id=1, source_target_pairs={{0,4},{4,0},{1,5},{5,1},{2,6},{6,2},{3,7},{7,3},{8,12},{12,8},{9,1... | collective-permute-start | bytes 1277960 | tf_op jit(solution)/shard_map/ppermute | solution.py:294
  189.0 6.6 %collective-permute-start.28 = (bf16[832,256]{1,0:T(8,128)(2,1)S(1)}, bf16[832,256]{1,0:T(8,128)(2,1)S(1)}, u32[]{:S(2)}, u32[]{:S(2)}) collective-permute-start(bf16[832,256]{1,0:T(8,128)(2,1)S(1)} %collective-permute-done.23.refs_6_), channel_id=1, source_target_pairs={{0,4},{4,0},{1,5},{5,1},{2,6},{6,2},{3,7},{7,3},{8,12},{12,8},{9,1... | collective-permute-start | bytes 1277960 | tf_op jit(solution)/shard_map/ppermute | solution.py:294
  192.9 2.3 %collective-permute-start.29 = (bf16[416,256]{1,0:T(8,128)(2,1)S(1)}, bf16[416,256]{1,0:T(8,128)(2,1)S(1)}, u32[]{:S(2)}, u32[]{:S(2)}) collective-permute-start(bf16[416,256]{1,0:T(8,128)(2,1)S(1)} %collective-permute-done.24.refs_7_), channel_id=1, source_target_pairs={{0,4},{4,0},{1,5},{5,1},{2,6},{6,2},{3,7},{7,3},{8,12},{12,8},{9,1... | collective-permute-start | bytes 638984 | tf_op jit(solution)/shard_map/ppermute | solution.py:294
  194.1 1.5 collective-permute-start.30
where the time goes:
time: 204 us
  blocking collectives  78.3 us (38%)
  starting transfers between devices  45.7 us (22%)
  waiting for transfers between devices  39.1 us (19%)
  Pallas kernels  25.7 us (13%)
  local copies, waits for them, and re-layouts  9.19 us (5%)
  matrix products  3.28 us (2%)
    all_to_all x4, blocking collectives, gather(): return lax.all_to_all(copies, axes, 0, 0)  62.2 us
    ppermute x20, waiting for transfers between devices, from_ahead(): lax.ppermute(block, axis, [((i + by) % parts, i) for i in range(parts)])  34.1 us
    ppermute x20, starting transfers between devices, from_ahead(): lax.ppermute(block, axis, [((i + by) % parts, i) for i in range(parts)])  31.7 us
    all_to_all x1, blocking collectives, scatter_sum(): return jnp.sum(lax.all_to_all(pieces, axes, 0, 0).astype(f32), axis=0)  16.1 us
    ppermute x11, starting transfers between devices, swap_cores(): return lax.ppermute(block, 'c', [(0, 1), (1, 0)])  14 us
    pallas_call x1, Pallas kernels, inverse_factor(): pl.pallas_call(inverse_factor_kernel, out_shape=jax.ShapeDtypeStruct((ran...  9.93 us
    pallas_call x1, Pallas kernels, finish(): pl.pallas_call(lambda *refs: finish_kernel(scaling, *refs), out_shape=[ou...  7.9 us
    pallas_call x1, Pallas kernels, cross(): pl.pallas_call(cross_kernel, out_shape=[jax.ShapeDtypeStruct((cols // NY,...  5.39 us
  transfers between devices with their start and end apart: 31, of which 15 were waited for; matrix products, arithmetic and copies ran while one was open for 0% of the time, Pallas kernels for 8%

commit v1 on v0

--- a/solution.py
+++ b/solution.py
@@ -134,83 +134,128 @@
     )(at, *pieces)
 
 
+def core_half(rows, width):
+    return pl.BlockSpec((rows, width), lambda i, at: (0, at[AT_CORE] * 2 + i))
+
+
 def project_kernel(at_ref, mine_ref, other_ref, *refs):
-    pieces, (out_mine_ref, out_other_ref, basis_ref) = refs[:5], refs[5:]
-    per_y = pieces[0].shape[0]
-    for n, ref in enumerate(pieces):
+    pieces, (out_mine_ref, out_other_ref, basis_ref) = refs[:NY], refs[NY:]
+    for by, ref in enumerate(pieces):
         size = ref.shape[0]
-        start = ahead(at_ref[AT_Y], RING_FROM[n], NY) * per_y + (size if n == 4 else 0)
-        basis_ref[pl.ds(pl.multiple_of(start, size), size), :] = ref[...]
-    width = mine_ref.shape[1] // 2
-    out_mine_ref[...] = jnp.zeros_like(out_mine_ref)
-    out_other_ref[...] = jnp.zeros_like(out_other_ref)
-
-    def add(step, carry):
-        columns = pl.ds(pl.multiple_of(step * width, 128), width)
-        basis = basis_ref[:, columns]
-        for ref, out_ref in ((mine_ref, out_mine_ref), (other_ref, out_other_ref)):
-            out_ref[...] += lax.dot_general(
-                ref[:, columns], basis, BOTH_LAST, preferred_element_type=f32
-            )
-        return carry
-
-    lax.fori_loop(0, 2, add, 0)
+        start = pl.multiple_of(ahead(at_ref[AT_Y], by, NY) * size, size)
+        basis_ref[pl.ds(start, size), :] = ref[...]
+    basis = basis_ref[...]
+    product_mine = lax.dot_general(mine_ref[...], basis, BOTH_LAST, preferred_element_type=f32)
+    product_other = lax.dot_general(other_ref[...], basis, BOTH_LAST, preferred_element_type=f32)
+    first = pl.program_id(0) == 0
+
+    @pl.when(first)
+    def _():
+        out_mine_ref[...] = product_mine
+        out_other_ref[...] = product_other
+
+    @pl.when(jnp.logical_not(first))
+    def _():
+        out_mine_ref[...] += product_mine
+        out_other_ref[...] += product_other
 
 
 def project(at, mine, other, pieces):
     rows, cols = mine.shape
     rank = pieces[0].shape[0] * NY
+    width = cols // 4
+    whole = pl.BlockSpec((rows, rank), lambda i, at: (0, 0))
+    piece = pl.BlockSpec((rank // NY, width), lambda i, at: (0, i))
     return pl.pallas_call(
         project_kernel,
         out_shape=[jax.ShapeDtypeStruct((rows, rank), f32)] * 2,
-        in_specs=[SMEM] + [VMEM] * 7,
-        out_specs=[VMEM, VMEM],
-        scratch_shapes=[pltpu.VMEM((rank, cols), bf16)],
-        compiler_params=pltpu.CompilerParams(vmem_limit_bytes=12 * MIB),
+        grid_spec=pltpu.PrefetchScalarGridSpec(
+            num_scalar_prefetch=1,
+            grid=(2,),
+            in_specs=[core_half(rows, width), core_half(rows, width)] + [piece] * NY,
+            out_specs=[whole, whole],
+            scratch_shapes=[pltpu.VMEM((rank, width), bf16)],
+        ),
+        compiler_params=pltpu.CompilerParams(vmem_limit_bytes=14 * MIB),
         cost_estimate=pl.CostEstimate(
-            flops=4 * rows * cols * rank, bytes_accessed=6 * rows * cols, transcendentals=0
+            flops=2 * rows * cols * rank, bytes_accessed=3 * rows * cols, transcendentals=0
         ),
     )(at, mine, other, *pieces)
+
+
+def gram_kernel(at_ref, own_ref, one_ref, two_ref, three_ref, projected_ref, keep_ref, send_ref, gram_ref):
+    projected = (own_ref[...] + two_ref[...]) + (one_ref[...] + three_ref[...])
+    projected_ref[...] = projected
+    gram_ref[...] = lax.dot_general(
+        projected, projected, BOTH_FIRST, preferred_element_type=f32, precision=HIGHEST
+    )
+    part = keep_ref.shape[0]
+    for other, ref in enumerate((keep_ref, send_ref)):
+        place = at_ref[AT_X] * 2 + (at_ref[AT_CORE] + other) % 2
+        ref[...] = gram_ref[pl.ds(pl.multiple_of(place * part, part), part), :]
+
+
+def gram_rows_of(at, pieces):
+    rows, rank = pieces[0].shape
+    part = jax.ShapeDtypeStruct((rank // (NX * 2), rank), f32)
+    return pl.pallas_call(
+        gram_kernel,
+        out_shape=[jax.ShapeDtypeStruct((rows, rank), f32), part, part],
+        in_specs=[SMEM] + [VMEM] * 4,
+        out_specs=[VMEM] * 3,
+        scratch_shapes=[pltpu.VMEM((rank, rank), f32)],
+        compiler_params=pltpu.CompilerParams(vmem_limit_bytes=8 * MIB),
+    )(at, *pieces)
 
 
 def cross_kernel(at_ref, mine_ref, other_ref, left_mine_ref, left_other_ref, *refs):
     pieces, (terms_ref, whole_ref) = refs[:NY], refs[NY:]
     rows, rank = left_mine_ref.shape
-    for n, ref in enumerate((left_mine_ref, left_other_ref)):
-        left = ref[...]
-        for t in range(3):
-            term = left.astype(bf16)
-            terms_ref[n * rows : (n + 1) * rows, t * rank : (t + 1) * rank] = term
-            left = left - term.astype(f32)
-    width = mine_ref.shape[1] // 2
-
-    def multiply(step, carry):
-        columns = pl.ds(pl.multiple_of(step * width, 128), width)
-        momentum = jnp.concatenate([mine_ref[:, columns], other_ref[:, columns]], axis=0)
-        product = lax.dot_general(momentum, terms_ref[...], BOTH_FIRST, preferred_element_type=f32)
-        total = (product[:, 2 * rank :] + product[:, rank : 2 * rank]) + product[:, :rank]
-        whole_ref[columns, :] = total
-        return carry
-
-    lax.fori_loop(0, 2, multiply, 0)
-    size = pieces[0].shape[0]
-    for by, ref in enumerate(pieces):
-        start = pl.multiple_of(ahead(at_ref[AT_Y], by, NY) * size, size)
-        ref[...] = whole_ref[pl.ds(start, size), :]
+    step = pl.program_id(0)
+    width = mine_ref.shape[1]
+
+    @pl.when(step == 0)
+    def _():
+        for n, ref in enumerate((left_mine_ref, left_other_ref)):
+            left = ref[...]
+            for t in range(3):
+                term = left.astype(bf16)
+                terms_ref[n * rows : (n + 1) * rows, t * rank : (t + 1) * rank] = term
+                left = left - term.astype(f32)
+
+    momentum = jnp.concatenate([mine_ref[...], other_ref[...]], axis=0)
+    product = lax.dot_general(momentum, terms_ref[...], BOTH_FIRST, preferred_element_type=f32)
+    total = (product[:, 2 * rank :] + product[:, rank : 2 * rank]) + product[:, :rank]
+    whole_ref[pl.ds(pl.multiple_of(step * width, 128), width), :] = total
+
+    @pl.when(step == pl.num_programs(0) - 1)
+    def _():
+        size = pieces[0].shape[0]
+        for by, ref in enumerate(pieces):
+            start = pl.multiple_of(ahead(at_ref[AT_Y], by, NY) * size, size)
+            ref[...] = whole_ref[pl.ds(start, size), :]
 
 
 def cross(at, mine, other, left_mine, left_other):
     rows, cols = mine.shape
     rank = left_mine.shape[1]
+    half = cols // 2
+    width, size = half // 2, half // NY
+    left = pl.BlockSpec((rows, rank), lambda i, at: (0, 0))
+    piece = pl.BlockSpec((size, rank), lambda i, at: (0, 0))
     return pl.pallas_call(
         cross_kernel,
-        out_shape=[jax.ShapeDtypeStruct((cols // NY, rank), f32)] * NY,
-        in_specs=[SMEM] + [VMEM] * 4,
-        out_specs=[VMEM] * NY,
-        scratch_shapes=[pltpu.VMEM((2 * rows, 3 * rank), bf16), pltpu.VMEM((cols, rank), f32)],
-        compiler_params=pltpu.CompilerParams(vmem_limit_bytes=16 * MIB),
+        out_shape=[jax.ShapeDtypeStruct((size, rank), f32)] * NY,
+        grid_spec=pltpu.PrefetchScalarGridSpec(
+            num_scalar_prefetch=1,
+            grid=(2,),
+            in_specs=[core_half(rows, width), core_half(rows, width), left, left],
+            out_specs=[piece] * NY,
+            scratch_shapes=[pltpu.VMEM((2 * rows, 3 * rank), bf16), pltpu.VMEM((half, rank), f32)],
+        ),
+        compiler_params=pltpu.CompilerParams(vmem_limit_bytes=26 * MIB),
         cost_estimate=pl.CostEstimate(
-            flops=12 * rows * cols * rank, bytes_accessed=4 * rows * cols + 8 * cols * rank, transcendentals=0
+            flops=6 * rows * cols * rank, bytes_accessed=2 * rows * cols + 4 * cols * rank, transcendentals=0
         ),
     )(at, mine, other, left_mine, left_other)
 
@@ -298,12 +343,16 @@
     return lax.ppermute(block, axis, [((i + by) % parts, i) for i in range(parts)])
 
 
+def all_of_four(block, axis):
+    return [block] + [from_ahead(block, axis, by) for by in (1, 2, 3)]
+
+
 def sum_four(block, axis):
-    one, two, three = (from_ahead(block, axis, by) for by in (1, 2, 3))
-    return (block + two) + (one + three)
-
-
-def ring_of_four(block, axis, beside=None):
+    own, one, two, three = all_of_four(block, axis)
+    return (own + two) + (one + three)
+
+
+def ring_of_four(block, axis, beside):
     middle = block.shape[0] // 2
     one, three = from_ahead(block, axis, 1), from_ahead(block, axis, 3)
     one, three, beside = lax.optimization_barrier((one, three, beside))
@@ -333,35 +382,25 @@
     def columns(array, of_core):
         return lax.dynamic_slice_in_dim(array, of_core * half, half, 1)
 
+    momentum_other = swap_cores(momentum)
     basis_half = q_basis.astype(bf16)
     basis_own = columns(basis_half, core)
     basis_other = swap_cores(columns(basis_half, 1 - core))
     basis_chip = jnp.concatenate(
         [jnp.where(core == 0, basis_own, basis_other), jnp.where(core == 0, basis_other, basis_own)]
     )
-    later, basis_chip = lax.optimization_barrier((momentum, basis_chip))
-    mine = columns(later, core)
-    other = swap_cores(columns(later, 1 - core))
-
     basis_z = gather(basis_chip, "z", NZ).reshape(rank // NY, half)
-    basis, other = ring_of_four(basis_z, "y", other)
-    proj_mine, proj_other = project(at, mine, other, basis)
-    projected = sum_four(proj_mine + swap_cores(proj_other), "x")
-
-    gram_own = jnp.dot(projected.T, projected, preferred_element_type=f32, precision=HIGHEST)
-    part = rank // (NX * 2)
-
-    def gram_part(of_core):
-        return lax.dynamic_slice_in_dim(gram_own, (at_x * 2 + of_core) * part, part, 0)
-
-    gram_rows = sum_four(gram_part(core) + swap_cores(gram_part(1 - core)), "y")
+    basis = all_of_four(basis_z, "y")
+    proj_mine, proj_other = project(at, momentum, momentum_other, basis)
+    projected, gram_keep, gram_send = gram_rows_of(
+        at, all_of_four(proj_mine + swap_cores(proj_other), "x")
+    )
+    gram_rows = sum_four(gram_keep + swap_cores(gram_send), "y")
     gram_rows = jnp.sum(gather(gram_rows, "z", NZ), axis=0)
     gram_chip = jnp.concatenate([gram_rows, swap_cores(gram_rows)])
-    inverse = inverse_factor(
-        at, [gram_chip] + [from_ahead(gram_chip, "x", by) for by in (1, 2, 3)]
-    )
-
-    crossed = cross(at, mine, other, projected, swap_cores(projected))
+    inverse = inverse_factor(at, all_of_four(gram_chip, "x"))
+
+    crossed = cross(at, momentum, momentum_other, projected, swap_cores(projected))
     right = crossed[0] + sum(from_ahead(crossed[by], "y", NY - by) for by in (1, 2, 3))
 
     def whiten(array):
@@ -374,8 +413,8 @@
     right = gather(right, "z", NZ).reshape(half // NY, rank)
     squares = jnp.sum(jnp.square(right.astype(f32)), axis=0, keepdims=True)
     squares = gather(squares, ("y", "c", "x"), NY * 2 * NX).reshape(NY * 2 * NX, rank)
-    pieces, squares = ring_of_four(right, "y", squares)
-    pieces = pieces + tuple(swap_cores(piece) for piece in pieces)
+    pieces, (squares, swapped) = ring_of_four(right, "y", (squares, swap_cores(right)))
+    pieces = pieces + (swapped,) + tuple(swap_cores(piece) for piece in pieces[1:])
 
     total_rows = rows * NZ * NY * 2
     total_cols = cols * NX

time: 204 us -> 214 us (1.049)
  waiting for transfers between devices: 39.1 us -> 43.7 us
  Pallas kernels: 25.7 us -> 28.3 us
    unnamed x19 -> x17, local copies, waits for them, and re-layouts: 5.33 us -> 9.1 us
    ppermute x11, starting transfers between devices: 14 us -> 17.3 us  [swap_cores(): return lax.ppermute(block, 'c', [(0, 1), (1, 0)])]
    ppermute x11, waiting for transfers between devices: 5.01 us -> 7.79 us  [swap_cores(): return lax.ppermute(block, 'c', [(0, 1), (1, 0)])]
    ppermute x20 -> x19, starting transfers between devices: 31.7 us -> 29.2 us  [from_ahead(): lax.ppermute(block, axis, [((i + by) % parts, i) for i in range(parts)])]
    dynamic_slice x2 -> x1, local copies, waits for them, and re-layouts: 2.21 us -> 0.02 us  [columns(): return lax.dynamic_slice_in_dim(array, of_core * half, half, 1)]
    ppermute x20 -> x19, waiting for transfers between devices: 34.1 us -> 35.9 us  [from_ahead(): lax.ppermute(block, axis, [((i + by) % parts, i) for i in range(parts)])]
    pallas_call x1 -> x2, Pallas kernels: 5.39 us -> 6.73 us  [the longest x1 5.75 us: cross(): pl.pallas_call(cross_kernel, out_shape=[jax.ShapeDtypeStruct((size, rank)...]
  transfers between devices with their start and end apart: 31 -> 30, of which waited for: 15 -> 14; matrix products, arithmetic and copies ran while one was open for 0% -> 2% of each run, Pallas kernels for 8% -> 7%
where the time goes in v1:
time: 214 us
  blocking collectives  77.3 us (36%)
  starting transfers between devices  46.5 us (22%)
  waiting for transfers between devices  43.7 us (20%)
  Pallas kernels  28.3 us (13%)
  local copies, waits for them, and re-layouts  9.25 us (4%)
  matrix products  4.23 us (2%)
  other arithmetic  3.3 us (2%)
    all_to_all x4, blocking collectives, gather(): return lax.all_to_all(copies, axes, 0, 0)  61.6 us
    ppermute x19, waiting for transfers between devices, from_ahead(): lax.ppermute(block, axis, [((i + by) % parts, i) for i in range(parts)])  35.9 us
    ppermute x19, starting transfers between devices, from_ahead(): lax.ppermute(block, axis, [((i + by) % parts, i) for i in range(parts)])  29.2 us
    ppermute x11, starting transfers between devices, swap_cores(): return lax.ppermute(block, 'c', [(0, 1), (1, 0)])  17.3 us
    all_to_all x1, blocking collectives, scatter_sum(): return jnp.sum(lax.all_to_all(pieces, axes, 0, 0).astype(f32), axis=0)  15.8 us
    pallas_call x1, Pallas kernels, inverse_factor(): pl.pallas_call(inverse_factor_kernel, out_shape=jax.ShapeDtypeStruct((ran...  9.93 us
    unnamed x17, local copies, waits for them, and re-layouts  9.1 us
    pallas_call x1, Pallas kernels, finish(): pl.pallas_call(lambda *refs: finish_kernel(scaling, *refs), out_shape=[ou...  7.91 us
  transfers between devices with their start and end apart: 30, of which 14 were waited for; matrix products, arithmetic and copies ran while one was open for 2% of the time, Pallas kernels for 7%

profile of v1, /device:TPU:1, one launch (start us, length us, event | category | flops | bytes accessed | tf_op | source)
XLA Modules:
  0.0 213.6 jit_solution(17668970506871780804)
XLA Ops:
  0.6 3.3 %collective-permute-start = (bf16[256,6656]{1,0:T(8,128)(2,1)}, bf16[256,6656]{1,0:T(8,128)(2,1)S(1)}, u32[]{:S(2)}, u32[]{:S(2)}) collective-permute-start(bf16[256,6656]{1,0:T(8,128)(2,1)} %refs_1_.1), channel_id=1, source_target_pairs={{0,4},{4,0},{1,5},{5,1},{2,6},{6,2},{3,7},{7,3},{8,12},{12,8},{9,1... | collective-permute-start | bytes 10223624 | tf_op jit(solution)/shard_map/ppermute | solution.py:339
  5.0 4.6 %collective-permute-done.1 = bf16[4,3328]{1,0:T(4,128)(2,1)S(1)} collective-permute-done((bf16[4,3328]{1,0:T(4,128)(2,1)S(1)}, bf16[4,3328]{1,0:T(4,128)(2,1)S(1)}, u32[]{:S(2)}, u32[]{:S(2)}) %collective-permute-start.1) | collective-permute-done | bytes 26656 | tf_op jit(solution)/shard_map/ppermute | solution.py:339
  9.8 20.9 %all_to_all.25 = bf16[8,8,3328]{2,1,0:T(8,128)(2,1)} all-to-all(bf16[8,8,3328]{2,1,0:T(8,128)(2,1)S(1)} %broadcast_in_dim.8), channel_id=1, replica_groups=mesh['z'=8,'y'=4,'c'=2,'x'=4] {'z'}, dimensions={0} | all-to-all | bytes 851968 | tf_op jit(solution)/shard_map/all_to_all | solution.py:365
  30.7 1.3 collective-permute-start.4
  32.0 2.6 %collective-permute-start.3 = (bf16[64,3328]{1,0:T(8,128)(2,1)}, bf16[64,3328]{1,0:T(8,128)(2,1)}, u32[]{:S(2)}, u32[]{:S(2)}) collective-permute-start(bf16[64,3328]{1,0:T(8,128)(2,1)} %bitcast.4.refs_0_), channel_id=1, source_target_pairs={{16,0},{24,8},{0,16},{8,24},{17,1},{25,9},{1,17},{9,25},{18,2},{26... | collective-permute-start | bytes 1277960 | tf_op jit(solution)/shard_map/ppermute | solution.py:343
  34.6 1.1 collective-permute-start.2
  35.8 6.1 %collective-permute-done.4.refs_3_ = bf16[64,3328]{1,0:T(8,128)(2,1)} collective-permute-done((bf16[64,3328]{1,0:T(8,128)(2,1)}, bf16[64,3328]{1,0:T(8,128)(2,1)}, u32[]{:S(2)}, u32[]{:S(2)}) %collective-permute-start.4) | collective-permute-done | bytes 426016 | tf_op jit(solution)/shard_map/ppermute | solution.py:343
  41.9 10.2 %collective-permute-done.3.refs_2_ = bf16[64,3328]{1,0:T(8,128)(2,1)} collective-permute-done((bf16[64,3328]{1,0:T(8,128)(2,1)}, bf16[64,3328]{1,0:T(8,128)(2,1)}, u32[]{:S(2)}, u32[]{:S(2)}) %collective-permute-start.3) | collective-permute-done | bytes 426016 | tf_op jit(solution)/shard_map/ppermute | solution.py:343
  52.7 1.7 copy-done.2
  54.5 2.0 copy-done
  56.4 2.0 copy-done.3
  58.4 3.8 %shard_map.49 = (f32[256,256]{1,0:T(8,128)S(1)}, f32[256,256]{1,0:T(8,128)S(1)}) custom-call(s32[4]{0:T(128)S(1)} %pad_add_fusion.at_ref.refs_0_, bf16[256,6656]{1,0:T(8,128)(2,1)S(1)} %copy-done, bf16[256,6656]{1,0:T(8,128)(2,1)S(1)} %copy-done.3, bf16[64,3328]{1,0:T(8,128)(2,1)} %bitcast.4.refs_0_, bf16[64,3328]{1,0:T(8,128)(2,1)} %collective-permute-done.2.refs_1_, ...), custom_call_target="tpu_custom_call" | custom-call | flops 872415232 | bytes 5111808 | tf_op jit(solution)/shard_map/pallas_call | solution.py:169
  62.2 2.2 %collective-permute-start.5 = (f32[256,256]{1,0:T(8,128)S(1)}, f32[256,256]{1,0:T(8,128)S(1)}, u32[]{:S(2)}, u32[]{:S(2)}) collective-permute-start(f32[256,256]{1,0:T(8,128)S(1)} %get-tuple-element.17), channel_id=1, source_target_pairs={{0,4},{4,0},{1,5},{5,1},{2,6},{6,2},{3,7},{7,3},{8,12},{12,8},{9,1... | collective-permute-start | bytes 786440 | tf_op jit(solution)/shard_map/ppermute | solution.py:339
  64.4 1.2 collective-permute-done.5
  65.6 1.3 collective-permute-start.8
  66.9 2.5 %collective-permute-start.7 = (f32[256,256]{1,0:T(8,128)S(1)}, f32[256,256]{1,0:T(8,128)S(1)}, u32[]{:S(2)}, u32[]{:S(2)}) collective-permute-start(f32[256,256]{1,0:T(8,128)S(1)} %add.40.own_ref), channel_id=1, source_target_pairs={{2,0},{3,1},{0,2},{1,3},{6,4},{7,5},{4,6},{5,7},{10,8},{11,9},{8,1... | collective-permute-start | bytes 786440 | tf_op jit(solution)/shard_map/ppermute | solution.py:343
  69.3 1.1 collective-permute-start.6
  70.5 3.9 %collective-permute-done.8.three_ref = f32[256,256]{1,0:T(8,128)S(1)} collective-permute-done((f32[256,256]{1,0:T(8,128)S(1)}, f32[256,256]{1,0:T(8,128)S(1)}, u32[]{:S(2)}, u32[]{:S(2)}) %collective-permute-start.8) | collective-permute-done | bytes 262176 | tf_op jit(solution)/shard_map/ppermute | solution.py:343
  74.4 6.6 %collective-permute-done.7.two_ref = f32[256,256]{1,0:T(8,128)S(1)} collective-permute-done((f32[256,256]{1,0:T(8,128)S(1)}, f32[256,256]{1,0:T(8,128)S(1)}, u32[]{:S(2)}, u32[]{:S(2)}) %collective-permute-start.7) | collective-permute-done | bytes 262176 | tf_op jit(solution)/shard_map/ppermute | solution.py:343
  82.0 1.3 collective-permute-start.17
  83.4 1.1 collective-permute-done.9
  85.4 1.8 collective-permute-start.11
  87.2 1.1 collective-permute-start.10
  88.3 2.0 copy-done.4
  90.3 5.8 %shard_map.52 = (f32[832,256]{1,0:T(8,128)S(1)}, f32[832,256]{1,0:T(8,128)}, f32[832,256]{1,0:T(8,128)}, f32[832,256]{1,0:T(8,128)}) custom-call(s32[4]{0:T(128)S(1)} %pad_add_fusion.at_ref.refs_0_, bf16[256,6656]{1,0:T(8,128)(2,1)S(1)} %copy-done.1, bf16[256,6656]{1,0:T(8,128)(2,1)S(1)} %copy-done.4, f32[256,256]{1,0:T(8,128)S(1)} %get-tuple-element.18.left_mine_ref, ...), custom_call_target="tpu_custom_call" | custom-call | flops 2617245696 | bytes 10223616 | tf_op jit(solution)/shard_map/pallas_call | solution.py:246
  97.0 2.1 collective-permute-start.19
  99.1 1.8 collective-permute-start.20
  100.9 12.3 %all_to_all.26 = f32[8,32,256]{2,1,0:T(8,128)} all-to-all(f32[8,32,256]{2,1,0:T(8,128)S(1)} %broadcast_in_dim.9), channel_id=1, replica_groups=mesh['z'=8,'y'=4,'c'=2,'x'=4] {'z'}, dimensions={0} | all-to-all | bytes 524288 | tf_op jit(solution)/shard_map/all_to_all | solution.py:365
  114.2 3.7 %collective-permute-start.13 = (f32[32,256]{1,0:T(8,128)S(1)}, f32[32,256]{1,0:T(8,128)S(1)}, u32[]{:S(2)}, u32[]{:S(2)}) collective-permute-start(f32[32,256]{1,0:T(8,128)S(1)} %reduce_sum.30), channel_id=1, source_target_pairs={{0,4},{4,0},{1,5},{5,1},{2,6},{6,2},{3,7},{7,3},{8,12},{12,8},{9,1... | collective-permute-start | bytes 98312 | tf_op jit(solution)/shard_map/ppermute | solution.py:339
  118.8 1.1 collective-permute-start.16
  119.8 2.1 collective-permute-start.15
  121.9 1.6 collective-permute-done.16.last_ref
  124.3 1.3 collective-permute-done.15.across_ref
  125.5 1.5 collective-permute-done.14.next_ref
  127.0 9.9 %shard_map.51 = f32[256,256]{1,0:T(8,128)S(1)} custom-call(s32[4]{0:T(128)S(1)} %pad_add_fusion.at_ref.refs_0_, f32[64,256]{1,0:T(8,128)S(1)} %pad_maximum_fusion.own_ref, f32[64,256]{1,0:T(8,128)S(1)} %collective-permute-done.14.next_ref, f32[64,256]{1,0:T(8,128)S(1)} %collective-permute-done.15.across_ref, f32[64,256]{1,0:T(8,128)S(1)} %collective-permute-done.16.last_ref), custom_call_target="tpu_custom_call" | custom-call | tf_op jit(solution)/shard_map/pallas_call | solution.py:127
  137.7 2.8 %convolution_convert_fusion = bf16[832,256]{1,0:T(8,128)(2,1)S(1)} fusion(f32[256,256]{1,0:T(8,128)S(1)} %shard_map.51, f32[832,256]{1,0:T(8,128)} %copy-done.6, f32[832,256]{1,0:T(8,128)} %collective-permute-done.20, f32[832,256]{1,0:T(8,128)} %collective-permute-done.18, f32[832,256]{1,0:T(8,128)} %collective-permute-done.19), kind=kOutput, calls=%fused_computation | convolution fusion | flops 655163392 | bytes 4096000 | tf_op jit(solution)/shard_map/dot_general | solution.py:407
  140.5 15.8 %all_to_all.27 = bf16[8,104,256]{2,1,0:T(8,128)(2,1)} all-to-all(bf16[8,104,256]{2,1,0:T(8,128)(2,1)S(1)} %bitcast.18), channel_id=1, replica_groups=mesh['z'=8,'y'=4,'c'=2,'x'=4] {'z'}, dimensions={0} | all-to-all | bytes 851968 | tf_op jit(solution)/shard_map/all_to_all | solution.py:370
  156.2 1.1 reduce_sum.31
  157.3 15.5 %all_to_all.28 = bf16[8,104,256]{2,1,0:T(8,128)(2,1)S(1)} all-to-all(bf16[8,104,256]{2,1,0:T(8,128)(2,1)S(1)} %broadcast_in_dim.10), channel_id=1, replica_groups=mesh['z'=8,'y'=4,'c'=2,'x'=4] {'z'}, dimensions={0} | all-to-all | bytes 851968 | tf_op jit(solution)/shard_map/all_to_all | solution.py:365
  172.9 4.3 %collective-permute-start.23 = (bf16[832,256]{1,0:T(8,128)(2,1)S(1)}, bf16[832,256]{1,0:T(8,128)(2,1)S(1)}, u32[]{:S(2)}, u32[]{:S(2)}) collective-permute-start(bf16[832,256]{1,0:T(8,128)(2,1)S(1)} %bitcast.13), channel_id=1, source_target_pairs={{0,4},{4,0},{1,5},{5,1},{2,6},{6,2},{3,7},{7,3},{8,12},{12,8},{9,1... | collective-permute-start | bytes 1277960 | tf_op jit(solution)/shard_map/ppermute | solution.py:339
  177.2 3.7 %collective-permute-start.22 = (bf16[832,256]{1,0:T(8,128)(2,1)S(1)}, bf16[832,256]{1,0:T(8,128)(2,1)S(1)}, u32[]{:S(2)}, u32[]{:S(2)}) collective-permute-start(bf16[832,256]{1,0:T(8,128)(2,1)S(1)} %bitcast.14), channel_id=1, source_target_pairs={{24,0},{0,8},{8,16},{16,24},{25,1},{1,9},{9,17},{17,25},{26,2},{2,... | collective-permute-start | bytes 1277960 | tf_op jit(solution)/shard_map/ppermute | solution.py:343
  180.9 1.1 collective-permute-start.21
  182.2 12.8 %all_to_all.29 = f32[32,1,256]{2,1,0:T(1,128)S(1)} all-to-all(f32[32,1,256]{2,1,0:T(1,128)S(1)} %broadcast_in_dim.11), channel_id=1, replica_groups=mesh['z'=8,'y'=4,'c'=2,'x'=4] {'y','c','x'}, dimensions={0} | all-to-all | bytes 65536 | tf_op jit(solution)/shard_map/all_to_all | solution.py:365
  195.5 2.4 %collective-permute-start.25 = (bf16[416,256]{1,0:T(8,128)(2,1)S(1)}, bf16[416,256]{1,0:T(8,128)(2,1)S(1)}, u32[]{:S(2)}, u32[]{:S(2)}) collective-permute-start(bf16[416,256]{1,0:T(8,128)(2,1)S(1)} %slice.7), channel_id=1, source_target_pairs={{8,0},{16,8},{24,16},{0,24},{9,1},{17,9},{25,17},{1,25},{10,2},{18... | collective-permute-start | bytes 638984 | tf_op jit(solution)/shard_map/ppermute | solution.py:343
  198.9 3.9 %collective-permute-done.24.refs_7_ = bf16[416,256]{1,0:T(8,128)(2,1)S(1)} collective-permute-done((bf16[416,256]{1,0:T(8,128)(2,1)S(1)}, bf16[416,256]{1,0:T(8,128)(2,1)S(1)}, u32[]{:S(2)}, u32[]{:S(2)}) %collective-permute-start.24) | collective-permute-done | bytes 213024 | tf_op jit(solution)/shard_map/ppermute | solution.py:343
  202.8 1.2 collective-permute-start.28
  204.0 1.4 fusion.3.refs_2_
  205.5 7.9 %shard_map.53 = (bf16[256,6656]{1,0:T(8,128)(2,1)}, bf16[256,6656]{1,0:T(8,128)(2,1)}, f32[4,6656]{1,0:T(4,128)}) custom-call(s32[4]{0:T(128)S(1)} %pad_add_fusion.at_ref.refs_0_, bf16[256,6656]{1,0:T(8,128)(2,1)S(1)} %copy-done.1, f32[256,256]{1,0:T(8,128)S(1)} %fusion.3.refs_2_, f32[32,256]{1,0:T(8,128)S(1)} %bitcast.17, bf16[832,256]{1,0:T(8,128)(2,1)S(1)} %bitcast.16, ...), custom_call_target="tpu_custom_call" | custom-call | flops 1744830464 | bytes 13631488 | tf_op jit(solution)/shard_map/pallas_call | solution.py:313
  (59 shorter events, 9.7 us)
Async XLA Ops:
  0.6 52.1 %collective-permute-start = (bf16[256,6656]{1,0:T(8,128)(2,1)}, bf16[256,6656]{1,0:T(8,128)(2,1)S(1)}, u32[]{:S(2)}, u32[]{:S(2)}) collective-permute-start(bf16[256,6656]{1,0:T(8,128)(2,1)} %refs_1_.1), channel_id=1, source_target_pairs={{0,4},{4,0},{1,5},{5,1},{2,6},{6,2},{3,7},{7,3},{8,12},{12,8},{9,1... | collective-permute-start | bytes 10223624 | tf_op jit(solution)/shard_map/ppermute | solution.py:339
  4.9 4.8 %collective-permute-start.1 = (bf16[4,3328]{1,0:T(4,128)(2,1)S(1)}, bf16[4,3328]{1,0:T(4,128)(2,1)S(1)}, u32[]{:S(2)}, u32[]{:S(2)}) collective-permute-start(bf16[4,3328]{1,0:T(4,128)(2,1)S(1)} %constant_dynamic-slice_fusion), channel_id=1, source_target_pairs={{0,4},{4,0},{1,5},{5,1},{2,6},{6,2},{3,7},{7,3},{8,12},{12,8},{9,1... | collective-permute-start | bytes 79880 | tf_op jit(solution)/shard_map/ppermute | solution.py:339
  30.7 11.2 %collective-permute-start.4 = (bf16[64,3328]{1,0:T(8,128)(2,1)}, bf16[64,3328]{1,0:T(8,128)(2,1)}, u32[]{:S(2)}, u32[]{:S(2)}) collective-permute-start(bf16[64,3328]{1,0:T(8,128)(2,1)} %bitcast.4.refs_0_), channel_id=1, source_target_pairs={{24,0},{0,8},{8,16},{16,24},{25,1},{1,9},{9,17},{17,25},{26,2},{2,... | collective-permute-start | bytes 1277960 | tf_op jit(solution)/shard_map/ppermute | solution.py:343
  32.0 20.2 %collective-permute-start.3 = (bf16[64,3328]{1,0:T(8,128)(2,1)}, bf16[64,3328]{1,0:T(8,128)(2,1)}, u32[]{:S(2)}, u32[]{:S(2)}) collective-permute-start(bf16[64,3328]{1,0:T(8,128)(2,1)} %bitcast.4.refs_0_), channel_id=1, source_target_pairs={{16,0},{24,8},{0,16},{8,24},{17,1},{25,9},{1,17},{9,25},{18,2},{26... | collective-permute-start | bytes 1277960 | tf_op jit(solution)/shard_map/ppermute | solution.py:343
  34.6 18.1 %collective-permute-start.2 = (bf16[64,3328]{1,0:T(8,128)(2,1)}, bf16[64,3328]{1,0:T(8,128)(2,1)}, u32[]{:S(2)}, u32[]{:S(2)}) collective-permute-start(bf16[64,3328]{1,0:T(8,128)(2,1)} %bitcast.4.refs_0_), channel_id=1, source_target_pairs={{8,0},{16,8},{24,16},{0,24},{9,1},{17,9},{25,17},{1,25},{10,2},{18... | collective-permute-start | bytes 1277960 | tf_op jit(solution)/shard_map/ppermute | solution.py:343
  52.7 1.8 copy-start.2
  54.5 2.0 copy-start
  56.4 2.0 copy-start.3
  58.4 29.9 %copy-start.1 = (bf16[256,6656]{1,0:T(8,128)(2,1)S(1)}, bf16[256,6656]{1,0:T(8,128)(2,1)}, u32[]{:S(2)}) copy-start(bf16[256,6656]{1,0:T(8,128)(2,1)} %refs_1_.1) | copy-start | bytes 10223620
  62.2 3.4 %collective-permute-start.5 = (f32[256,256]{1,0:T(8,128)S(1)}, f32[256,256]{1,0:T(8,128)S(1)}, u32[]{:S(2)}, u32[]{:S(2)}) collective-permute-start(f32[256,256]{1,0:T(8,128)S(1)} %get-tuple-element.17), channel_id=1, source_target_pairs={{0,4},{4,0},{1,5},{5,1},{2,6},{6,2},{3,7},{7,3},{8,12},{12,8},{9,1... | collective-permute-start | bytes 786440 | tf_op jit(solution)/shard_map/ppermute | solution.py:339
  65.6 8.8 %collective-permute-start.8 = (f32[256,256]{1,0:T(8,128)S(1)}, f32[256,256]{1,0:T(8,128)S(1)}, u32[]{:S(2)}, u32[]{:S(2)}) collective-permute-start(f32[256,256]{1,0:T(8,128)S(1)} %add.40.own_ref), channel_id=1, source_target_pairs={{3,0},{0,1},{1,2},{2,3},{7,4},{4,5},{5,6},{6,7},{11,8},{8,9},{9,10... | collective-permute-start | bytes 786440 | tf_op jit(solution)/shard_map/ppermute | solution.py:343
  66.9 14.1 %collective-permute-start.7 = (f32[256,256]{1,0:T(8,128)S(1)}, f32[256,256]{1,0:T(8,128)S(1)}, u32[]{:S(2)}, u32[]{:S(2)}) collective-permute-start(f32[256,256]{1,0:T(8,128)S(1)} %add.40.own_ref), channel_id=1, source_target_pairs={{2,0},{3,1},{0,2},{1,3},{6,4},{7,5},{4,6},{5,7},{10,8},{11,9},{8,1... | collective-permute-start | bytes 786440 | tf_op jit(solution)/shard_map/ppermute | solution.py:343
  69.3 11.7 %collective-permute-start.6 = (f32[256,256]{1,0:T(8,128)S(1)}, f32[256,256]{1,0:T(8,128)S(1)}, u32[]{:S(2)}, u32[]{:S(2)}) collective-permute-start(f32[256,256]{1,0:T(8,128)S(1)} %add.40.own_ref), channel_id=1, source_target_pairs={{1,0},{2,1},{3,2},{0,3},{5,4},{6,5},{7,6},{4,7},{9,8},{10,9},{11,1... | collective-permute-start | bytes 786440 | tf_op jit(solution)/shard_map/ppermute | solution.py:343
  82.0 14.0 %copy-start.7 = (f32[256,256]{1,0:T(8,128)}, f32[256,256]{1,0:T(8,128)S(1)}, u32[]{:S(2)}) copy-start(f32[256,256]{1,0:T(8,128)S(1)} %get-tuple-element.18.left_mine_ref) | copy-start | bytes 786436
  82.0 6.3 %collective-permute-start.17 = (f32[256,256]{1,0:T(8,128)S(1)}, f32[256,256]{1,0:T(8,128)S(1)}, u32[]{:S(2)}, u32[]{:S(2)}) collective-permute-start(f32[256,256]{1,0:T(8,128)S(1)} %get-tuple-element.18.left_mine_ref), channel_id=1, source_target_pairs={{0,4},{4,0},{1,5},{5,1},{2,6},{6,2},{3,7},{7,3},{8,12},{12,8},{9,1... | collective-permute-start | bytes 786440 | tf_op jit(solution)/shard_map/ppermute | solution.py:339
  83.3 1.2 collective-permute-start.9
  84.5 14.5 %collective-permute-start.12 = (f32[32,256]{1,0:T(8,128)S(1)}, f32[32,256]{1,0:T(8,128)S(1)}, u32[]{:S(2)}, u32[]{:S(2)}) collective-permute-start(f32[32,256]{1,0:T(8,128)S(1)} %add.41), channel_id=1, source_target_pairs={{24,0},{0,8},{8,16},{16,24},{25,1},{1,9},{9,17},{17,25},{26,2},{2,... | collective-permute-start | bytes 98312 | tf_op jit(solution)/shard_map/ppermute | solution.py:343
  85.4 15.5 %collective-permute-start.11 = (f32[32,256]{1,0:T(8,128)S(1)}, f32[32,256]{1,0:T(8,128)S(1)}, u32[]{:S(2)}, u32[]{:S(2)}) collective-permute-start(f32[32,256]{1,0:T(8,128)S(1)} %add.41), channel_id=1, source_target_pairs={{8,0},{16,8},{24,16},{0,24},{9,1},{17,9},{25,17},{1,25},{10,2},{18... | collective-permute-start | bytes 98312 | tf_op jit(solution)/shard_map/ppermute | solution.py:343
  87.2 13.7 %collective-permute-start.10 = (f32[32,256]{1,0:T(8,128)S(1)}, f32[32,256]{1,0:T(8,128)S(1)}, u32[]{:S(2)}, u32[]{:S(2)}) collective-permute-start(f32[32,256]{1,0:T(8,128)S(1)} %add.41), channel_id=1, source_target_pairs={{16,0},{24,8},{0,16},{8,24},{17,1},{25,9},{1,17},{9,25},{18,2},{26... | collective-permute-start | bytes 98312 | tf_op jit(solution)/shard_map/ppermute | solution.py:343
  88.3 2.0 copy-start.4
  96.0 0.9 copy-start.6
  96.9 40.0 %collective-permute-start.18 = (f32[832,256]{1,0:T(8,128)}, f32[832,256]{1,0:T(8,128)}, u32[]{:S(2)}, u32[]{:S(2)}) collective-permute-start(f32[832,256]{1,0:T(8,128)} %get-tuple-element.22), channel_id=1, source_target_pairs={{24,0},{0,8},{8,16},{16,24},{25,1},{1,9},{9,17},{17,25},{26,2},{2,... | collective-permute-start | bytes 2555912 | tf_op jit(solution)/shard_map/ppermute | solution.py:343
  97.0 40.0 %collective-permute-start.19 = (f32[832,256]{1,0:T(8,128)}, f32[832,256]{1,0:T(8,128)}, u32[]{:S(2)}, u32[]{:S(2)}) collective-permute-start(f32[832,256]{1,0:T(8,128)} %get-tuple-element.23), channel_id=1, source_target_pairs={{16,0},{24,8},{0,16},{8,24},{17,1},{25,9},{1,17},{9,25},{18,2},{26... | collective-permute-start | bytes 2555912 | tf_op jit(solution)/shard_map/ppermute | solution.py:343
  99.1 38.1 %collective-permute-start.20 = (f32[832,256]{1,0:T(8,128)}, f32[832,256]{1,0:T(8,128)}, u32[]{:S(2)}, u32[]{:S(2)}) collective-permute-start(f32[832,256]{1,0:T(8,128)} %get-tuple-element.24), channel_id=1, source_target_pairs={{8,0},{16,8},{24,16},{0,24},{9,1},{17,9},{25,17},{1,25},{10,2},{18... | collective-permute-start | bytes 2555912 | tf_op jit(solution)/shard_map/ppermute | solution.py:343
  114.2 4.6 %collective-permute-start.13 = (f32[32,256]{1,0:T(8,128)S(1)}, f32[32,256]{1,0:T(8,128)S(1)}, u32[]{:S(2)}, u32[]{:S(2)}) collective-permute-start(f32[32,256]{1,0:T(8,128)S(1)} %reduce_sum.30), channel_id=1, source_target_pairs={{0,4},{4,0},{1,5},{5,1},{2,6},{6,2},{3,7},{7,3},{8,12},{12,8},{9,1... | collective-permute-start | bytes 98312 | tf_op jit(solution)/shard_map/ppermute | solution.py:339
  118.8 4.7 %collective-permute-start.16 = (f32[64,256]{1,0:T(8,128)S(1)}, f32[64,256]{1,0:T(8,128)S(1)}, u32[]{:S(2)}, u32[]{:S(2)}) collective-permute-start(f32[64,256]{1,0:T(8,128)S(1)} %pad_maximum_fusion.own_ref), channel_id=1, source_target_pairs={{3,0},{0,1},{1,2},{2,3},{7,4},{4,5},{5,6},{6,7},{11,8},{8,9},{9,10... | collective-permute-start | bytes 196616 | tf_op jit(solution)/shard_map/ppermute | solution.py:343
  119.8 5.7 %collective-permute-start.15 = (f32[64,256]{1,0:T(8,128)S(1)}, f32[64,256]{1,0:T(8,128)S(1)}, u32[]{:S(2)}, u32[]{:S(2)}) collective-permute-start(f32[64,256]{1,0:T(8,128)S(1)} %pad_maximum_fusion.own_ref), channel_id=1, source_target_pairs={{2,0},{3,1},{0,2},{1,3},{6,4},{7,5},{4,6},{5,7},{10,8},{11,9},{8,1... | collective-permute-start | bytes 196616 | tf_op jit(solution)/shard_map/ppermute | solution.py:343
  123.5 3.5 %collective-permute-start.14 = (f32[64,256]{1,0:T(8,128)S(1)}, f32[64,256]{1,0:T(8,128)S(1)}, u32[]{:S(2)}, u32[]{:S(2)}) collective-permute-start(f32[64,256]{1,0:T(8,128)S(1)} %pad_maximum_fusion.own_ref), channel_id=1, source_target_pairs={{1,0},{2,1},{3,2},{0,3},{5,4},{6,5},{7,6},{4,7},{9,8},{10,9},{11,1... | collective-permute-start | bytes 196616 | tf_op jit(solution)/shard_map/ppermute | solution.py:343
  137.0 0.7 copy-start.5
  172.9 22.2 %collective-permute-start.23 = (bf16[832,256]{1,0:T(8,128)(2,1)S(1)}, bf16[832,256]{1,0:T(8,128)(2,1)S(1)}, u32[]{:S(2)}, u32[]{:S(2)}) collective-permute-start(bf16[832,256]{1,0:T(8,128)(2,1)S(1)} %bitcast.13), channel_id=1, source_target_pairs={{0,4},{4,0},{1,5},{5,1},{2,6},{6,2},{3,7},{7,3},{8,12},{12,8},{9,1... | collective-permute-start | bytes 1277960 | tf_op jit(solution)/shard_map/ppermute | solution.py:339
  177.2 17.9 %collective-permute-start.22 = (bf16[832,256]{1,0:T(8,128)(2,1)S(1)}, bf16[832,256]{1,0:T(8,128)(2,1)S(1)}, u32[]{:S(2)}, u32[]{:S(2)}) collective-permute-start(bf16[832,256]{1,0:T(8,128)(2,1)S(1)} %bitcast.14), channel_id=1, source_target_pairs={{24,0},{0,8},{8,16},{16,24},{25,1},{1,9},{9,17},{17,25},{26,2},{2,... | collective-permute-start | bytes 1277960 | tf_op jit(solution)/shard_map/ppermute | solution.py:343
  180.9 14.1 %collective-permute-start.21 = (bf16[832,256]{1,0:T(8,128)(2,1)S(1)}, bf16[832,256]{1,0:T(8,128)(2,1)S(1)}, u32[]{:S(2)}, u32[]{:S(2)}) collective-permute-start(bf16[832,256]{1,0:T(8,128)(2,1)S(1)} %bitcast.15), channel_id=1, source_target_pairs={{8,0},{16,8},{24,16},{0,24},{9,1},{17,9},{25,17},{1,25},{10,2},{18... | collective-permute-start | bytes 1277960 | tf_op jit(solution)/shard_map/ppermute | solution.py:343
  195.1 7.7 %collective-permute-start.24 = (bf16[416,256]{1,0:T(8,128)(2,1)S(1)}, bf16[416,256]{1,0:T(8,128)(2,1)S(1)}, u32[]{:S(2)}, u32[]{:S(2)}) collective-permute-start(bf16[416,256]{1,0:T(8,128)(2,1)S(1)} %slice.6), channel_id=1, source_target_pairs={{24,0},{0,8},{8,16},{16,24},{25,1},{1,9},{9,17},{17,25},{26,2},{2,... | collective-permute-start | bytes 638984 | tf_op jit(solution)/shard_map/ppermute | solution.py:343
  195.5 8.5 %collective-permute-start.25 = (bf16[416,256]{1,0:T(8,128)(2,1)S(1)}, bf16[416,256]{1,0:T(8,128)(2,1)S(1)}, u32[]{:S(2)}, u32[]{:S(2)}) collective-permute-start(bf16[416,256]{1,0:T(8,128)(2,1)S(1)} %slice.7), channel_id=1, source_target_pairs={{8,0},{16,8},{24,16},{0,24},{9,1},{17,9},{25,17},{1,25},{10,2},{18... | collective-permute-start | bytes 638984 | tf_op jit(solution)/shard_map/ppermute | solution.py:343
  197.9 7.6 %collective-permute-start.26 = (bf16[832,256]{1,0:T(8,128)(2,1)S(1)}, bf16[832,256]{1,0:T(8,128)(2,1)S(1)}, u32[]{:S(2)}, u32[]{:S(2)}) collective-permute-start(bf16[832,256]{1,0:T(8,128)(2,1)S(1)} %collective-permute-done.21.refs_5_), channel_id=1, source_target_pairs={{0,4},{4,0},{1,5},{5,1},{2,6},{6,2},{3,7},{7,3},{8,12},{12,8},{9,1... | collective-permute-start | bytes 1277960 | tf_op jit(solution)/shard_map/ppermute | solution.py:339
  198.9 6.6 %collective-permute-start.27 = (bf16[832,256]{1,0:T(8,128)(2,1)S(1)}, bf16[832,256]{1,0:T(8,128)(2,1)S(1)}, u32[]{:S(2)}, u32[]{:S(2)}) collective-permute-start(bf16[832,256]{1,0:T(8,128)(2,1)S(1)} %collective-permute-done.22.refs_6_), channel_id=1, source_target_pairs={{0,4},{4,0},{1,5},{5,1},{2,6},{6,2},{3,7},{7,3},{8,12},{12,8},{9,1... | collective-permute-start | bytes 1277960 | tf_op jit(solution)/shard_map/ppermute | solution.py:339
  202.8 2.7 %collective-permute-start.28 = (bf16[416,256]{1,0:T(8,128)(2,1)S(1)}, bf16[416,256]{1,0:T(8,128)(2,1)S(1)}, u32[]{:S(2)}, u32[]{:S(2)}) collective-permute-start(bf16[416,256]{1,0:T(8,128)(2,1)S(1)} %collective-permute-done.24.refs_7_), channel_id=1, source_target_pairs={{0,4},{4,0},{1,5},{5,1},{2,6},{6,2},{3,7},{7,3},{8,12},{12,8},{9,1... | collective-permute-start | bytes 638984 | tf_op jit(solution)/shard_map/ppermute | solution.py:339
  204.0 1.5 collective-permute-start.29

commit v2 on v0

--- a/solution.py
+++ b/solution.py
@@ -131,16 +131,16 @@
         out_specs=VMEM,
         scratch_shapes=[pltpu.VMEM((rows, rank), f32) for rows in (rank, rank // 2, rank // 2)],
         compiler_params=pltpu.CompilerParams(vmem_limit_bytes=8 * MIB),
+        cost_estimate=pl.CostEstimate(flops=10**9, bytes_accessed=2**20, transcendentals=0),
     )(at, *pieces)
 
 
 def project_kernel(at_ref, mine_ref, other_ref, *refs):
-    pieces, (out_mine_ref, out_other_ref, basis_ref) = refs[:5], refs[5:]
-    per_y = pieces[0].shape[0]
-    for n, ref in enumerate(pieces):
+    pieces, (out_mine_ref, out_other_ref, basis_ref) = refs[:NY], refs[NY:]
+    for by, ref in enumerate(pieces):
         size = ref.shape[0]
-        start = ahead(at_ref[AT_Y], RING_FROM[n], NY) * per_y + (size if n == 4 else 0)
-        basis_ref[pl.ds(pl.multiple_of(start, size), size), :] = ref[...]
+        start = pl.multiple_of(ahead(at_ref[AT_Y], by, NY) * size, size)
+        basis_ref[pl.ds(start, size), :] = ref[...]
     width = mine_ref.shape[1] // 2
     out_mine_ref[...] = jnp.zeros_like(out_mine_ref)
     out_other_ref[...] = jnp.zeros_like(out_other_ref)
@@ -163,7 +163,7 @@
     return pl.pallas_call(
         project_kernel,
         out_shape=[jax.ShapeDtypeStruct((rows, rank), f32)] * 2,
-        in_specs=[SMEM] + [VMEM] * 7,
+        in_specs=[SMEM] + [VMEM] * 6,
         out_specs=[VMEM, VMEM],
         scratch_shapes=[pltpu.VMEM((rank, cols), bf16)],
         compiler_params=pltpu.CompilerParams(vmem_limit_bytes=12 * MIB),
@@ -171,6 +171,110 @@
             flops=4 * rows * cols * rank, bytes_accessed=6 * rows * cols, transcendentals=0
         ),
     )(at, mine, other, *pieces)
+
+
+def small(kernel, out, *args):
+    specs = [SMEM if arg.dtype == jnp.int32 else VMEM for arg in args]
+    return pl.pallas_call(
+        kernel,
+        out_shape=out,
+        in_specs=specs,
+        out_specs=VMEM,
+        compiler_params=pltpu.CompilerParams(vmem_limit_bytes=8 * MIB),
+        cost_estimate=pl.CostEstimate(flops=2**20, bytes_accessed=2**20, transcendentals=0),
+    )(*args)
+
+
+def add(one, two):
+    def kernel(one_ref, two_ref, out_ref):
+        out_ref[...] = one_ref[...] + two_ref[...]
+
+    return small(kernel, jax.ShapeDtypeStruct(one.shape, f32), one, two)
+
+
+def sum_four_copies(pieces, copies):
+    def kernel(own_ref, one_ref, two_ref, three_ref, out_ref):
+        total = (own_ref[...] + two_ref[...]) + (one_ref[...] + three_ref[...])
+        for n in range(copies):
+            out_ref[n] = total
+
+    return small(kernel, jax.ShapeDtypeStruct((copies,) + pieces[0].shape, f32), *pieces)
+
+
+def sum_copies(pieces, copies):
+    def kernel(pieces_ref, out_ref):
+        total = jnp.sum(pieces_ref[...].astype(f32), axis=0).astype(pieces_ref.dtype)
+        for n in range(copies):
+            out_ref[n] = total
+
+    shape = (copies,) + pieces.shape[1:]
+    return small(kernel, jax.ShapeDtypeStruct(shape, pieces.dtype), pieces)
+
+
+def basis_copies(at, basis, received, copies):
+    shard_rank, half = received.shape
+
+    def kernel(at_ref, basis_ref, received_ref, out_ref):
+        core = at_ref[AT_CORE]
+        own = basis_ref[:, pl.ds(pl.multiple_of(core * half, half), half)]
+        other = received_ref[...]
+        first = jnp.where(core == 0, own, other)
+        second = jnp.where(core == 0, other, own)
+        chip = jnp.concatenate([first, second], axis=0).astype(bf16)
+        for n in range(copies):
+            out_ref[n] = chip
+
+    return small(kernel, jax.ShapeDtypeStruct((copies, 2 * shard_rank, half), bf16), at, basis, received)
+
+
+def square_copies(right, copies):
+    rank = right.shape[1]
+
+    def kernel(right_ref, out_ref):
+        right = right_ref[...].astype(f32)
+        out_ref[...] = jnp.broadcast_to(
+            jnp.sum(right * right, axis=0, keepdims=True), out_ref.shape
+        )
+
+    return small(kernel, jax.ShapeDtypeStruct((copies * 8, rank), f32), right)
+
+
+def whiten(inverse, pieces, out):
+    def kernel(inverse_ref, *refs):
+        total = refs[0][...]
+        for ref in refs[1:-1]:
+            total = total + ref[...]
+        refs[-1][...] = lax.dot_general(
+            total, inverse_ref[...], BOTH_LAST, preferred_element_type=f32, precision=HIGHEST
+        ).astype(out)
+
+    return small(kernel, jax.ShapeDtypeStruct(pieces[0].shape, out), inverse, *pieces)
+
+
+def gram_kernel(at_ref, own_ref, one_ref, two_ref, three_ref, projected_ref, keep_ref, send_ref, gram_ref):
+    projected = (own_ref[...] + two_ref[...]) + (one_ref[...] + three_ref[...])
+    projected_ref[...] = projected
+    gram_ref[...] = lax.dot_general(
+        projected, projected, BOTH_FIRST, preferred_element_type=f32, precision=HIGHEST
+    )
+    part = keep_ref.shape[0]
+    for other, ref in enumerate((keep_ref, send_ref)):
+        place = at_ref[AT_X] * 2 + (at_ref[AT_CORE] + other) % 2
+        ref[...] = gram_ref[pl.ds(pl.multiple_of(place * part, part), part), :]
+
+
+def gram_rows_of(at, pieces):
+    rows, rank = pieces[0].shape
+    part = jax.ShapeDtypeStruct((rank // (NX * 2), rank), f32)
+    return pl.pallas_call(
+        gram_kernel,
+        out_shape=[jax.ShapeDtypeStruct((rows, rank), f32), part, part],
+        in_specs=[SMEM] + [VMEM] * 4,
+        out_specs=[VMEM] * 3,
+        scratch_shapes=[pltpu.VMEM((rank, rank), f32)],
+        compiler_params=pltpu.CompilerParams(vmem_limit_bytes=8 * MIB),
+        cost_estimate=pl.CostEstimate(flops=2**28, bytes_accessed=2**20, transcendentals=0),
+    )(at, *pieces)
 
 
 def cross_kernel(at_ref, mine_ref, other_ref, left_mine_ref, left_other_ref, *refs):
@@ -237,7 +341,7 @@
             copy.start()
             copies.append(copy)
         solved = solved_ref[...]
-        squares = jnp.sum(squares_ref[...], axis=0, keepdims=True)
+        squares = jnp.sum(squares_ref[...], axis=0, keepdims=True) / 8
         inverse_lengths = lax.rsqrt(squares + 1e-06)
         left_ref[:rows, :] = solved.astype(bf16)
         left_ref[rows : 2 * rows, :] = (solved * (scaling * inverse_lengths)).astype(bf16)
@@ -298,9 +402,8 @@
     return lax.ppermute(block, axis, [((i + by) % parts, i) for i in range(parts)])
 
 
-def sum_four(block, axis):
-    one, two, three = (from_ahead(block, axis, by) for by in (1, 2, 3))
-    return (block + two) + (one + three)
+def all_of_four(block, axis):
+    return [block] + [from_ahead(block, axis, by) for by in (1, 2, 3)]
 
 
 def ring_of_four(block, axis, beside=None):
@@ -311,14 +414,8 @@
     return (block, one, three) + across, beside
 
 
-def gather(block, axes, parts):
-    copies = jnp.broadcast_to(block[None], (parts,) + block.shape)
-    return lax.all_to_all(copies, axes, 0, 0)
-
-
-def scatter_sum(block, axes, parts):
-    pieces = block.reshape((parts, block.shape[0] // parts) + block.shape[1:])
-    return jnp.sum(lax.all_to_all(pieces, axes, 0, 0).astype(f32), axis=0)
+def exchange(pieces, axes):
+    return lax.all_to_all(pieces, axes, 0, 0)
 
 
 def per_device(momentum, q_basis):
@@ -330,52 +427,39 @@
     position = (lax.axis_index("z") * NY + at_y) * 2 + core
     at = jnp.stack([at_y, core, at_x, position * shard_rank]).astype(jnp.int32)
 
+
     def columns(array, of_core):
         return lax.dynamic_slice_in_dim(array, of_core * half, half, 1)
 
-    basis_half = q_basis.astype(bf16)
-    basis_own = columns(basis_half, core)
-    basis_other = swap_cores(columns(basis_half, 1 - core))
-    basis_chip = jnp.concatenate(
-        [jnp.where(core == 0, basis_own, basis_other), jnp.where(core == 0, basis_other, basis_own)]
-    )
-    later, basis_chip = lax.optimization_barrier((momentum, basis_chip))
+    received = swap_cores(columns(q_basis, 1 - core))
+    later, received = lax.optimization_barrier((momentum, received))
     mine = columns(later, core)
     other = swap_cores(columns(later, 1 - core))
 
-    basis_z = gather(basis_chip, "z", NZ).reshape(rank // NY, half)
-    basis, other = ring_of_four(basis_z, "y", other)
+    basis = exchange(basis_copies(at, q_basis, received, NZ), "z").reshape(rank // NY, half)
+    basis = all_of_four(basis, "y")
     proj_mine, proj_other = project(at, mine, other, basis)
-    projected = sum_four(proj_mine + swap_cores(proj_other), "x")
-
-    gram_own = jnp.dot(projected.T, projected, preferred_element_type=f32, precision=HIGHEST)
-    part = rank // (NX * 2)
-
-    def gram_part(of_core):
-        return lax.dynamic_slice_in_dim(gram_own, (at_x * 2 + of_core) * part, part, 0)
-
-    gram_rows = sum_four(gram_part(core) + swap_cores(gram_part(1 - core)), "y")
-    gram_rows = jnp.sum(gather(gram_rows, "z", NZ), axis=0)
+    proj_chip = add(proj_mine, swap_cores(proj_other))
+    projected, gram_keep, gram_send = gram_rows_of(at, all_of_four(proj_chip, "x"))
+
+    gram_rows = add(gram_keep, swap_cores(gram_send))
+    gram_rows, proj_swapped = lax.optimization_barrier((gram_rows, swap_cores(projected)))
+    gram_rows = all_of_four(gram_rows, "y")
+    gram_rows = sum_copies(exchange(sum_four_copies(gram_rows, NZ), "z"), 1)[0]
     gram_chip = jnp.concatenate([gram_rows, swap_cores(gram_rows)])
-    inverse = inverse_factor(
-        at, [gram_chip] + [from_ahead(gram_chip, "x", by) for by in (1, 2, 3)]
-    )
-
-    crossed = cross(at, mine, other, projected, swap_cores(projected))
-    right = crossed[0] + sum(from_ahead(crossed[by], "y", NY - by) for by in (1, 2, 3))
-
-    def whiten(array):
-        return lax.dot_general(
-            array, inverse, BOTH_LAST, preferred_element_type=f32, precision=HIGHEST
-        )
-
-    solved = whiten(projected)
-    right = scatter_sum(whiten(right).astype(bf16), "z", NZ).astype(bf16)
-    right = gather(right, "z", NZ).reshape(half // NY, rank)
-    squares = jnp.sum(jnp.square(right.astype(f32)), axis=0, keepdims=True)
-    squares = gather(squares, ("y", "c", "x"), NY * 2 * NX).reshape(NY * 2 * NX, rank)
-    pieces, squares = ring_of_four(right, "y", squares)
-    pieces = pieces + tuple(swap_cores(piece) for piece in pieces)
+    inverse = inverse_factor(at, all_of_four(gram_chip, "x"))
+
+    crossed = cross(at, mine, other, projected, proj_swapped)
+    right = [crossed[0]] + [from_ahead(crossed[by], "y", NY - by) for by in (1, 2, 3)]
+    right = whiten(inverse, right, bf16).reshape(NZ, half // (NY * NZ), rank)
+    right = exchange(sum_copies(exchange(right, "z"), NZ), "z").reshape(half // NY, rank)
+    solved = whiten(inverse, [projected], f32)
+
+    parts = NY * 2 * NX
+    squares = square_copies(right, parts).reshape(parts, 8, rank)
+    squares = exchange(squares, ("y", "c", "x")).reshape(parts * 8, rank)
+    pieces, (squares, swapped) = ring_of_four(right, "y", (squares, swap_cores(right)))
+    pieces = pieces + (swapped,) + tuple(swap_cores(piece) for piece in pieces[1:])
 
     total_rows = rows * NZ * NY * 2
     total_cols = cols * NX

time: 204 us -> 201 us (0.985)
  waiting for transfers between devices: 39.1 us -> 44 us
  local copies, waits for them, and re-layouts: 9.19 us -> 5.66 us
  matrix products: 3.28 us -> 0 us
    ppermute x20 -> x19, waiting for transfers between devices: 34.1 us -> 38.9 us  [from_ahead(): lax.ppermute(block, axis, [((i + by) % parts, i) for i in range(parts)])]
    unnamed x19 -> x8, local copies, waits for them, and re-layouts: 5.33 us -> 1.44 us
    ppermute x20 -> x19, starting transfers between devices: 31.7 us -> 28.1 us  [from_ahead(): lax.ppermute(block, axis, [((i + by) % parts, i) for i in range(parts)])]
    dot_general x3 -> x0, matrix products: 3.28 us -> none  [the longest x2 2.69 us: whiten(): lax.dot_general(array, inverse, BOTH_LAST, preferred_element_type=f32, pr...]
    pallas_call x0 -> x10, Pallas kernels: none -> 3.11 us  [the longest x9 2.12 us: small(): pl.pallas_call(kernel, out_shape=out, in_specs=specs, out_specs=VMEM, com...]
    ppermute x11, starting transfers between devices: 14 us -> 16.2 us  [swap_cores(): return lax.ppermute(block, 'c', [(0, 1), (1, 0)])]
  transfers between devices with their start and end apart: 31 -> 30, of which waited for: 15 -> 16; matrix products, arithmetic and copies ran while one was open for 0% -> 0% of each run, Pallas kernels for 8% -> 7%
where the time goes in v2:
time: 201 us
  blocking collectives  79 us (39%)
  starting transfers between devices  44.2 us (22%)
  waiting for transfers between devices  44 us (22%)
  Pallas kernels  27 us (13%)
  local copies, waits for them, and re-layouts  5.66 us (3%)
    all_to_all x5, blocking collectives, exchange(): return lax.all_to_all(pieces, axes, 0, 0)  79 us
    ppermute x19, waiting for transfers between devices, from_ahead(): lax.ppermute(block, axis, [((i + by) % parts, i) for i in range(parts)])  38.9 us
    ppermute x19, starting transfers between devices, from_ahead(): lax.ppermute(block, axis, [((i + by) % parts, i) for i in range(parts)])  28.1 us
    ppermute x11, starting transfers between devices, swap_cores(): return lax.ppermute(block, 'c', [(0, 1), (1, 0)])  16.2 us
    pallas_call x1, Pallas kernels, inverse_factor(): pl.pallas_call(inverse_factor_kernel, out_shape=jax.ShapeDtypeStruct((ran...  9.93 us
    pallas_call x1, Pallas kernels, finish(): pl.pallas_call(lambda *refs: finish_kernel(scaling, *refs), out_shape=[ou...  7.93 us
    ppermute x11, waiting for transfers between devices, swap_cores(): return lax.ppermute(block, 'c', [(0, 1), (1, 0)])  5.07 us
    dynamic_slice x2, local copies, waits for them, and re-layouts, columns(): return lax.dynamic_slice_in_dim(array, of_core * half, half, 1)  4.19 us
  transfers between devices with their start and end apart: 30, of which 16 were waited for; matrix products, arithmetic and copies ran while one was open for 0% of the time, Pallas kernels for 7%

profile of v2, /device:TPU:1, one launch (start us, length us, event | category | flops | bytes accessed | tf_op | source)
XLA Modules:
  0.0 200.9 jit_solution(12060456398435408034)
XLA Ops:
  0.6 0.8 constant_dynamic-slice_fusion.2
  1.5 3.2 %collective-permute-start = (f32[4,3328]{1,0:T(4,128)S(1)}, f32[4,3328]{1,0:T(4,128)S(1)}, u32[]{:S(2)}, u32[]{:S(2)}) collective-permute-start(f32[4,3328]{1,0:T(4,128)S(1)} %constant_dynamic-slice_fusion.2), channel_id=1, source_target_pairs={{0,4},{4,0},{1,5},{5,1},{2,6},{6,2},{3,7},{7,3},{8,12},{12,8},{9,1... | collective-permute-start | bytes 159752 | tf_op jit(solution)/shard_map/ppermute | solution.py:398
  4.7 0.9 collective-permute-done.received_ref
  6.2 3.4 %constant_dynamic-slice_fusion = (bf16[256,3328]{1,0:T(8,128)(2,1)}, bf16[256,3328]{1,0:T(8,128)(2,1)S(1)}) fusion(bf16[256,6656]{1,0:T(8,128)(2,1)} %refs_1_.1, s32[]{:T(128)S(6)} %select_n.7, s32[]{:T(128)S(6)} %select_n.8), kind=kLoop, calls=%fused_computation.1 | loop fusion | bytes 6815752 | tf_op jit(solution)/shard_map/dynamic_slice | solution.py:432
  10.0 0.8 copy-done.3
  11.4 22.0 %all_to_all.25 = bf16[8,8,3328]{2,1,0:T(8,128)(2,1)S(1)} all-to-all(bf16[8,8,3328]{2,1,0:T(8,128)(2,1)S(1)} %shard_map.49), channel_id=1, replica_groups=mesh['z'=8,'y'=4,'c'=2,'x'=4] {'z'}, dimensions={0} | all-to-all | bytes 851968 | tf_op jit(solution)/shard_map/all_to_all | solution.py:418
  33.4 1.3 collective-permute-start.4
  34.7 2.6 %collective-permute-start.3 = (bf16[64,3328]{1,0:T(8,128)(2,1)S(1)}, bf16[64,3328]{1,0:T(8,128)(2,1)S(1)}, u32[]{:S(2)}, u32[]{:S(2)}) collective-permute-start(bf16[64,3328]{1,0:T(8,128)(2,1)S(1)} %bitcast.16), channel_id=1, source_target_pairs={{16,0},{24,8},{0,16},{8,24},{17,1},{25,9},{1,17},{9,25},{18,2},{26... | collective-permute-start | bytes 1277960 | tf_op jit(solution)/shard_map/ppermute | solution.py:402
  37.3 1.1 collective-permute-start.2
  38.4 7.2 %collective-permute-done.4.refs_3_ = bf16[64,3328]{1,0:T(8,128)(2,1)S(1)} collective-permute-done((bf16[64,3328]{1,0:T(8,128)(2,1)S(1)}, bf16[64,3328]{1,0:T(8,128)(2,1)S(1)}, u32[]{:S(2)}, u32[]{:S(2)}) %collective-permute-start.4) | collective-permute-done | bytes 426016 | tf_op jit(solution)/shard_map/ppermute | solution.py:402
  45.6 10.2 %collective-permute-done.3.refs_2_ = bf16[64,3328]{1,0:T(8,128)(2,1)S(1)} collective-permute-done((bf16[64,3328]{1,0:T(8,128)(2,1)S(1)}, bf16[64,3328]{1,0:T(8,128)(2,1)S(1)}, u32[]{:S(2)}, u32[]{:S(2)}) %collective-permute-start.3) | collective-permute-done | bytes 426016 | tf_op jit(solution)/shard_map/ppermute | solution.py:402
  55.8 2.0 %shard_map.50 = (f32[256,256]{1,0:T(8,128)S(1)}, f32[256,256]{1,0:T(8,128)S(1)}) custom-call(s32[4]{0:T(128)S(1)} %pad_add_fusion.at_ref.refs_0_, bf16[256,3328]{1,0:T(8,128)(2,1)S(1)} %get-tuple-element.38.mine_ref, bf16[256,3328]{1,0:T(8,128)(2,1)S(1)} %collective-permute-done.1.other_ref, bf16[64,3328]{1,0:T(8,128)(2,1)S(1)} %bitcast.18, ...), custom_call_target="tpu_custom_call" | custom-call | flops 872415232 | bytes 5111808 | tf_op jit(solution)/shard_map/pallas_call | solution.py:163
  57.9 1.5 collective-permute-start.5
  59.4 1.2 collective-permute-done.5.two_ref
  60.6 1.3 collective-permute-start.8
  61.8 2.5 %collective-permute-start.7 = (f32[256,256]{1,0:T(8,128)S(1)}, f32[256,256]{1,0:T(8,128)S(1)}, u32[]{:S(2)}, u32[]{:S(2)}) collective-permute-start(f32[256,256]{1,0:T(8,128)S(1)} %shard_map.51.own_ref), channel_id=1, source_target_pairs={{2,0},{3,1},{0,2},{1,3},{6,4},{7,5},{4,6},{5,7},{10,8},{11,9},{8,1... | collective-permute-start | bytes 786440 | tf_op jit(solution)/shard_map/ppermute | solution.py:402
  64.3 1.1 collective-permute-start.6
  65.5 3.9 %collective-permute-done.8.three_ref = f32[256,256]{1,0:T(8,128)S(1)} collective-permute-done((f32[256,256]{1,0:T(8,128)S(1)}, f32[256,256]{1,0:T(8,128)S(1)}, u32[]{:S(2)}, u32[]{:S(2)}) %collective-permute-start.8) | collective-permute-done | bytes 262176 | tf_op jit(solution)/shard_map/ppermute | solution.py:402
  69.4 6.6 %collective-permute-done.7.two_ref = f32[256,256]{1,0:T(8,128)S(1)} collective-permute-done((f32[256,256]{1,0:T(8,128)S(1)}, f32[256,256]{1,0:T(8,128)S(1)}, u32[]{:S(2)}, u32[]{:S(2)}) %collective-permute-start.7) | collective-permute-done | bytes 262176 | tf_op jit(solution)/shard_map/ppermute | solution.py:402
  76.0 1.0 shard_map.52
  77.0 1.3 collective-permute-start.10
  78.4 1.1 collective-permute-done.9.two_ref
  79.5 0.9 collective-permute-start.13
  80.4 2.1 %collective-permute-start.12 = (f32[32,256]{1,0:T(8,128)S(1)}, f32[32,256]{1,0:T(8,128)S(1)}, u32[]{:S(2)}, u32[]{:S(2)}) collective-permute-start(f32[32,256]{1,0:T(8,128)S(1)} %shard_map.53.own_ref), channel_id=1, source_target_pairs={{16,0},{24,8},{0,16},{8,24},{17,1},{25,9},{1,17},{9,25},{18,2},{26... | collective-permute-start | bytes 98312 | tf_op jit(solution)/shard_map/ppermute | solution.py:402
  82.5 1.4 collective-permute-start.11
  83.9 4.0 %shard_map.58 = (f32[832,256]{1,0:T(8,128)S(1)}, f32[832,256]{1,0:T(8,128)S(1)}, f32[832,256]{1,0:T(8,128)S(1)}, f32[832,256]{1,0:T(8,128)S(1)}) custom-call(s32[4]{0:T(128)S(1)} %pad_add_fusion.at_ref.refs_0_, bf16[256,3328]{1,0:T(8,128)(2,1)S(1)} %get-tuple-element.38.mine_ref, bf16[256,3328]{1,0:T(8,128)(2,1)S(1)} %collective-permute-done.1.other_ref, ...), custom_call_target="tpu_custom_call" | custom-call | flops 2617245696 | bytes 10223616 | tf_op jit(solution)/shard_map/pallas_call | solution.py:309
  88.0 1.1 collective-permute-start.19
  89.2 1.6 collective-permute-start.20
  90.8 11.6 %all_to_all.26.pieces_ref = f32[8,32,256]{2,1,0:T(8,128)S(1)} all-to-all(f32[8,32,256]{2,1,0:T(8,128)S(1)} %shard_map.54), channel_id=1, replica_groups=mesh['z'=8,'y'=4,'c'=2,'x'=4] {'z'}, dimensions={0} | all-to-all | bytes 524288 | tf_op jit(solution)/shard_map/all_to_all | solution.py:418
  102.4 3.7 %collective-permute-start.14 = (f32[32,256]{1,0:T(8,128)S(1)}, f32[32,256]{1,0:T(8,128)S(1)}, u32[]{:S(2)}, u32[]{:S(2)}) collective-permute-start(f32[32,256]{1,0:T(8,128)S(1)} %bitcast.22), channel_id=1, source_target_pairs={{0,4},{4,0},{1,5},{5,1},{2,6},{6,2},{3,7},{7,3},{8,12},{12,8},{9,1... | collective-permute-start | bytes 98312 | tf_op jit(solution)/shard_map/ppermute | solution.py:398
  106.1 0.9 collective-permute-done.14
  107.0 1.1 collective-permute-start.17
  108.0 2.1 %collective-permute-start.16 = (f32[64,256]{1,0:T(8,128)S(1)}, f32[64,256]{1,0:T(8,128)S(1)}, u32[]{:S(2)}, u32[]{:S(2)}) collective-permute-start(f32[64,256]{1,0:T(8,128)S(1)} %pad_maximum_fusion.own_ref), channel_id=1, source_target_pairs={{2,0},{3,1},{0,2},{1,3},{6,4},{7,5},{4,6},{5,7},{10,8},{11,9},{8,1... | collective-permute-start | bytes 196616 | tf_op jit(solution)/shard_map/ppermute | solution.py:402
  110.1 1.5 collective-permute-done.17.last_ref
  112.4 1.3 collective-permute-done.16.across_ref
  113.7 1.3 collective-permute-done.15.next_ref
  115.0 9.9 %shard_map.56.inverse_ref = f32[256,256]{1,0:T(8,128)S(1)} custom-call(s32[4]{0:T(128)S(1)} %pad_add_fusion.at_ref.refs_0_, f32[64,256]{1,0:T(8,128)S(1)} %pad_maximum_fusion.own_ref, f32[64,256]{1,0:T(8,128)S(1)} %collective-permute-done.15.next_ref, f32[64,256]{1,0:T(8,128)S(1)} %collective-permute-done.16.across_ref, ...), custom_call_target="tpu_custom_call" | custom-call | flops 1000000000 | bytes 1048576 | tf_op jit(solution)/shard_map/pallas_call | solution.py:127
  125.5 1.9 collective-permute-done.20.refs_3_
  127.4 0.9 shard_map.59
  128.4 15.1 %all_to_all.27.pieces_ref = bf16[8,104,256]{2,1,0:T(8,128)(2,1)S(1)} all-to-all(bf16[8,104,256]{2,1,0:T(8,128)(2,1)S(1)} %bitcast.19), channel_id=1, replica_groups=mesh['z'=8,'y'=4,'c'=2,'x'=4] {'z'}, dimensions={0} | all-to-all | bytes 851968 | tf_op jit(solution)/shard_map/all_to_all | solution.py:418
  143.5 15.8 %all_to_all.28 = bf16[8,104,256]{2,1,0:T(8,128)(2,1)S(1)} all-to-all(bf16[8,104,256]{2,1,0:T(8,128)(2,1)S(1)} %shard_map.60), channel_id=1, replica_groups=mesh['z'=8,'y'=4,'c'=2,'x'=4] {'z'}, dimensions={0} | all-to-all | bytes 851968 | tf_op jit(solution)/shard_map/all_to_all | solution.py:418
  159.3 4.3 %collective-permute-start.23 = (bf16[832,256]{1,0:T(8,128)(2,1)S(1)}, bf16[832,256]{1,0:T(8,128)(2,1)S(1)}, u32[]{:S(2)}, u32[]{:S(2)}) collective-permute-start(bf16[832,256]{1,0:T(8,128)(2,1)S(1)} %bitcast.10), channel_id=1, source_target_pairs={{0,4},{4,0},{1,5},{5,1},{2,6},{6,2},{3,7},{7,3},{8,12},{12,8},{9,1... | collective-permute-start | bytes 1277960 | tf_op jit(solution)/shard_map/ppermute | solution.py:398
  163.6 3.5 %collective-permute-start.22 = (bf16[832,256]{1,0:T(8,128)(2,1)S(1)}, bf16[832,256]{1,0:T(8,128)(2,1)S(1)}, u32[]{:S(2)}, u32[]{:S(2)}) collective-permute-start(bf16[832,256]{1,0:T(8,128)(2,1)S(1)} %bitcast.11), channel_id=1, source_target_pairs={{24,0},{0,8},{8,16},{16,24},{25,1},{1,9},{9,17},{17,25},{26,2},{2,... | collective-permute-start | bytes 1277960 | tf_op jit(solution)/shard_map/ppermute | solution.py:402
  167.8 14.5 %all_to_all.29 = f32[32,8,256]{2,1,0:T(8,128)S(1)} all-to-all(f32[32,8,256]{2,1,0:T(8,128)S(1)} %bitcast.20), channel_id=1, replica_groups=mesh['z'=8,'y'=4,'c'=2,'x'=4] {'y','c','x'}, dimensions={0} | all-to-all | bytes 524288 | tf_op jit(solution)/shard_map/all_to_all | solution.py:418
  182.8 2.4 %collective-permute-start.25 = (bf16[416,256]{1,0:T(8,128)(2,1)S(1)}, bf16[416,256]{1,0:T(8,128)(2,1)S(1)}, u32[]{:S(2)}, u32[]{:S(2)}) collective-permute-start(bf16[416,256]{1,0:T(8,128)(2,1)S(1)} %slice.7), channel_id=1, source_target_pairs={{8,0},{16,8},{24,16},{0,24},{9,1},{17,9},{25,17},{1,25},{10,2},{18... | collective-permute-start | bytes 638984 | tf_op jit(solution)/shard_map/ppermute | solution.py:402
  186.0 4.4 %collective-permute-done.24.refs_7_ = bf16[416,256]{1,0:T(8,128)(2,1)S(1)} collective-permute-done((bf16[416,256]{1,0:T(8,128)(2,1)S(1)}, bf16[416,256]{1,0:T(8,128)(2,1)S(1)}, u32[]{:S(2)}, u32[]{:S(2)}) %collective-permute-start.24) | collective-permute-done | bytes 213024 | tf_op jit(solution)/shard_map/ppermute | solution.py:402
  190.4 1.0 collective-permute-start.28
  192.8 7.9 %shard_map.62 = (bf16[256,6656]{1,0:T(8,128)(2,1)}, bf16[256,6656]{1,0:T(8,128)(2,1)}, f32[4,6656]{1,0:T(4,128)}) custom-call(s32[4]{0:T(128)S(1)} %pad_add_fusion.at_ref.refs_0_, bf16[256,6656]{1,0:T(8,128)(2,1)S(1)} %copy-done, f32[256,256]{1,0:T(8,128)S(1)} %shard_map.57.refs_2_, f32[256,256]{1,0:T(8,128)S(1)} %bitcast.21, bf16[832,256]{1,0:T(8,128)(2,1)S(1)} %bitcast.14, ...), custom_call_target="tpu_custom_call" | custom-call | flops 1744830464 | bytes 13631488 | tf_op jit(solution)/shard_map/pallas_call | solution.py:372
  (45 shorter events, 6.7 us)
Async XLA Ops:
  1.5 4.1 %collective-permute-start = (f32[4,3328]{1,0:T(4,128)S(1)}, f32[4,3328]{1,0:T(4,128)S(1)}, u32[]{:S(2)}, u32[]{:S(2)}) collective-permute-start(f32[4,3328]{1,0:T(4,128)S(1)} %constant_dynamic-slice_fusion.2), channel_id=1, source_target_pairs={{0,4},{4,0},{1,5},{5,1},{2,6},{6,2},{3,7},{7,3},{8,12},{12,8},{9,1... | collective-permute-start | bytes 159752 | tf_op jit(solution)/shard_map/ppermute | solution.py:398
  4.7 5.3 %copy-start.1 = (f32[4,6656]{1,0:T(4,128)S(1)}, f32[4,6656]{1,0:T(4,128)}, u32[]{:S(2)}) copy-start(f32[4,6656]{1,0:T(4,128)} %basis_ref.1) | copy-start | bytes 319492
  5.6 0.6 copy-start.2
  9.6 46.3 %collective-permute-start.1 = (bf16[256,3328]{1,0:T(8,128)(2,1)}, bf16[256,3328]{1,0:T(8,128)(2,1)S(1)}, u32[]{:S(2)}, u32[]{:S(2)}) collective-permute-start(bf16[256,3328]{1,0:T(8,128)(2,1)} %get-tuple-element.37), channel_id=1, source_target_pairs={{0,4},{4,0},{1,5},{5,1},{2,6},{6,2},{3,7},{7,3},{8,12},{12,8},{9,1... | collective-permute-start | bytes 5111816 | tf_op jit(solution)/shard_map/ppermute | solution.py:398
  10.0 0.8 copy-start.3
  33.4 12.1 %collective-permute-start.4 = (bf16[64,3328]{1,0:T(8,128)(2,1)S(1)}, bf16[64,3328]{1,0:T(8,128)(2,1)S(1)}, u32[]{:S(2)}, u32[]{:S(2)}) collective-permute-start(bf16[64,3328]{1,0:T(8,128)(2,1)S(1)} %bitcast.15), channel_id=1, source_target_pairs={{24,0},{0,8},{8,16},{16,24},{25,1},{1,9},{9,17},{17,25},{26,2},{2,... | collective-permute-start | bytes 1277960 | tf_op jit(solution)/shard_map/ppermute | solution.py:402
  34.7 21.1 %collective-permute-start.3 = (bf16[64,3328]{1,0:T(8,128)(2,1)S(1)}, bf16[64,3328]{1,0:T(8,128)(2,1)S(1)}, u32[]{:S(2)}, u32[]{:S(2)}) collective-permute-start(bf16[64,3328]{1,0:T(8,128)(2,1)S(1)} %bitcast.16), channel_id=1, source_target_pairs={{16,0},{24,8},{0,16},{8,24},{17,1},{25,9},{1,17},{9,25},{18,2},{26... | collective-permute-start | bytes 1277960 | tf_op jit(solution)/shard_map/ppermute | solution.py:402
  37.3 18.5 %collective-permute-start.2 = (bf16[64,3328]{1,0:T(8,128)(2,1)S(1)}, bf16[64,3328]{1,0:T(8,128)(2,1)S(1)}, u32[]{:S(2)}, u32[]{:S(2)}) collective-permute-start(bf16[64,3328]{1,0:T(8,128)(2,1)S(1)} %bitcast.17), channel_id=1, source_target_pairs={{8,0},{16,8},{24,16},{0,24},{9,1},{17,9},{25,17},{1,25},{10,2},{18... | collective-permute-start | bytes 1277960 | tf_op jit(solution)/shard_map/ppermute | solution.py:402
  57.9 2.7 %collective-permute-start.5 = (f32[256,256]{1,0:T(8,128)S(1)}, f32[256,256]{1,0:T(8,128)S(1)}, u32[]{:S(2)}, u32[]{:S(2)}) collective-permute-start(f32[256,256]{1,0:T(8,128)S(1)} %get-tuple-element.23), channel_id=1, source_target_pairs={{0,4},{4,0},{1,5},{5,1},{2,6},{6,2},{3,7},{7,3},{8,12},{12,8},{9,1... | collective-permute-start | bytes 786440 | tf_op jit(solution)/shard_map/ppermute | solution.py:398
  60.6 8.8 %collective-permute-start.8 = (f32[256,256]{1,0:T(8,128)S(1)}, f32[256,256]{1,0:T(8,128)S(1)}, u32[]{:S(2)}, u32[]{:S(2)}) collective-permute-start(f32[256,256]{1,0:T(8,128)S(1)} %shard_map.51.own_ref), channel_id=1, source_target_pairs={{3,0},{0,1},{1,2},{2,3},{7,4},{4,5},{5,6},{6,7},{11,8},{8,9},{9,10... | collective-permute-start | bytes 786440 | tf_op jit(solution)/shard_map/ppermute | solution.py:402
  61.8 14.1 %collective-permute-start.7 = (f32[256,256]{1,0:T(8,128)S(1)}, f32[256,256]{1,0:T(8,128)S(1)}, u32[]{:S(2)}, u32[]{:S(2)}) collective-permute-start(f32[256,256]{1,0:T(8,128)S(1)} %shard_map.51.own_ref), channel_id=1, source_target_pairs={{2,0},{3,1},{0,2},{1,3},{6,4},{7,5},{4,6},{5,7},{10,8},{11,9},{8,1... | collective-permute-start | bytes 786440 | tf_op jit(solution)/shard_map/ppermute | solution.py:402
  64.3 11.7 %collective-permute-start.6 = (f32[256,256]{1,0:T(8,128)S(1)}, f32[256,256]{1,0:T(8,128)S(1)}, u32[]{:S(2)}, u32[]{:S(2)}) collective-permute-start(f32[256,256]{1,0:T(8,128)S(1)} %shard_map.51.own_ref), channel_id=1, source_target_pairs={{1,0},{2,1},{3,2},{0,3},{5,4},{6,5},{7,6},{4,7},{9,8},{10,9},{11,1... | collective-permute-start | bytes 786440 | tf_op jit(solution)/shard_map/ppermute | solution.py:402
  77.0 2.5 %collective-permute-start.10 = (f32[256,256]{1,0:T(8,128)S(1)}, f32[256,256]{1,0:T(8,128)S(1)}, u32[]{:S(2)}, u32[]{:S(2)}) collective-permute-start(f32[256,256]{1,0:T(8,128)S(1)} %get-tuple-element.26.refs_0_.left_mine_ref), channel_id=1, source_target_pairs={{0,4},{4,0},{1,5},{5,1},{2,6},{6,2},{3,7},{7,3},{8,12},{12,8},{9,1... | collective-permute-start | bytes 786440 | tf_op jit(solution)/shard_map/ppermute | solution.py:398
  78.2 1.2 collective-permute-start.9
  79.5 9.7 %collective-permute-start.13 = (f32[32,256]{1,0:T(8,128)S(1)}, f32[32,256]{1,0:T(8,128)S(1)}, u32[]{:S(2)}, u32[]{:S(2)}) collective-permute-start(f32[32,256]{1,0:T(8,128)S(1)} %shard_map.53.own_ref), channel_id=1, source_target_pairs={{24,0},{0,8},{8,16},{16,24},{25,1},{1,9},{9,17},{17,25},{26,2},{2,... | collective-permute-start | bytes 98312 | tf_op jit(solution)/shard_map/ppermute | solution.py:402
  80.4 10.3 %collective-permute-start.12 = (f32[32,256]{1,0:T(8,128)S(1)}, f32[32,256]{1,0:T(8,128)S(1)}, u32[]{:S(2)}, u32[]{:S(2)}) collective-permute-start(f32[32,256]{1,0:T(8,128)S(1)} %shard_map.53.own_ref), channel_id=1, source_target_pairs={{16,0},{24,8},{0,16},{8,24},{17,1},{25,9},{1,17},{9,25},{18,2},{26... | collective-permute-start | bytes 98312 | tf_op jit(solution)/shard_map/ppermute | solution.py:402
  82.5 8.2 %collective-permute-start.11 = (f32[32,256]{1,0:T(8,128)S(1)}, f32[32,256]{1,0:T(8,128)S(1)}, u32[]{:S(2)}, u32[]{:S(2)}) collective-permute-start(f32[32,256]{1,0:T(8,128)S(1)} %shard_map.53.own_ref), channel_id=1, source_target_pairs={{8,0},{16,8},{24,16},{0,24},{9,1},{17,9},{25,17},{1,25},{10,2},{18... | collective-permute-start | bytes 98312 | tf_op jit(solution)/shard_map/ppermute | solution.py:402
  87.9 37.1 %collective-permute-start.18 = (f32[832,256]{1,0:T(8,128)S(1)}, f32[832,256]{1,0:T(8,128)S(1)}, u32[]{:S(2)}, u32[]{:S(2)}) collective-permute-start(f32[832,256]{1,0:T(8,128)S(1)} %get-tuple-element.30), channel_id=1, source_target_pairs={{24,0},{0,8},{8,16},{16,24},{25,1},{1,9},{9,17},{17,25},{26,2},{2,... | collective-permute-start | bytes 2555912 | tf_op jit(solution)/shard_map/ppermute | solution.py:402
  88.0 37.4 %collective-permute-start.19 = (f32[832,256]{1,0:T(8,128)S(1)}, f32[832,256]{1,0:T(8,128)S(1)}, u32[]{:S(2)}, u32[]{:S(2)}) collective-permute-start(f32[832,256]{1,0:T(8,128)S(1)} %get-tuple-element.31), channel_id=1, source_target_pairs={{16,0},{24,8},{0,16},{8,24},{17,1},{25,9},{1,17},{9,25},{18,2},{26... | collective-permute-start | bytes 2555912 | tf_op jit(solution)/shard_map/ppermute | solution.py:402
  89.2 38.3 %collective-permute-start.20 = (f32[832,256]{1,0:T(8,128)S(1)}, f32[832,256]{1,0:T(8,128)S(1)}, u32[]{:S(2)}, u32[]{:S(2)}) collective-permute-start(f32[832,256]{1,0:T(8,128)S(1)} %get-tuple-element.32), channel_id=1, source_target_pairs={{8,0},{16,8},{24,16},{0,24},{9,1},{17,9},{25,17},{1,25},{10,2},{18... | collective-permute-start | bytes 2555912 | tf_op jit(solution)/shard_map/ppermute | solution.py:402
  102.4 4.6 %collective-permute-start.14 = (f32[32,256]{1,0:T(8,128)S(1)}, f32[32,256]{1,0:T(8,128)S(1)}, u32[]{:S(2)}, u32[]{:S(2)}) collective-permute-start(f32[32,256]{1,0:T(8,128)S(1)} %bitcast.22), channel_id=1, source_target_pairs={{0,4},{4,0},{1,5},{5,1},{2,6},{6,2},{3,7},{7,3},{8,12},{12,8},{9,1... | collective-permute-start | bytes 98312 | tf_op jit(solution)/shard_map/ppermute | solution.py:398
  107.0 4.6 %collective-permute-start.17 = (f32[64,256]{1,0:T(8,128)S(1)}, f32[64,256]{1,0:T(8,128)S(1)}, u32[]{:S(2)}, u32[]{:S(2)}) collective-permute-start(f32[64,256]{1,0:T(8,128)S(1)} %pad_maximum_fusion.own_ref), channel_id=1, source_target_pairs={{3,0},{0,1},{1,2},{2,3},{7,4},{4,5},{5,6},{6,7},{11,8},{8,9},{9,10... | collective-permute-start | bytes 196616 | tf_op jit(solution)/shard_map/ppermute | solution.py:402
  108.0 5.6 %collective-permute-start.16 = (f32[64,256]{1,0:T(8,128)S(1)}, f32[64,256]{1,0:T(8,128)S(1)}, u32[]{:S(2)}, u32[]{:S(2)}) collective-permute-start(f32[64,256]{1,0:T(8,128)S(1)} %pad_maximum_fusion.own_ref), channel_id=1, source_target_pairs={{2,0},{3,1},{0,2},{1,3},{6,4},{7,5},{4,6},{5,7},{10,8},{11,9},{8,1... | collective-permute-start | bytes 196616 | tf_op jit(solution)/shard_map/ppermute | solution.py:402
  111.6 3.4 %collective-permute-start.15 = (f32[64,256]{1,0:T(8,128)S(1)}, f32[64,256]{1,0:T(8,128)S(1)}, u32[]{:S(2)}, u32[]{:S(2)}) collective-permute-start(f32[64,256]{1,0:T(8,128)S(1)} %pad_maximum_fusion.own_ref), channel_id=1, source_target_pairs={{1,0},{2,1},{3,2},{0,3},{5,4},{6,5},{7,6},{4,7},{9,8},{10,9},{11,1... | collective-permute-start | bytes 196616 | tf_op jit(solution)/shard_map/ppermute | solution.py:402
  143.5 49.3 %copy-start = (bf16[256,6656]{1,0:T(8,128)(2,1)S(1)}, bf16[256,6656]{1,0:T(8,128)(2,1)}, u32[]{:S(2)}) copy-start(bf16[256,6656]{1,0:T(8,128)(2,1)} %refs_1_.1) | copy-start | bytes 10223620
  159.3 23.1 %collective-permute-start.23 = (bf16[832,256]{1,0:T(8,128)(2,1)S(1)}, bf16[832,256]{1,0:T(8,128)(2,1)S(1)}, u32[]{:S(2)}, u32[]{:S(2)}) collective-permute-start(bf16[832,256]{1,0:T(8,128)(2,1)S(1)} %bitcast.10), channel_id=1, source_target_pairs={{0,4},{4,0},{1,5},{5,1},{2,6},{6,2},{3,7},{7,3},{8,12},{12,8},{9,1... | collective-permute-start | bytes 1277960 | tf_op jit(solution)/shard_map/ppermute | solution.py:398
  163.6 18.8 %collective-permute-start.22 = (bf16[832,256]{1,0:T(8,128)(2,1)S(1)}, bf16[832,256]{1,0:T(8,128)(2,1)S(1)}, u32[]{:S(2)}, u32[]{:S(2)}) collective-permute-start(bf16[832,256]{1,0:T(8,128)(2,1)S(1)} %bitcast.11), channel_id=1, source_target_pairs={{24,0},{0,8},{8,16},{16,24},{25,1},{1,9},{9,17},{17,25},{26,2},{2,... | collective-permute-start | bytes 1277960 | tf_op jit(solution)/shard_map/ppermute | solution.py:402
  167.1 15.3 %collective-permute-start.21 = (bf16[832,256]{1,0:T(8,128)(2,1)S(1)}, bf16[832,256]{1,0:T(8,128)(2,1)S(1)}, u32[]{:S(2)}, u32[]{:S(2)}) collective-permute-start(bf16[832,256]{1,0:T(8,128)(2,1)S(1)} %bitcast.12), channel_id=1, source_target_pairs={{8,0},{16,8},{24,16},{0,24},{9,1},{17,9},{25,17},{1,25},{10,2},{18... | collective-permute-start | bytes 1277960 | tf_op jit(solution)/shard_map/ppermute | solution.py:402
  182.4 8.0 %collective-permute-start.24 = (bf16[416,256]{1,0:T(8,128)(2,1)S(1)}, bf16[416,256]{1,0:T(8,128)(2,1)S(1)}, u32[]{:S(2)}, u32[]{:S(2)}) collective-permute-start(bf16[416,256]{1,0:T(8,128)(2,1)S(1)} %slice.6), channel_id=1, source_target_pairs={{24,0},{0,8},{8,16},{16,24},{25,1},{1,9},{9,17},{17,25},{26,2},{2,... | collective-permute-start | bytes 638984 | tf_op jit(solution)/shard_map/ppermute | solution.py:402
  182.8 8.5 %collective-permute-start.25 = (bf16[416,256]{1,0:T(8,128)(2,1)S(1)}, bf16[416,256]{1,0:T(8,128)(2,1)S(1)}, u32[]{:S(2)}, u32[]{:S(2)}) collective-permute-start(bf16[416,256]{1,0:T(8,128)(2,1)S(1)} %slice.7), channel_id=1, source_target_pairs={{8,0},{16,8},{24,16},{0,24},{9,1},{17,9},{25,17},{1,25},{10,2},{18... | collective-permute-start | bytes 638984 | tf_op jit(solution)/shard_map/ppermute | solution.py:402
  185.2 7.6 %collective-permute-start.26 = (bf16[832,256]{1,0:T(8,128)(2,1)S(1)}, bf16[832,256]{1,0:T(8,128)(2,1)S(1)}, u32[]{:S(2)}, u32[]{:S(2)}) collective-permute-start(bf16[832,256]{1,0:T(8,128)(2,1)S(1)} %collective-permute-done.21.refs_5_), channel_id=1, source_target_pairs={{0,4},{4,0},{1,5},{5,1},{2,6},{6,2},{3,7},{7,3},{8,12},{12,8},{9,1... | collective-permute-start | bytes 1277960 | tf_op jit(solution)/shard_map/ppermute | solution.py:398
  186.0 6.9 %collective-permute-start.27 = (bf16[832,256]{1,0:T(8,128)(2,1)S(1)}, bf16[832,256]{1,0:T(8,128)(2,1)S(1)}, u32[]{:S(2)}, u32[]{:S(2)}) collective-permute-start(bf16[832,256]{1,0:T(8,128)(2,1)S(1)} %collective-permute-done.22.refs_6_), channel_id=1, source_target_pairs={{0,4},{4,0},{1,5},{5,1},{2,6},{6,2},{3,7},{7,3},{8,12},{12,8},{9,1... | collective-permute-start | bytes 1277960 | tf_op jit(solution)/shard_map/ppermute | solution.py:398
  190.4 2.1 %collective-permute-start.28 = (bf16[416,256]{1,0:T(8,128)(2,1)S(1)}, bf16[416,256]{1,0:T(8,128)(2,1)S(1)}, u32[]{:S(2)}, u32[]{:S(2)}) collective-permute-start(bf16[416,256]{1,0:T(8,128)(2,1)S(1)} %collective-permute-done.24.refs_7_), channel_id=1, source_target_pairs={{0,4},{4,0},{1,5},{5,1},{2,6},{6,2},{3,7},{7,3},{8,12},{12,8},{9,1... | collective-permute-start | bytes 638984 | tf_op jit(solution)/shard_map/ppermute | solution.py:398
  191.4 1.5 collective-permute-start.29

commit v3 on v2

--- a/solution.py
+++ b/solution.py
@@ -211,6 +211,32 @@
     return small(kernel, jax.ShapeDtypeStruct(shape, pieces.dtype), pieces)
 
 
+def cut(at, momentum):
+    rows, cols = momentum.shape
+    half = cols // 2
+
+    def kernel(at_ref, momentum_ref, mine_ref, theirs_ref, semaphores):
+        copies = []
+        for n, ref in enumerate((mine_ref, theirs_ref)):
+            start = pl.multiple_of((at_ref[AT_CORE] + n) % 2 * half, 128)
+            source = momentum_ref.at[:, pl.ds(start, half)]
+            copies.append(pltpu.make_async_copy(source, ref, semaphores.at[n]))
+        for copy in copies:
+            copy.start()
+        for copy in copies:
+            copy.wait()
+
+    return pl.pallas_call(
+        kernel,
+        out_shape=[jax.ShapeDtypeStruct((rows, half), bf16)] * 2,
+        in_specs=[SMEM, ANY],
+        out_specs=[VMEM, VMEM],
+        scratch_shapes=[pltpu.SemaphoreType.DMA((2,))],
+        compiler_params=pltpu.CompilerParams(vmem_limit_bytes=58 * MIB),
+        cost_estimate=pl.CostEstimate(flops=0, bytes_accessed=4 * rows * cols, transcendentals=0),
+    )(at, momentum)
+
+
 def basis_copies(at, basis, received, copies):
     shard_rank, half = received.shape
 
@@ -232,11 +258,11 @@
 
     def kernel(right_ref, out_ref):
         right = right_ref[...].astype(f32)
-        out_ref[...] = jnp.broadcast_to(
-            jnp.sum(right * right, axis=0, keepdims=True), out_ref.shape
-        )
-
-    return small(kernel, jax.ShapeDtypeStruct((copies * 8, rank), f32), right)
+        total = jnp.sum(right * right, axis=0, keepdims=True)
+        for n in range(copies):
+            out_ref[n] = total
+
+    return small(kernel, jax.ShapeDtypeStruct((copies, 1, rank), f32), right)
 
 
 def whiten(inverse, pieces, out):
@@ -341,7 +367,7 @@
             copy.start()
             copies.append(copy)
         solved = solved_ref[...]
-        squares = jnp.sum(squares_ref[...], axis=0, keepdims=True) / 8
+        squares = jnp.sum(squares_ref[...], axis=0)
         inverse_lengths = lax.rsqrt(squares + 1e-06)
         left_ref[:rows, :] = solved.astype(bf16)
         left_ref[rows : 2 * rows, :] = (solved * (scaling * inverse_lengths)).astype(bf16)
@@ -377,7 +403,7 @@
             SMEM,
             columns,
             pl.BlockSpec(solved.shape, lambda i: (0, 0)),
-            pl.BlockSpec(squares.shape, lambda i: (0, 0)),
+            pl.BlockSpec(squares.shape, lambda i: (0, 0, 0)),
         ]
         + [ANY] * 10,
         out_specs=[columns, columns, pl.BlockSpec((shard_rank, width), lambda i: (0, i))],
@@ -432,9 +458,9 @@
         return lax.dynamic_slice_in_dim(array, of_core * half, half, 1)
 
     received = swap_cores(columns(q_basis, 1 - core))
-    later, received = lax.optimization_barrier((momentum, received))
-    mine = columns(later, core)
-    other = swap_cores(columns(later, 1 - core))
+    later, received = lax.optimization_barrier((at, received))
+    mine, theirs = cut(later, momentum)
+    other = swap_cores(theirs)
 
     basis = exchange(basis_copies(at, q_basis, received, NZ), "z").reshape(rank // NY, half)
     basis = all_of_four(basis, "y")
@@ -456,8 +482,7 @@
     solved = whiten(inverse, [projected], f32)
 
     parts = NY * 2 * NX
-    squares = square_copies(right, parts).reshape(parts, 8, rank)
-    squares = exchange(squares, ("y", "c", "x")).reshape(parts * 8, rank)
+    squares = exchange(square_copies(right, parts), ("y", "c", "x"))
     pieces, (squares, swapped) = ring_of_four(right, "y", (squares, swap_cores(right)))
     pieces = pieces + (swapped,) + tuple(swap_cores(piece) for piece in pieces[1:])
 

time: 201 us -> 201 us (level)
  Pallas kernels: 27 us -> 31.4 us
  local copies, waits for them, and re-layouts: 5.66 us -> 2.37 us
    pallas_call x0 -> x1, Pallas kernels: none -> 4.4 us  [cut(): pl.pallas_call(kernel, out_shape=[jax.ShapeDtypeStruct((rows, half), bf16...]
    dynamic_slice x2 -> x1, local copies, waits for them, and re-layouts: 4.19 us -> 0.87 us  [columns(): return lax.dynamic_slice_in_dim(array, of_core * half, half, 1)]
where the time goes in v3:
time: 201 us; the launch traced here: 200 us
  blocking collectives  77.2 us (38%)
  starting transfers between devices  45 us (22%)
  waiting for transfers between devices  42.9 us (21%)
  Pallas kernels  31.4 us (16%)
  local copies, waits for them, and re-layouts  2.37 us (1%)
    all_to_all x5, blocking collectives, exchange(): return lax.all_to_all(pieces, axes, 0, 0)  77.2 us
    ppermute x19, waiting for transfers between devices, from_ahead(): lax.ppermute(block, axis, [((i + by) % parts, i) for i in range(parts)])  38.4 us
    ppermute x19, starting transfers between devices, from_ahead(): lax.ppermute(block, axis, [((i + by) % parts, i) for i in range(parts)])  28.2 us
    ppermute x11, starting transfers between devices, swap_cores(): return lax.ppermute(block, 'c', [(0, 1), (1, 0)])  16.8 us
    pallas_call x1, Pallas kernels, inverse_factor(): pl.pallas_call(inverse_factor_kernel, out_shape=jax.ShapeDtypeStruct((ran...  9.92 us
    pallas_call x1, Pallas kernels, finish(): pl.pallas_call(lambda *refs: finish_kernel(scaling, *refs), out_shape=[ou...  7.93 us
    ppermute x11, waiting for transfers between devices, swap_cores(): return lax.ppermute(block, 'c', [(0, 1), (1, 0)])  4.47 us
    pallas_call x1, Pallas kernels, cut(): pl.pallas_call(kernel, out_shape=[jax.ShapeDtypeStruct((rows, half), bf16...  4.4 us
  transfers between devices with their start and end apart: 30, of which 16 were waited for; matrix products, arithmetic and copies ran while one was open for 0% of the time, Pallas kernels for 7%

profile of v3, /device:TPU:1, one launch (start us, length us, event | category | flops | bytes accessed | tf_op | source)
XLA Modules:
  0.0 200.5 jit_solution(12392671914045227512)
XLA Ops:
  0.6 0.9 constant_dynamic-slice_fusion
  1.5 3.2 %collective-permute-start = (f32[4,3328]{1,0:T(4,128)S(1)}, f32[4,3328]{1,0:T(4,128)S(1)}, u32[]{:S(2)}, u32[]{:S(2)}) collective-permute-start(f32[4,3328]{1,0:T(4,128)S(1)} %constant_dynamic-slice_fusion), channel_id=1, source_target_pairs={{0,4},{4,0},{1,5},{5,1},{2,6},{6,2},{3,7},{7,3},{8,12},{12,8},{9,1... | collective-permute-start | bytes 159752 | tf_op jit(solution)/shard_map/ppermute | solution.py:424
  5.6 4.4 %shard_map.49 = (bf16[256,3328]{1,0:T(8,128)(2,1)}, bf16[256,3328]{1,0:T(8,128)(2,1)}) custom-call(s32[4]{0:T(128)} %pad_add_fusion.at_ref.refs_0_, bf16[256,6656]{1,0:T(8,128)(2,1)} %refs_1_.1), custom_call_target="tpu_custom_call" | custom-call | bytes 6815744 | tf_op jit(solution)/shard_map/pallas_call | solution.py:229
  11.1 22.0 %all_to_all.25 = bf16[8,8,3328]{2,1,0:T(8,128)(2,1)S(1)} all-to-all(bf16[8,8,3328]{2,1,0:T(8,128)(2,1)S(1)} %shard_map.50), channel_id=1, replica_groups=mesh['z'=8,'y'=4,'c'=2,'x'=4] {'z'}, dimensions={0} | all-to-all | bytes 851968 | tf_op jit(solution)/shard_map/all_to_all | solution.py:444
  33.1 1.3 collective-permute-start.4
  34.4 2.6 %collective-permute-start.3 = (bf16[64,3328]{1,0:T(8,128)(2,1)S(1)}, bf16[64,3328]{1,0:T(8,128)(2,1)S(1)}, u32[]{:S(2)}, u32[]{:S(2)}) collective-permute-start(bf16[64,3328]{1,0:T(8,128)(2,1)S(1)} %bitcast.14), channel_id=1, source_target_pairs={{16,0},{24,8},{0,16},{8,24},{17,1},{25,9},{1,17},{9,25},{18,2},{26... | collective-permute-start | bytes 1277960 | tf_op jit(solution)/shard_map/ppermute | solution.py:428
  37.0 1.1 collective-permute-start.2
  38.1 7.2 %collective-permute-done.4.refs_3_ = bf16[64,3328]{1,0:T(8,128)(2,1)S(1)} collective-permute-done((bf16[64,3328]{1,0:T(8,128)(2,1)S(1)}, bf16[64,3328]{1,0:T(8,128)(2,1)S(1)}, u32[]{:S(2)}, u32[]{:S(2)}) %collective-permute-start.4) | collective-permute-done | bytes 426016 | tf_op jit(solution)/shard_map/ppermute | solution.py:428
  45.3 10.2 %collective-permute-done.3.refs_2_ = bf16[64,3328]{1,0:T(8,128)(2,1)S(1)} collective-permute-done((bf16[64,3328]{1,0:T(8,128)(2,1)S(1)}, bf16[64,3328]{1,0:T(8,128)(2,1)S(1)}, u32[]{:S(2)}, u32[]{:S(2)}) %collective-permute-start.3) | collective-permute-done | bytes 426016 | tf_op jit(solution)/shard_map/ppermute | solution.py:428
  55.5 1.5 copy-done.1
  57.0 2.0 %shard_map.51 = (f32[256,256]{1,0:T(8,128)S(1)}, f32[256,256]{1,0:T(8,128)S(1)}) custom-call(s32[4]{0:T(128)S(1)} %copy-done.4, bf16[256,3328]{1,0:T(8,128)(2,1)S(1)} %copy-done.1, bf16[256,3328]{1,0:T(8,128)(2,1)S(1)} %collective-permute-done.1.other_ref, bf16[64,3328]{1,0:T(8,128)(2,1)S(1)} %bitcast.16, ...), custom_call_target="tpu_custom_call" | custom-call | flops 872415232 | bytes 5111808 | tf_op jit(solution)/shard_map/pallas_call | solution.py:163
  59.0 1.5 collective-permute-start.5
  60.5 1.2 collective-permute-done.5.two_ref
  61.7 1.3 collective-permute-start.8
  63.0 2.5 %collective-permute-start.7 = (f32[256,256]{1,0:T(8,128)S(1)}, f32[256,256]{1,0:T(8,128)S(1)}, u32[]{:S(2)}, u32[]{:S(2)}) collective-permute-start(f32[256,256]{1,0:T(8,128)S(1)} %shard_map.52.own_ref), channel_id=1, source_target_pairs={{2,0},{3,1},{0,2},{1,3},{6,4},{7,5},{4,6},{5,7},{10,8},{11,9},{8,1... | collective-permute-start | bytes 786440 | tf_op jit(solution)/shard_map/ppermute | solution.py:428
  65.4 1.1 collective-permute-start.6
  66.6 3.9 %collective-permute-done.8.three_ref = f32[256,256]{1,0:T(8,128)S(1)} collective-permute-done((f32[256,256]{1,0:T(8,128)S(1)}, f32[256,256]{1,0:T(8,128)S(1)}, u32[]{:S(2)}, u32[]{:S(2)}) %collective-permute-start.8) | collective-permute-done | bytes 262176 | tf_op jit(solution)/shard_map/ppermute | solution.py:428
  70.5 6.6 %collective-permute-done.7.two_ref = f32[256,256]{1,0:T(8,128)S(1)} collective-permute-done((f32[256,256]{1,0:T(8,128)S(1)}, f32[256,256]{1,0:T(8,128)S(1)}, u32[]{:S(2)}, u32[]{:S(2)}) %collective-permute-start.7) | collective-permute-done | bytes 262176 | tf_op jit(solution)/shard_map/ppermute | solution.py:428
  77.1 1.0 shard_map.53
  78.1 1.3 collective-permute-start.10
  79.5 1.1 collective-permute-done.9.two_ref
  80.6 0.9 collective-permute-start.13
  81.5 2.1 %collective-permute-start.12 = (f32[32,256]{1,0:T(8,128)S(1)}, f32[32,256]{1,0:T(8,128)S(1)}, u32[]{:S(2)}, u32[]{:S(2)}) collective-permute-start(f32[32,256]{1,0:T(8,128)S(1)} %shard_map.54.own_ref), channel_id=1, source_target_pairs={{16,0},{24,8},{0,16},{8,24},{17,1},{25,9},{1,17},{9,25},{18,2},{26... | collective-permute-start | bytes 98312 | tf_op jit(solution)/shard_map/ppermute | solution.py:428
  83.7 1.4 collective-permute-start.11
  85.1 4.0 %shard_map.59 = (f32[832,256]{1,0:T(8,128)S(1)}, f32[832,256]{1,0:T(8,128)S(1)}, f32[832,256]{1,0:T(8,128)S(1)}, f32[832,256]{1,0:T(8,128)S(1)}) custom-call(s32[4]{0:T(128)S(1)} %copy-done.4, bf16[256,3328]{1,0:T(8,128)(2,1)S(1)} %copy-done.2, bf16[256,3328]{1,0:T(8,128)(2,1)S(1)} %collective-permute-done.1.other_ref, ...), custom_call_target="tpu_custom_call" | custom-call | flops 2617245696 | bytes 10223616 | tf_op jit(solution)/shard_map/pallas_call | solution.py:335
  89.4 1.1 collective-permute-start.19
  90.5 1.6 collective-permute-start.20
  92.1 11.6 %all_to_all.26.pieces_ref = f32[8,32,256]{2,1,0:T(8,128)S(1)} all-to-all(f32[8,32,256]{2,1,0:T(8,128)S(1)} %shard_map.55), channel_id=1, replica_groups=mesh['z'=8,'y'=4,'c'=2,'x'=4] {'z'}, dimensions={0} | all-to-all | bytes 524288 | tf_op jit(solution)/shard_map/all_to_all | solution.py:444
  103.7 3.7 %collective-permute-start.14 = (f32[32,256]{1,0:T(8,128)S(1)}, f32[32,256]{1,0:T(8,128)S(1)}, u32[]{:S(2)}, u32[]{:S(2)}) collective-permute-start(f32[32,256]{1,0:T(8,128)S(1)} %bitcast.18), channel_id=1, source_target_pairs={{0,4},{4,0},{1,5},{5,1},{2,6},{6,2},{3,7},{7,3},{8,12},{12,8},{9,1... | collective-permute-start | bytes 98312 | tf_op jit(solution)/shard_map/ppermute | solution.py:424
  107.4 0.9 collective-permute-done.14
  108.3 1.1 collective-permute-start.17
  109.4 2.1 %collective-permute-start.16 = (f32[64,256]{1,0:T(8,128)S(1)}, f32[64,256]{1,0:T(8,128)S(1)}, u32[]{:S(2)}, u32[]{:S(2)}) collective-permute-start(f32[64,256]{1,0:T(8,128)S(1)} %pad_maximum_fusion.own_ref), channel_id=1, source_target_pairs={{2,0},{3,1},{0,2},{1,3},{6,4},{7,5},{4,6},{5,7},{10,8},{11,9},{8,1... | collective-permute-start | bytes 196616 | tf_op jit(solution)/shard_map/ppermute | solution.py:428
  111.5 1.5 collective-permute-done.17.last_ref
  113.7 1.3 collective-permute-done.16.across_ref
  115.0 1.3 collective-permute-done.15.next_ref
  116.3 9.9 %shard_map.57.inverse_ref = f32[256,256]{1,0:T(8,128)S(1)} custom-call(s32[4]{0:T(128)S(1)} %copy-done.4, f32[64,256]{1,0:T(8,128)S(1)} %pad_maximum_fusion.own_ref, f32[64,256]{1,0:T(8,128)S(1)} %collective-permute-done.15.next_ref, f32[64,256]{1,0:T(8,128)S(1)} %collective-permute-done.16.across_ref, f32[64,256]{1,0:T(8,128)S(1)} %collective-permute-done.17.last_ref), custom_call_target="tpu_custom_call" | custom-call | flops 1000000000 | bytes 1048576 | tf_op jit(solution)/shard_map/pallas_call | solution.py:127
  126.8 1.9 collective-permute-done.20.refs_3_
  128.8 0.9 shard_map.60
  129.7 15.2 %all_to_all.27.pieces_ref = bf16[8,104,256]{2,1,0:T(8,128)(2,1)S(1)} all-to-all(bf16[8,104,256]{2,1,0:T(8,128)(2,1)S(1)} %bitcast.17), channel_id=1, replica_groups=mesh['z'=8,'y'=4,'c'=2,'x'=4] {'z'}, dimensions={0} | all-to-all | bytes 851968 | tf_op jit(solution)/shard_map/all_to_all | solution.py:444
  144.9 15.6 %all_to_all.28 = bf16[8,104,256]{2,1,0:T(8,128)(2,1)S(1)} all-to-all(bf16[8,104,256]{2,1,0:T(8,128)(2,1)S(1)} %shard_map.61), channel_id=1, replica_groups=mesh['z'=8,'y'=4,'c'=2,'x'=4] {'z'}, dimensions={0} | all-to-all | bytes 851968 | tf_op jit(solution)/shard_map/all_to_all | solution.py:444
  160.5 4.3 %collective-permute-start.23 = (bf16[832,256]{1,0:T(8,128)(2,1)S(1)}, bf16[832,256]{1,0:T(8,128)(2,1)S(1)}, u32[]{:S(2)}, u32[]{:S(2)}) collective-permute-start(bf16[832,256]{1,0:T(8,128)(2,1)S(1)} %bitcast.8), channel_id=1, source_target_pairs={{0,4},{4,0},{1,5},{5,1},{2,6},{6,2},{3,7},{7,3},{8,12},{12,8},{9,1... | collective-permute-start | bytes 1277960 | tf_op jit(solution)/shard_map/ppermute | solution.py:424
  164.8 3.5 %collective-permute-start.22 = (bf16[832,256]{1,0:T(8,128)(2,1)S(1)}, bf16[832,256]{1,0:T(8,128)(2,1)S(1)}, u32[]{:S(2)}, u32[]{:S(2)}) collective-permute-start(bf16[832,256]{1,0:T(8,128)(2,1)S(1)} %bitcast.9), channel_id=1, source_target_pairs={{24,0},{0,8},{8,16},{16,24},{25,1},{1,9},{9,17},{17,25},{26,2},{2,... | collective-permute-start | bytes 1277960 | tf_op jit(solution)/shard_map/ppermute | solution.py:428
  169.0 12.9 %all_to_all.29.refs_3_ = f32[32,1,256]{2,1,0:T(1,128)S(1)} all-to-all(f32[32,1,256]{2,1,0:T(1,128)S(1)} %shard_map.62), channel_id=1, replica_groups=mesh['z'=8,'y'=4,'c'=2,'x'=4] {'y','c','x'}, dimensions={0} | all-to-all | bytes 65536 | tf_op jit(solution)/shard_map/all_to_all | solution.py:444
  182.3 2.4 %collective-permute-start.25 = (bf16[416,256]{1,0:T(8,128)(2,1)S(1)}, bf16[416,256]{1,0:T(8,128)(2,1)S(1)}, u32[]{:S(2)}, u32[]{:S(2)}) collective-permute-start(bf16[416,256]{1,0:T(8,128)(2,1)S(1)} %slice.7), channel_id=1, source_target_pairs={{8,0},{16,8},{24,16},{0,24},{9,1},{17,9},{25,17},{1,25},{10,2},{18... | collective-permute-start | bytes 638984 | tf_op jit(solution)/shard_map/ppermute | solution.py:428
  184.8 1.0 collective-permute-start.26
  185.7 3.9 %collective-permute-done.24.refs_7_ = bf16[416,256]{1,0:T(8,128)(2,1)S(1)} collective-permute-done((bf16[416,256]{1,0:T(8,128)(2,1)S(1)}, bf16[416,256]{1,0:T(8,128)(2,1)S(1)}, u32[]{:S(2)}, u32[]{:S(2)}) %collective-permute-start.24) | collective-permute-done | bytes 213024 | tf_op jit(solution)/shard_map/ppermute | solution.py:428
  189.6 1.2 collective-permute-start.28
  192.3 7.9 %shard_map.63 = (bf16[256,6656]{1,0:T(8,128)(2,1)}, bf16[256,6656]{1,0:T(8,128)(2,1)}, f32[4,6656]{1,0:T(4,128)}) custom-call(s32[4]{0:T(128)S(1)} %copy-done.4, bf16[256,6656]{1,0:T(8,128)(2,1)S(1)} %copy-done, f32[256,256]{1,0:T(8,128)S(1)} %shard_map.58.refs_2_, f32[32,1,256]{2,1,0:T(1,128)S(1)} %all_to_all.29.refs_3_, bf16[832,256]{1,0:T(8,128)(2,1)S(1)} %bitcast.12, ...), custom_call_target="tpu_custom_call" | custom-call | flops 1744830464 | bytes 13631488 | tf_op jit(solution)/shard_map/pallas_call | solution.py:398
  (47 shorter events, 6.5 us)
Async XLA Ops:
  0.6 9.9 %copy-start.3 = (f32[4,6656]{1,0:T(4,128)S(1)}, f32[4,6656]{1,0:T(4,128)}, u32[]{:S(2)}) copy-start(f32[4,6656]{1,0:T(4,128)} %basis_ref.1) | copy-start | bytes 319492
  1.5 4.1 %collective-permute-start = (f32[4,3328]{1,0:T(4,128)S(1)}, f32[4,3328]{1,0:T(4,128)S(1)}, u32[]{:S(2)}, u32[]{:S(2)}) collective-permute-start(f32[4,3328]{1,0:T(4,128)S(1)} %constant_dynamic-slice_fusion), channel_id=1, source_target_pairs={{0,4},{4,0},{1,5},{5,1},{2,6},{6,2},{3,7},{7,3},{8,12},{12,8},{9,1... | collective-permute-start | bytes 159752 | tf_op jit(solution)/shard_map/ppermute | solution.py:424
  5.4 5.1 %copy-start.4 = (s32[4]{0:T(128)S(1)}, s32[4]{0:T(128)}, u32[]{:S(2)}) copy-start(s32[4]{0:T(128)} %pad_add_fusion.at_ref.refs_0_) | copy-start | bytes 52
  10.1 45.5 %collective-permute-start.1 = (bf16[256,3328]{1,0:T(8,128)(2,1)}, bf16[256,3328]{1,0:T(8,128)(2,1)S(1)}, u32[]{:S(2)}, u32[]{:S(2)}) collective-permute-start(bf16[256,3328]{1,0:T(8,128)(2,1)} %get-tuple-element.24), channel_id=1, source_target_pairs={{0,4},{4,0},{1,5},{5,1},{2,6},{6,2},{3,7},{7,3},{8,12},{12,8},{9,1... | collective-permute-start | bytes 5111816 | tf_op jit(solution)/shard_map/ppermute | solution.py:424
  33.1 12.1 %collective-permute-start.4 = (bf16[64,3328]{1,0:T(8,128)(2,1)S(1)}, bf16[64,3328]{1,0:T(8,128)(2,1)S(1)}, u32[]{:S(2)}, u32[]{:S(2)}) collective-permute-start(bf16[64,3328]{1,0:T(8,128)(2,1)S(1)} %bitcast.13), channel_id=1, source_target_pairs={{24,0},{0,8},{8,16},{16,24},{25,1},{1,9},{9,17},{17,25},{26,2},{2,... | collective-permute-start | bytes 1277960 | tf_op jit(solution)/shard_map/ppermute | solution.py:428
  34.4 21.1 %collective-permute-start.3 = (bf16[64,3328]{1,0:T(8,128)(2,1)S(1)}, bf16[64,3328]{1,0:T(8,128)(2,1)S(1)}, u32[]{:S(2)}, u32[]{:S(2)}) collective-permute-start(bf16[64,3328]{1,0:T(8,128)(2,1)S(1)} %bitcast.14), channel_id=1, source_target_pairs={{16,0},{24,8},{0,16},{8,24},{17,1},{25,9},{1,17},{9,25},{18,2},{26... | collective-permute-start | bytes 1277960 | tf_op jit(solution)/shard_map/ppermute | solution.py:428
  37.0 18.5 %collective-permute-start.2 = (bf16[64,3328]{1,0:T(8,128)(2,1)S(1)}, bf16[64,3328]{1,0:T(8,128)(2,1)S(1)}, u32[]{:S(2)}, u32[]{:S(2)}) collective-permute-start(bf16[64,3328]{1,0:T(8,128)(2,1)S(1)} %bitcast.15), channel_id=1, source_target_pairs={{8,0},{16,8},{24,16},{0,24},{9,1},{17,9},{25,17},{1,25},{10,2},{18... | collective-permute-start | bytes 1277960 | tf_op jit(solution)/shard_map/ppermute | solution.py:428
  55.5 1.5 copy-start.1
  57.0 28.1 %copy-start.2 = (bf16[256,3328]{1,0:T(8,128)(2,1)S(1)}, bf16[256,3328]{1,0:T(8,128)(2,1)}, u32[]{:S(2)}) copy-start(bf16[256,3328]{1,0:T(8,128)(2,1)} %get-tuple-element.23.mine_ref) | copy-start | bytes 5111812
  59.0 2.7 %collective-permute-start.5 = (f32[256,256]{1,0:T(8,128)S(1)}, f32[256,256]{1,0:T(8,128)S(1)}, u32[]{:S(2)}, u32[]{:S(2)}) collective-permute-start(f32[256,256]{1,0:T(8,128)S(1)} %get-tuple-element.27), channel_id=1, source_target_pairs={{0,4},{4,0},{1,5},{5,1},{2,6},{6,2},{3,7},{7,3},{8,12},{12,8},{9,1... | collective-permute-start | bytes 786440 | tf_op jit(solution)/shard_map/ppermute | solution.py:424
  61.7 8.8 %collective-permute-start.8 = (f32[256,256]{1,0:T(8,128)S(1)}, f32[256,256]{1,0:T(8,128)S(1)}, u32[]{:S(2)}, u32[]{:S(2)}) collective-permute-start(f32[256,256]{1,0:T(8,128)S(1)} %shard_map.52.own_ref), channel_id=1, source_target_pairs={{3,0},{0,1},{1,2},{2,3},{7,4},{4,5},{5,6},{6,7},{11,8},{8,9},{9,10... | collective-permute-start | bytes 786440 | tf_op jit(solution)/shard_map/ppermute | solution.py:428
  63.0 14.1 %collective-permute-start.7 = (f32[256,256]{1,0:T(8,128)S(1)}, f32[256,256]{1,0:T(8,128)S(1)}, u32[]{:S(2)}, u32[]{:S(2)}) collective-permute-start(f32[256,256]{1,0:T(8,128)S(1)} %shard_map.52.own_ref), channel_id=1, source_target_pairs={{2,0},{3,1},{0,2},{1,3},{6,4},{7,5},{4,6},{5,7},{10,8},{11,9},{8,1... | collective-permute-start | bytes 786440 | tf_op jit(solution)/shard_map/ppermute | solution.py:428
  65.4 11.7 %collective-permute-start.6 = (f32[256,256]{1,0:T(8,128)S(1)}, f32[256,256]{1,0:T(8,128)S(1)}, u32[]{:S(2)}, u32[]{:S(2)}) collective-permute-start(f32[256,256]{1,0:T(8,128)S(1)} %shard_map.52.own_ref), channel_id=1, source_target_pairs={{1,0},{2,1},{3,2},{0,3},{5,4},{6,5},{7,6},{4,7},{9,8},{10,9},{11,1... | collective-permute-start | bytes 786440 | tf_op jit(solution)/shard_map/ppermute | solution.py:428
  78.1 2.5 %collective-permute-start.10 = (f32[256,256]{1,0:T(8,128)S(1)}, f32[256,256]{1,0:T(8,128)S(1)}, u32[]{:S(2)}, u32[]{:S(2)}) collective-permute-start(f32[256,256]{1,0:T(8,128)S(1)} %get-tuple-element.30.refs_0_.left_mine_ref), channel_id=1, source_target_pairs={{0,4},{4,0},{1,5},{5,1},{2,6},{6,2},{3,7},{7,3},{8,12},{12,8},{9,1... | collective-permute-start | bytes 786440 | tf_op jit(solution)/shard_map/ppermute | solution.py:424
  79.4 1.2 collective-permute-start.9
  80.6 9.9 %collective-permute-start.13 = (f32[32,256]{1,0:T(8,128)S(1)}, f32[32,256]{1,0:T(8,128)S(1)}, u32[]{:S(2)}, u32[]{:S(2)}) collective-permute-start(f32[32,256]{1,0:T(8,128)S(1)} %shard_map.54.own_ref), channel_id=1, source_target_pairs={{24,0},{0,8},{8,16},{16,24},{25,1},{1,9},{9,17},{17,25},{26,2},{2,... | collective-permute-start | bytes 98312 | tf_op jit(solution)/shard_map/ppermute | solution.py:428
  81.5 10.5 %collective-permute-start.12 = (f32[32,256]{1,0:T(8,128)S(1)}, f32[32,256]{1,0:T(8,128)S(1)}, u32[]{:S(2)}, u32[]{:S(2)}) collective-permute-start(f32[32,256]{1,0:T(8,128)S(1)} %shard_map.54.own_ref), channel_id=1, source_target_pairs={{16,0},{24,8},{0,16},{8,24},{17,1},{25,9},{1,17},{9,25},{18,2},{26... | collective-permute-start | bytes 98312 | tf_op jit(solution)/shard_map/ppermute | solution.py:428
  83.7 8.4 %collective-permute-start.11 = (f32[32,256]{1,0:T(8,128)S(1)}, f32[32,256]{1,0:T(8,128)S(1)}, u32[]{:S(2)}, u32[]{:S(2)}) collective-permute-start(f32[32,256]{1,0:T(8,128)S(1)} %shard_map.54.own_ref), channel_id=1, source_target_pairs={{8,0},{16,8},{24,16},{0,24},{9,1},{17,9},{25,17},{1,25},{10,2},{18... | collective-permute-start | bytes 98312 | tf_op jit(solution)/shard_map/ppermute | solution.py:428
  89.0 37.2 %collective-permute-start.18 = (f32[832,256]{1,0:T(8,128)S(1)}, f32[832,256]{1,0:T(8,128)S(1)}, u32[]{:S(2)}, u32[]{:S(2)}) collective-permute-start(f32[832,256]{1,0:T(8,128)S(1)} %get-tuple-element.34), channel_id=1, source_target_pairs={{24,0},{0,8},{8,16},{16,24},{25,1},{1,9},{9,17},{17,25},{26,2},{2,... | collective-permute-start | bytes 2555912 | tf_op jit(solution)/shard_map/ppermute | solution.py:428
  89.4 37.4 %collective-permute-start.19 = (f32[832,256]{1,0:T(8,128)S(1)}, f32[832,256]{1,0:T(8,128)S(1)}, u32[]{:S(2)}, u32[]{:S(2)}) collective-permute-start(f32[832,256]{1,0:T(8,128)S(1)} %get-tuple-element.35), channel_id=1, source_target_pairs={{16,0},{24,8},{0,16},{8,24},{17,1},{25,9},{1,17},{9,25},{18,2},{26... | collective-permute-start | bytes 2555912 | tf_op jit(solution)/shard_map/ppermute | solution.py:428
  90.5 38.3 %collective-permute-start.20 = (f32[832,256]{1,0:T(8,128)S(1)}, f32[832,256]{1,0:T(8,128)S(1)}, u32[]{:S(2)}, u32[]{:S(2)}) collective-permute-start(f32[832,256]{1,0:T(8,128)S(1)} %get-tuple-element.36), channel_id=1, source_target_pairs={{8,0},{16,8},{24,16},{0,24},{9,1},{17,9},{25,17},{1,25},{10,2},{18... | collective-permute-start | bytes 2555912 | tf_op jit(solution)/shard_map/ppermute | solution.py:428
  103.7 4.6 %collective-permute-start.14 = (f32[32,256]{1,0:T(8,128)S(1)}, f32[32,256]{1,0:T(8,128)S(1)}, u32[]{:S(2)}, u32[]{:S(2)}) collective-permute-start(f32[32,256]{1,0:T(8,128)S(1)} %bitcast.18), channel_id=1, source_target_pairs={{0,4},{4,0},{1,5},{5,1},{2,6},{6,2},{3,7},{7,3},{8,12},{12,8},{9,1... | collective-permute-start | bytes 98312 | tf_op jit(solution)/shard_map/ppermute | solution.py:424
  108.3 4.6 %collective-permute-start.17 = (f32[64,256]{1,0:T(8,128)S(1)}, f32[64,256]{1,0:T(8,128)S(1)}, u32[]{:S(2)}, u32[]{:S(2)}) collective-permute-start(f32[64,256]{1,0:T(8,128)S(1)} %pad_maximum_fusion.own_ref), channel_id=1, source_target_pairs={{3,0},{0,1},{1,2},{2,3},{7,4},{4,5},{5,6},{6,7},{11,8},{8,9},{9,10... | collective-permute-start | bytes 196616 | tf_op jit(solution)/shard_map/ppermute | solution.py:428
  109.4 5.6 %collective-permute-start.16 = (f32[64,256]{1,0:T(8,128)S(1)}, f32[64,256]{1,0:T(8,128)S(1)}, u32[]{:S(2)}, u32[]{:S(2)}) collective-permute-start(f32[64,256]{1,0:T(8,128)S(1)} %pad_maximum_fusion.own_ref), channel_id=1, source_target_pairs={{2,0},{3,1},{0,2},{1,3},{6,4},{7,5},{4,6},{5,7},{10,8},{11,9},{8,1... | collective-permute-start | bytes 196616 | tf_op jit(solution)/shard_map/ppermute | solution.py:428
  112.9 3.4 %collective-permute-start.15 = (f32[64,256]{1,0:T(8,128)S(1)}, f32[64,256]{1,0:T(8,128)S(1)}, u32[]{:S(2)}, u32[]{:S(2)}) collective-permute-start(f32[64,256]{1,0:T(8,128)S(1)} %pad_maximum_fusion.own_ref), channel_id=1, source_target_pairs={{1,0},{2,1},{3,2},{0,3},{5,4},{6,5},{7,6},{4,7},{9,8},{10,9},{11,1... | collective-permute-start | bytes 196616 | tf_op jit(solution)/shard_map/ppermute | solution.py:428
  128.8 63.6 %copy-start = (bf16[256,6656]{1,0:T(8,128)(2,1)S(1)}, bf16[256,6656]{1,0:T(8,128)(2,1)}, u32[]{:S(2)}) copy-start(bf16[256,6656]{1,0:T(8,128)(2,1)} %refs_1_.1) | copy-start | bytes 10223620
  160.5 21.4 %collective-permute-start.23 = (bf16[832,256]{1,0:T(8,128)(2,1)S(1)}, bf16[832,256]{1,0:T(8,128)(2,1)S(1)}, u32[]{:S(2)}, u32[]{:S(2)}) collective-permute-start(bf16[832,256]{1,0:T(8,128)(2,1)S(1)} %bitcast.8), channel_id=1, source_target_pairs={{0,4},{4,0},{1,5},{5,1},{2,6},{6,2},{3,7},{7,3},{8,12},{12,8},{9,1... | collective-permute-start | bytes 1277960 | tf_op jit(solution)/shard_map/ppermute | solution.py:424
  164.8 17.1 %collective-permute-start.22 = (bf16[832,256]{1,0:T(8,128)(2,1)S(1)}, bf16[832,256]{1,0:T(8,128)(2,1)S(1)}, u32[]{:S(2)}, u32[]{:S(2)}) collective-permute-start(bf16[832,256]{1,0:T(8,128)(2,1)S(1)} %bitcast.9), channel_id=1, source_target_pairs={{24,0},{0,8},{8,16},{16,24},{25,1},{1,9},{9,17},{17,25},{26,2},{2,... | collective-permute-start | bytes 1277960 | tf_op jit(solution)/shard_map/ppermute | solution.py:428
  168.3 13.6 %collective-permute-start.21 = (bf16[832,256]{1,0:T(8,128)(2,1)S(1)}, bf16[832,256]{1,0:T(8,128)(2,1)S(1)}, u32[]{:S(2)}, u32[]{:S(2)}) collective-permute-start(bf16[832,256]{1,0:T(8,128)(2,1)S(1)} %bitcast.10), channel_id=1, source_target_pairs={{8,0},{16,8},{24,16},{0,24},{9,1},{17,9},{25,17},{1,25},{10,2},{18... | collective-permute-start | bytes 1277960 | tf_op jit(solution)/shard_map/ppermute | solution.py:428
  181.9 7.7 %collective-permute-start.24 = (bf16[416,256]{1,0:T(8,128)(2,1)S(1)}, bf16[416,256]{1,0:T(8,128)(2,1)S(1)}, u32[]{:S(2)}, u32[]{:S(2)}) collective-permute-start(bf16[416,256]{1,0:T(8,128)(2,1)S(1)} %slice.6), channel_id=1, source_target_pairs={{24,0},{0,8},{8,16},{16,24},{25,1},{1,9},{9,17},{17,25},{26,2},{2,... | collective-permute-start | bytes 638984 | tf_op jit(solution)/shard_map/ppermute | solution.py:428
  182.3 8.5 %collective-permute-start.25 = (bf16[416,256]{1,0:T(8,128)(2,1)S(1)}, bf16[416,256]{1,0:T(8,128)(2,1)S(1)}, u32[]{:S(2)}, u32[]{:S(2)}) collective-permute-start(bf16[416,256]{1,0:T(8,128)(2,1)S(1)} %slice.7), channel_id=1, source_target_pairs={{8,0},{16,8},{24,16},{0,24},{9,1},{17,9},{25,17},{1,25},{10,2},{18... | collective-permute-start | bytes 638984 | tf_op jit(solution)/shard_map/ppermute | solution.py:428
  184.8 7.6 %collective-permute-start.26 = (bf16[832,256]{1,0:T(8,128)(2,1)S(1)}, bf16[832,256]{1,0:T(8,128)(2,1)S(1)}, u32[]{:S(2)}, u32[]{:S(2)}) collective-permute-start(bf16[832,256]{1,0:T(8,128)(2,1)S(1)} %collective-permute-done.21.refs_5_), channel_id=1, source_target_pairs={{0,4},{4,0},{1,5},{5,1},{2,6},{6,2},{3,7},{7,3},{8,12},{12,8},{9,1... | collective-permute-start | bytes 1277960 | tf_op jit(solution)/shard_map/ppermute | solution.py:424
  185.7 6.6 %collective-permute-start.27 = (bf16[832,256]{1,0:T(8,128)(2,1)S(1)}, bf16[832,256]{1,0:T(8,128)(2,1)S(1)}, u32[]{:S(2)}, u32[]{:S(2)}) collective-permute-start(bf16[832,256]{1,0:T(8,128)(2,1)S(1)} %collective-permute-done.22.refs_6_), channel_id=1, source_target_pairs={{0,4},{4,0},{1,5},{5,1},{2,6},{6,2},{3,7},{7,3},{8,12},{12,8},{9,1... | collective-permute-start | bytes 1277960 | tf_op jit(solution)/shard_map/ppermute | solution.py:424
  189.6 2.3 %collective-permute-start.28 = (bf16[416,256]{1,0:T(8,128)(2,1)S(1)}, bf16[416,256]{1,0:T(8,128)(2,1)S(1)}, u32[]{:S(2)}, u32[]{:S(2)}) collective-permute-start(bf16[416,256]{1,0:T(8,128)(2,1)S(1)} %collective-permute-done.24.refs_7_), channel_id=1, source_target_pairs={{0,4},{4,0},{1,5},{5,1},{2,6},{6,2},{3,7},{7,3},{8,12},{12,8},{9,1... | collective-permute-start | bytes 638984 | tf_op jit(solution)/shard_map/ppermute | solution.py:424
  190.9 1.5 collective-permute-start.29

commit v4 on v2

--- a/solution.py
+++ b/solution.py
@@ -19,7 +19,7 @@
 MIB = 2**20
 NZ, NY, NX = 8, 4, 4
 PIVOTS = 8
-RING_FROM = (0, 1, 3, 2, 2)
+MAIN, TAIL = 768, 64
 AT_Y, AT_CORE, AT_X, FIRST_RANK = range(4)
 
 
@@ -211,32 +211,16 @@
     return small(kernel, jax.ShapeDtypeStruct(shape, pieces.dtype), pieces)
 
 
-def basis_copies(at, basis, received, copies):
-    shard_rank, half = received.shape
-
-    def kernel(at_ref, basis_ref, received_ref, out_ref):
-        core = at_ref[AT_CORE]
-        own = basis_ref[:, pl.ds(pl.multiple_of(core * half, half), half)]
-        other = received_ref[...]
-        first = jnp.where(core == 0, own, other)
-        second = jnp.where(core == 0, other, own)
-        chip = jnp.concatenate([first, second], axis=0).astype(bf16)
-        for n in range(copies):
-            out_ref[n] = chip
-
-    return small(kernel, jax.ShapeDtypeStruct((copies, 2 * shard_rank, half), bf16), at, basis, received)
-
-
 def square_copies(right, copies):
     rank = right.shape[1]
 
     def kernel(right_ref, out_ref):
         right = right_ref[...].astype(f32)
-        out_ref[...] = jnp.broadcast_to(
-            jnp.sum(right * right, axis=0, keepdims=True), out_ref.shape
-        )
-
-    return small(kernel, jax.ShapeDtypeStruct((copies * 8, rank), f32), right)
+        total = jnp.sum(right * right, axis=0, keepdims=True)
+        for n in range(copies):
+            out_ref[n] = total
+
+    return small(kernel, jax.ShapeDtypeStruct((copies, 1, rank), f32), right)
 
 
 def whiten(inverse, pieces, out):
@@ -297,10 +281,10 @@
         return carry
 
     lax.fori_loop(0, 2, multiply, 0)
-    size = pieces[0].shape[0]
     for by, ref in enumerate(pieces):
-        start = pl.multiple_of(ahead(at_ref[AT_Y], by, NY) * size, size)
-        ref[...] = whole_ref[pl.ds(start, size), :]
+        place = ahead(at_ref[AT_Y], by, NY)
+        ref[:MAIN, :] = whole_ref[pl.ds(pl.multiple_of(place * MAIN, MAIN), MAIN), :]
+        ref[MAIN:, :] = whole_ref[pl.ds(pl.multiple_of(NY * MAIN + place * TAIL, TAIL), TAIL), :]
 
 
 def cross(at, mine, other, left_mine, left_other):
@@ -319,79 +303,172 @@
     )(at, mine, other, left_mine, left_other)
 
 
-def finish_kernel(scaling, at_ref, momentum_ref, solved_ref, squares_ref, *refs):
-    pieces = refs[:10]
-    new_momentum_ref, update_ref, q_next_ref, right_ref, left_ref, inverse_ref, semaphores = refs[10:]
+def prepare_left(scaling, at_ref, solved_ref, squares_ref, left_ref, inverse_ref):
     rows, rank = solved_ref.shape
-    step = pl.program_id(0)
-    width = momentum_ref.shape[1]
-    shard_rank = q_next_ref.shape[0]
-    size = pieces[0].shape[0]
-
-    @pl.when(step == 0)
-    def _():
-        copies = []
-        for n, ref in enumerate(pieces):
-            side = at_ref[AT_CORE] if n < 5 else 1 - at_ref[AT_CORE]
-            start = (side * NY + ahead(at_ref[AT_Y], RING_FROM[n % 5], NY)) * size
-            start = pl.multiple_of(start + (ref.shape[0] if n % 5 == 4 else 0), 16)
-            copy = pltpu.make_async_copy(
-                ref, right_ref.at[pl.ds(start, ref.shape[0]), :], semaphores.at[n]
-            )
-            copy.start()
-            copies.append(copy)
-        solved = solved_ref[...]
-        squares = jnp.sum(squares_ref[...], axis=0, keepdims=True) / 8
-        inverse_lengths = lax.rsqrt(squares + 1e-06)
-        left_ref[:rows, :] = solved.astype(bf16)
-        left_ref[rows : 2 * rows, :] = (solved * (scaling * inverse_lengths)).astype(bf16)
-        wanted = lax.broadcasted_iota(jnp.int32, (16, rank), 0) + at_ref[FIRST_RANK]
-        picked = jnp.where(wanted == lax.broadcasted_iota(jnp.int32, (16, rank), 1), 1.0, 0.0)
-        left_ref[2 * rows :, :] = picked.astype(bf16)
-        own = jnp.sum(picked * inverse_lengths, axis=1, keepdims=True)
-        inverse_ref[...] = jnp.broadcast_to(own, inverse_ref.shape)
-        for copy in copies:
-            copy.wait()
-
-    right = right_ref[pl.ds(pl.multiple_of(step * width, width), width), :]
-    product = lax.dot_general(left_ref[...], right, BOTH_LAST, preferred_element_type=f32)
-    momentum = momentum_ref[...].astype(f32)
-    new_momentum_ref[...] = (momentum - (1.0 - momentum_decay) * product[:rows]).astype(bf16)
-    update_ref[...] = product[rows : 2 * rows].astype(bf16)
-    q_next_ref[...] = (
-        product[2 * rows : 2 * rows + shard_rank] * inverse_ref[:shard_rank, :1]
-    )
-
-
-def finish(at, momentum, solved, squares, pieces, scaling, shard_rank):
+    solved = solved_ref[...]
+    squares = jnp.sum(squares_ref[...], axis=0)
+    inverse_lengths = lax.rsqrt(squares + 1e-06)
+    left_ref[:rows, :] = solved.astype(bf16)
+    left_ref[rows : 2 * rows, :] = (solved * (scaling * inverse_lengths)).astype(bf16)
+    wanted = lax.broadcasted_iota(jnp.int32, (16, rank), 0) + at_ref[FIRST_RANK]
+    picked = jnp.where(wanted == lax.broadcasted_iota(jnp.int32, (16, rank), 1), 1.0, 0.0)
+    left_ref[2 * rows :, :] = picked.astype(bf16)
+    own = jnp.sum(picked * inverse_lengths, axis=1, keepdims=True)
+    inverse_ref[...] = jnp.broadcast_to(own, inverse_ref.shape)
+
+
+def write_blocks(column_of, right_ref, momentum_ref, out_refs, stage_refs, left_ref, inverse_ref, semaphores):
+    taken_ref, stages = stage_refs[0], stage_refs[1:]
+    blocks, rows, width = taken_ref.shape
+    shard_rank = stages[2].shape[1]
+
+    def take(n):
+        columns = pl.ds(pl.multiple_of(column_of(n), 128), width)
+        return pltpu.make_async_copy(momentum_ref.at[:, columns], taken_ref.at[n], semaphores.at[0, n])
+
+    def give(n, out):
+        columns = pl.ds(pl.multiple_of(column_of(n), 128), width)
+        return pltpu.make_async_copy(
+            stages[out].at[n], out_refs[out].at[:, columns], semaphores.at[1 + out, n]
+        )
+
+    def write(n, carry):
+        right = right_ref[pl.ds(pl.multiple_of(n * width, width), width), :]
+        product = lax.dot_general(left_ref[...], right, BOTH_LAST, preferred_element_type=f32)
+        stages[1][n] = product[rows : 2 * rows].astype(bf16)
+        stages[2][n] = product[2 * rows : 2 * rows + shard_rank] * inverse_ref[:shard_rank, :1]
+        take(n).wait()
+        momentum = taken_ref[n].astype(f32)
+        stages[0][n] = (momentum - (1.0 - momentum_decay) * product[:rows]).astype(bf16)
+        for out in range(3):
+            give(n, out).start()
+        return carry
+
+    def start():
+        for n in range(blocks):
+            take(n).start()
+
+    def wait():
+        for n in range(blocks):
+            for out in range(3):
+                give(n, out).wait()
+
+    return start, lambda: lax.fori_loop(0, blocks, write, 0), wait
+
+
+def stages_of(blocks, rows, width, shard_rank):
+    return [
+        pltpu.VMEM((blocks, rows, width), bf16),
+        pltpu.VMEM((blocks, rows, width), bf16),
+        pltpu.VMEM((blocks, rows, width), bf16),
+        pltpu.VMEM((blocks, shard_rank, width), f32),
+        pltpu.SemaphoreType.DMA((4, blocks)),
+    ]
+
+
+def first_kernel(scaling, at_ref, momentum_ref, solved_ref, squares_ref, *refs):
+    pieces, outs = refs[:6], refs[6:9]
+    right_ref, left_ref, inverse_ref, loads = refs[9:13]
+    stages, semaphores = refs[13:17], refs[17]
+    half = momentum_ref.shape[1] // 2
+
+    def column_of(n):
+        side = lax.rem(at_ref[AT_CORE] + n // 3, 2)
+        by = n % 3 + n % 3 // 2
+        return side * half + ahead(at_ref[AT_Y], by, NY) * MAIN
+
+    start, write, wait = write_blocks(
+        column_of, right_ref, momentum_ref, outs, stages, left_ref, inverse_ref, semaphores
+    )
+    copies = [
+        pltpu.make_async_copy(
+            ref.at[pl.ds(0, MAIN), :], right_ref.at[pl.ds(n * MAIN, MAIN), :], loads.at[n]
+        )
+        for n, ref in enumerate(pieces)
+    ]
+    for copy in copies:
+        copy.start()
+    start()
+    prepare_left(scaling, at_ref, solved_ref, squares_ref, left_ref, inverse_ref)
+    for copy in copies:
+        copy.wait()
+    write()
+    wait()
+
+
+def second_kernel(scaling, at_ref, momentum_ref, solved_ref, squares_ref, *refs):
+    pieces, outs = refs[:10], refs[13:16]
+    main_ref, tail_ref, left_ref, inverse_ref = refs[16:20]
+    main_stages, main_semaphores = refs[20:24], refs[24]
+    tail_stages, tail_semaphores = refs[25:29], refs[29]
+    half = momentum_ref.shape[1] // 2
+
+    def side_of(n):
+        return lax.rem(at_ref[AT_CORE] + n, 2)
+
+    start_main, write_main, wait_main = write_blocks(
+        lambda n: side_of(n) * half + ahead(at_ref[AT_Y], 2, NY) * MAIN,
+        main_ref, momentum_ref, outs, main_stages, left_ref, inverse_ref, main_semaphores,
+    )
+    start_tail, write_tail, wait_tail = write_blocks(
+        lambda n: side_of(n) * half + NY * MAIN,
+        tail_ref, momentum_ref, outs, tail_stages, left_ref, inverse_ref, tail_semaphores,
+    )
+    start_main()
+    start_tail()
+    prepare_left(scaling, at_ref, solved_ref, squares_ref, left_ref, inverse_ref)
+    for side in range(2):
+        own, one, three, front, back = pieces[5 * side : 5 * side + 5]
+        size = front.shape[0]
+        main_ref[side * MAIN : side * MAIN + size, :] = front[...]
+        main_ref[side * MAIN + size : (side + 1) * MAIN, :] = back[: MAIN - size, :]
+        for by, ref, begin in ((0, own, MAIN), (1, one, MAIN), (3, three, MAIN), (2, back, MAIN - size)):
+            place = side * NY * TAIL + ahead(at_ref[AT_Y], by, NY) * TAIL
+            tail_ref[pl.ds(pl.multiple_of(place, TAIL), TAIL), :] = ref[begin : begin + TAIL, :]
+    write_main()
+    write_tail()
+    wait_main()
+    wait_tail()
+
+
+def finish(at, momentum, solved, squares, near, far, scaling, shard_rank):
     rows, cols = momentum.shape
     rank = solved.shape[1]
-    width = cols // 4
-    columns = pl.BlockSpec((rows, width), lambda i: (0, i))
-    out = jax.ShapeDtypeStruct((rows, cols), bf16)
+    outs = [jax.ShapeDtypeStruct((rows, cols), bf16)] * 2 + [jax.ShapeDtypeStruct((shard_rank, cols), f32)]
+    both = [pltpu.VMEM((2 * rows + 16, rank), bf16), pltpu.VMEM((16, 128), f32)]
+    first = pl.pallas_call(
+        lambda *refs: first_kernel(scaling, *refs),
+        out_shape=outs,
+        in_specs=[SMEM, ANY, VMEM, VMEM] + [ANY] * 6,
+        out_specs=[ANY] * 3,
+        scratch_shapes=[pltpu.VMEM((6 * MAIN, rank), bf16)]
+        + both
+        + [pltpu.SemaphoreType.DMA((6,))]
+        + stages_of(6, rows, MAIN, shard_rank),
+        compiler_params=pltpu.CompilerParams(vmem_limit_bytes=18 * MIB),
+        cost_estimate=pl.CostEstimate(
+            flops=3 * rows * cols * rank, bytes_accessed=6 * rows * cols, transcendentals=0
+        ),
+    )(at, momentum, solved, squares, *near)
+    first = list(first)
+    first[2], far = lax.optimization_barrier((first[2], far))
+    far = far + tuple(swap_cores(block) for block in far)
+    pieces = near[:3] + far[:2] + near[3:] + far[2:]
     return pl.pallas_call(
-        lambda *refs: finish_kernel(scaling, *refs),
-        out_shape=[out, out, jax.ShapeDtypeStruct((shard_rank, cols), f32)],
-        grid=(4,),
-        in_specs=[
-            SMEM,
-            columns,
-            pl.BlockSpec(solved.shape, lambda i: (0, 0)),
-            pl.BlockSpec(squares.shape, lambda i: (0, 0)),
-        ]
-        + [ANY] * 10,
-        out_specs=[columns, columns, pl.BlockSpec((shard_rank, width), lambda i: (0, i))],
-        scratch_shapes=[
-            pltpu.VMEM((cols, rank), bf16),
-            pltpu.VMEM((2 * rows + 16, rank), bf16),
-            pltpu.VMEM((16, 128), f32),
-            pltpu.SemaphoreType.DMA((10,)),
-        ],
-        compiler_params=pltpu.CompilerParams(vmem_limit_bytes=20 * MIB),
+        lambda *refs: second_kernel(scaling, *refs),
+        out_shape=outs,
+        in_specs=[SMEM, ANY, VMEM, VMEM] + [VMEM] * 10 + [ANY] * 3,
+        out_specs=[ANY] * 3,
+        scratch_shapes=[pltpu.VMEM((2 * MAIN, rank), bf16), pltpu.VMEM((2 * NY * TAIL, rank), bf16)]
+        + both
+        + stages_of(2, rows, MAIN, shard_rank)
+        + stages_of(2, rows, NY * TAIL, shard_rank),
+        input_output_aliases={14: 0, 15: 1, 16: 2},
+        compiler_params=pltpu.CompilerParams(vmem_limit_bytes=18 * MIB),
         cost_estimate=pl.CostEstimate(
-            flops=4 * rows * cols * rank, bytes_accessed=8 * rows * cols, transcendentals=0
+            flops=rows * cols * rank, bytes_accessed=2 * rows * cols, transcendentals=0
         ),
-    )(at, momentum, solved, squares, *pieces)
+    )(at, momentum, solved, squares, *pieces, *first)
 
 
 def swap_cores(block):
@@ -406,12 +483,12 @@
     return [block] + [from_ahead(block, axis, by) for by in (1, 2, 3)]
 
 
-def ring_of_four(block, axis, beside=None):
+def ring_of_four(block, axis, beside):
     middle = block.shape[0] // 2
     one, three = from_ahead(block, axis, 1), from_ahead(block, axis, 3)
     one, three, beside = lax.optimization_barrier((one, three, beside))
     across = (from_ahead(three[:middle], axis, 3), from_ahead(one[middle:], axis, 1))
-    return (block, one, three) + across, beside
+    return (block, one, three), across, beside
 
 
 def exchange(pieces, axes):
@@ -431,14 +508,19 @@
     def columns(array, of_core):
         return lax.dynamic_slice_in_dim(array, of_core * half, half, 1)
 
-    received = swap_cores(columns(q_basis, 1 - core))
-    later, received = lax.optimization_barrier((momentum, received))
+    basis_half = q_basis.astype(bf16)
+    basis_own = columns(basis_half, core)
+    basis_other = swap_cores(columns(basis_half, 1 - core))
+    basis_chip = jnp.concatenate(
+        [jnp.where(core == 0, basis_own, basis_other), jnp.where(core == 0, basis_other, basis_own)]
+    )
+    later, basis_chip, at = lax.optimization_barrier((momentum, basis_chip, at))
     mine = columns(later, core)
     other = swap_cores(columns(later, 1 - core))
 
-    basis = exchange(basis_copies(at, q_basis, received, NZ), "z").reshape(rank // NY, half)
-    basis = all_of_four(basis, "y")
-    proj_mine, proj_other = project(at, mine, other, basis)
+    basis = exchange(jnp.broadcast_to(basis_chip[None], (NZ,) + basis_chip.shape), "z")
+    basis = basis.reshape(rank // NY, half)
+    proj_mine, proj_other = project(at, mine, other, all_of_four(basis, "y"))
     proj_chip = add(proj_mine, swap_cores(proj_other))
     projected, gram_keep, gram_send = gram_rows_of(at, all_of_four(proj_chip, "x"))
 
@@ -456,15 +538,14 @@
     solved = whiten(inverse, [projected], f32)
 
     parts = NY * 2 * NX
-    squares = square_copies(right, parts).reshape(parts, 8, rank)
-    squares = exchange(squares, ("y", "c", "x")).reshape(parts * 8, rank)
-    pieces, (squares, swapped) = ring_of_four(right, "y", (squares, swap_cores(right)))
-    pieces = pieces + (swapped,) + tuple(swap_cores(piece) for piece in pieces[1:])
+    squares = exchange(square_copies(right, parts), ("y", "c", "x"))
+    near, far, (squares, swapped) = ring_of_four(right, "y", (squares, swap_cores(right)))
+    near = near + (swapped,) + tuple(swap_cores(block) for block in near[1:])
 
     total_rows = rows * NZ * NY * 2
     total_cols = cols * NX
     scaling = math.sqrt(total_rows * total_cols / rank)
-    return tuple(finish(at, momentum, solved, squares, pieces, scaling, shard_rank))
+    return tuple(finish(at, momentum, solved, squares, near, far, scaling, shard_rank))
 
 
 def solution(mesh):

time: 201 us -> 194 us (0.965)
  waiting for transfers between devices: 44 us -> 39.8 us
  local copies, waits for them, and re-layouts: 5.66 us -> 2.28 us
    ppermute x19, waiting for transfers between devices: 38.9 us -> 34.5 us  [from_ahead(): lax.ppermute(block, axis, [((i + by) % parts, i) for i in range(parts)])]
    pallas_call x1 -> x2, Pallas kernels: 7.93 us -> 9.44 us  [the longest x1 6.19 us: finish(): pl.pallas_call(lambda *refs: first_kernel(scaling, *refs), out_shape=outs...]
  transfers between devices with their start and end apart: 30 -> 30, of which waited for: 16 -> 15; matrix products, arithmetic and copies ran while one was open for 0% -> 0% of each run, Pallas kernels for 7% -> 11%
where the time goes in v4:
time: 194 us
  blocking collectives  77.2 us (40%)
  starting transfers between devices  44.4 us (23%)
  waiting for transfers between devices  39.8 us (21%)
  Pallas kernels  27.9 us (14%)
  local copies, waits for them, and re-layouts  2.28 us (1%)
    all_to_all x5, blocking collectives, exchange(): return lax.all_to_all(pieces, axes, 0, 0)  77.2 us
    ppermute x19, waiting for transfers between devices, from_ahead(): lax.ppermute(block, axis, [((i + by) % parts, i) for i in range(parts)])  34.5 us
    ppermute x19, starting transfers between devices, from_ahead(): lax.ppermute(block, axis, [((i + by) % parts, i) for i in range(parts)])  28 us
    ppermute x11, starting transfers between devices, swap_cores(): return lax.ppermute(block, 'c', [(0, 1), (1, 0)])  16.4 us
    pallas_call x1, Pallas kernels, inverse_factor(): pl.pallas_call(inverse_factor_kernel, out_shape=jax.ShapeDtypeStruct((ran...  9.93 us
    pallas_call x1, Pallas kernels, finish(): pl.pallas_call(lambda *refs: first_kernel(scaling, *refs), out_shape=outs...  6.19 us
    ppermute x11, waiting for transfers between devices, swap_cores(): return lax.ppermute(block, 'c', [(0, 1), (1, 0)])  5.28 us
    pallas_call x1, Pallas kernels, cross(): pl.pallas_call(cross_kernel, out_shape=[jax.ShapeDtypeStruct((cols // NY,...  3.98 us
  transfers between devices with their start and end apart: 30, of which 15 were waited for; matrix products, arithmetic and copies ran while one was open for 0% of the time, Pallas kernels for 11%

profile of v4, /device:TPU:1, one launch (start us, length us, event | category | flops | bytes accessed | tf_op | source)
XLA Modules:
  0.0 193.7 jit_solution(9374635685887947621)
XLA Ops:
  0.6 0.9 convert_element_type.3
  1.6 3.3 %collective-permute-start = (bf16[4,3328]{1,0:T(4,128)(2,1)S(1)}, bf16[4,3328]{1,0:T(4,128)(2,1)S(1)}, u32[]{:S(2)}, u32[]{:S(2)}) collective-permute-start(bf16[4,3328]{1,0:T(4,128)(2,1)S(1)} %constant_dynamic-slice_fusion.2), channel_id=1, source_target_pairs={{0,4},{4,0},{1,5},{5,1},{2,6},{6,2},{3,7},{7,3},{8,12},{12,8},{9,1... | collective-permute-start | bytes 79880 | tf_op jit(solution)/shard_map/ppermute | solution.py:475
  5.8 2.2 %constant_dynamic-slice_fusion = (bf16[256,3328]{1,0:T(8,128)(2,1)S(1)}, bf16[256,3328]{1,0:T(8,128)(2,1)S(1)}) fusion(bf16[256,6656]{1,0:T(8,128)(2,1)} %refs_1_.3, s32[]{:T(128)S(6)} %select_n.22, s32[]{:T(128)S(6)} %select_n.21), kind=kLoop, calls=%fused_computation.4 | loop fusion | bytes 6815752 | tf_op jit(solution)/shard_map/dynamic_slice | solution.py:509
  8.5 22.0 %all_to_all.25 = bf16[8,8,3328]{2,1,0:T(8,128)(2,1)S(1)} all-to-all(bf16[8,8,3328]{2,1,0:T(8,128)(2,1)S(1)} %broadcast_in_dim.2), channel_id=1, replica_groups=mesh['z'=8,'y'=4,'c'=2,'x'=4] {'z'}, dimensions={0} | all-to-all | bytes 851968 | tf_op jit(solution)/shard_map/all_to_all | solution.py:495
  30.5 1.3 collective-permute-start.4
  31.8 2.6 %collective-permute-start.3 = (bf16[64,3328]{1,0:T(8,128)(2,1)S(1)}, bf16[64,3328]{1,0:T(8,128)(2,1)S(1)}, u32[]{:S(2)}, u32[]{:S(2)}) collective-permute-start(bf16[64,3328]{1,0:T(8,128)(2,1)S(1)} %bitcast.15), channel_id=1, source_target_pairs={{16,0},{24,8},{0,16},{8,24},{17,1},{25,9},{1,17},{9,25},{18,2},{26... | collective-permute-start | bytes 1277960 | tf_op jit(solution)/shard_map/ppermute | solution.py:479
  34.4 1.1 collective-permute-start.2
  35.5 7.2 %collective-permute-done.4.refs_3_ = bf16[64,3328]{1,0:T(8,128)(2,1)S(1)} collective-permute-done((bf16[64,3328]{1,0:T(8,128)(2,1)S(1)}, bf16[64,3328]{1,0:T(8,128)(2,1)S(1)}, u32[]{:S(2)}, u32[]{:S(2)}) %collective-permute-start.4) | collective-permute-done | bytes 426016 | tf_op jit(solution)/shard_map/ppermute | solution.py:479
  42.7 10.2 %collective-permute-done.3.refs_2_ = bf16[64,3328]{1,0:T(8,128)(2,1)S(1)} collective-permute-done((bf16[64,3328]{1,0:T(8,128)(2,1)S(1)}, bf16[64,3328]{1,0:T(8,128)(2,1)S(1)}, u32[]{:S(2)}, u32[]{:S(2)}) %collective-permute-start.3) | collective-permute-done | bytes 426016 | tf_op jit(solution)/shard_map/ppermute | solution.py:479
  52.9 2.0 %shard_map.49 = (f32[256,256]{1,0:T(8,128)S(1)}, f32[256,256]{1,0:T(8,128)S(1)}) custom-call(s32[4]{0:T(128)S(1)} %pad_add_fusion.at_ref.refs_0_, bf16[256,3328]{1,0:T(8,128)(2,1)S(1)} %get-tuple-element.52.mine_ref, bf16[256,3328]{1,0:T(8,128)(2,1)S(1)} %collective-permute-done.1.other_ref, bf16[64,3328]{1,0:T(8,128)(2,1)S(1)} %bitcast.17, ...), custom_call_target="tpu_custom_call" | custom-call | flops 872415232 | bytes 5111808 | tf_op jit(solution)/shard_map/pallas_call | solution.py:163
  55.0 1.5 collective-permute-start.5
  56.5 1.2 collective-permute-done.5.two_ref
  57.7 1.3 collective-permute-start.8
  59.0 2.4 %collective-permute-start.7 = (f32[256,256]{1,0:T(8,128)S(1)}, f32[256,256]{1,0:T(8,128)S(1)}, u32[]{:S(2)}, u32[]{:S(2)}) collective-permute-start(f32[256,256]{1,0:T(8,128)S(1)} %shard_map.50.own_ref), channel_id=1, source_target_pairs={{2,0},{3,1},{0,2},{1,3},{6,4},{7,5},{4,6},{5,7},{10,8},{11,9},{8,1... | collective-permute-start | bytes 786440 | tf_op jit(solution)/shard_map/ppermute | solution.py:479
  61.4 1.2 collective-permute-start.6
  62.6 3.9 %collective-permute-done.8.three_ref = f32[256,256]{1,0:T(8,128)S(1)} collective-permute-done((f32[256,256]{1,0:T(8,128)S(1)}, f32[256,256]{1,0:T(8,128)S(1)}, u32[]{:S(2)}, u32[]{:S(2)}) %collective-permute-start.8) | collective-permute-done | bytes 262176 | tf_op jit(solution)/shard_map/ppermute | solution.py:479
  66.5 6.6 %collective-permute-done.7.two_ref = f32[256,256]{1,0:T(8,128)S(1)} collective-permute-done((f32[256,256]{1,0:T(8,128)S(1)}, f32[256,256]{1,0:T(8,128)S(1)}, u32[]{:S(2)}, u32[]{:S(2)}) %collective-permute-start.7) | collective-permute-done | bytes 262176 | tf_op jit(solution)/shard_map/ppermute | solution.py:479
  73.1 1.0 shard_map.51
  74.1 1.3 collective-permute-start.10
  75.4 1.1 collective-permute-done.9.two_ref
  76.6 0.9 collective-permute-start.13
  77.5 2.1 %collective-permute-start.12 = (f32[32,256]{1,0:T(8,128)S(1)}, f32[32,256]{1,0:T(8,128)S(1)}, u32[]{:S(2)}, u32[]{:S(2)}) collective-permute-start(f32[32,256]{1,0:T(8,128)S(1)} %shard_map.52.own_ref), channel_id=1, source_target_pairs={{16,0},{24,8},{0,16},{8,24},{17,1},{25,9},{1,17},{9,25},{18,2},{26... | collective-permute-start | bytes 98312 | tf_op jit(solution)/shard_map/ppermute | solution.py:479
  79.6 1.4 collective-permute-start.11
  81.0 4.0 %shard_map.57 = (f32[832,256]{1,0:T(8,128)S(1)}, f32[832,256]{1,0:T(8,128)S(1)}, f32[832,256]{1,0:T(8,128)S(1)}, f32[832,256]{1,0:T(8,128)S(1)}) custom-call(s32[4]{0:T(128)S(1)} %pad_add_fusion.at_ref.refs_0_, bf16[256,3328]{1,0:T(8,128)(2,1)S(1)} %get-tuple-element.52.mine_ref, bf16[256,3328]{1,0:T(8,128)(2,1)S(1)} %collective-permute-done.1.other_ref, ...), custom_call_target="tpu_custom_call" | custom-call | flops 2617245696 | bytes 10223616 | tf_op jit(solution)/shard_map/pallas_call | solution.py:293
  85.1 1.1 collective-permute-start.19
  86.3 1.6 collective-permute-start.20
  87.9 11.6 %all_to_all.26.pieces_ref = f32[8,32,256]{2,1,0:T(8,128)S(1)} all-to-all(f32[8,32,256]{2,1,0:T(8,128)S(1)} %shard_map.53), channel_id=1, replica_groups=mesh['z'=8,'y'=4,'c'=2,'x'=4] {'z'}, dimensions={0} | all-to-all | bytes 524288 | tf_op jit(solution)/shard_map/all_to_all | solution.py:495
  99.5 3.7 %collective-permute-start.14 = (f32[32,256]{1,0:T(8,128)S(1)}, f32[32,256]{1,0:T(8,128)S(1)}, u32[]{:S(2)}, u32[]{:S(2)}) collective-permute-start(f32[32,256]{1,0:T(8,128)S(1)} %bitcast.19), channel_id=1, source_target_pairs={{0,4},{4,0},{1,5},{5,1},{2,6},{6,2},{3,7},{7,3},{8,12},{12,8},{9,1... | collective-permute-start | bytes 98312 | tf_op jit(solution)/shard_map/ppermute | solution.py:475
  103.2 0.9 collective-permute-done.14
  104.1 1.1 collective-permute-start.17
  105.1 2.1 %collective-permute-start.16 = (f32[64,256]{1,0:T(8,128)S(1)}, f32[64,256]{1,0:T(8,128)S(1)}, u32[]{:S(2)}, u32[]{:S(2)}) collective-permute-start(f32[64,256]{1,0:T(8,128)S(1)} %pad_maximum_fusion.own_ref), channel_id=1, source_target_pairs={{2,0},{3,1},{0,2},{1,3},{6,4},{7,5},{4,6},{5,7},{10,8},{11,9},{8,1... | collective-permute-start | bytes 196616 | tf_op jit(solution)/shard_map/ppermute | solution.py:479
  107.3 1.4 collective-permute-done.17.last_ref
  108.7 0.8 collective-permute-start.15
  109.5 1.3 collective-permute-done.16.across_ref
  110.8 1.3 collective-permute-done.15.next_ref
  112.1 9.9 %shard_map.55.inverse_ref = f32[256,256]{1,0:T(8,128)S(1)} custom-call(s32[4]{0:T(128)S(1)} %pad_add_fusion.at_ref.refs_0_, f32[64,256]{1,0:T(8,128)S(1)} %pad_maximum_fusion.own_ref, f32[64,256]{1,0:T(8,128)S(1)} %collective-permute-done.15.next_ref, f32[64,256]{1,0:T(8,128)S(1)} %collective-permute-done.16.across_ref, ...), custom_call_target="tpu_custom_call" | custom-call | flops 1000000000 | bytes 1048576 | tf_op jit(solution)/shard_map/pallas_call | solution.py:127
  122.6 1.9 %collective-permute-done.20.refs_3_ = f32[832,256]{1,0:T(8,128)S(1)} collective-permute-done((f32[832,256]{1,0:T(8,128)S(1)}, f32[832,256]{1,0:T(8,128)S(1)}, u32[]{:S(2)}, u32[]{:S(2)}) %collective-permute-start.20) | collective-permute-done | bytes 852000 | tf_op jit(solution)/shard_map/ppermute | solution.py:479
  124.5 0.9 shard_map.58
  125.5 15.2 %all_to_all.27.pieces_ref = bf16[8,104,256]{2,1,0:T(8,128)(2,1)S(1)} all-to-all(bf16[8,104,256]{2,1,0:T(8,128)(2,1)S(1)} %bitcast.18), channel_id=1, replica_groups=mesh['z'=8,'y'=4,'c'=2,'x'=4] {'z'}, dimensions={0} | all-to-all | bytes 851968 | tf_op jit(solution)/shard_map/all_to_all | solution.py:495
  140.8 15.5 %all_to_all.28 = bf16[8,104,256]{2,1,0:T(8,128)(2,1)S(1)} all-to-all(bf16[8,104,256]{2,1,0:T(8,128)(2,1)S(1)} %shard_map.59), channel_id=1, replica_groups=mesh['z'=8,'y'=4,'c'=2,'x'=4] {'z'}, dimensions={0} | all-to-all | bytes 851968 | tf_op jit(solution)/shard_map/all_to_all | solution.py:495
  156.3 4.3 %collective-permute-start.23 = (bf16[832,256]{1,0:T(8,128)(2,1)S(1)}, bf16[832,256]{1,0:T(8,128)(2,1)S(1)}, u32[]{:S(2)}, u32[]{:S(2)}) collective-permute-start(bf16[832,256]{1,0:T(8,128)(2,1)S(1)} %bitcast.8), channel_id=1, source_target_pairs={{0,4},{4,0},{1,5},{5,1},{2,6},{6,2},{3,7},{7,3},{8,12},{12,8},{9,1... | collective-permute-start | bytes 1277960 | tf_op jit(solution)/shard_map/ppermute | solution.py:475
  160.6 3.5 %collective-permute-start.22 = (bf16[832,256]{1,0:T(8,128)(2,1)S(1)}, bf16[832,256]{1,0:T(8,128)(2,1)S(1)}, u32[]{:S(2)}, u32[]{:S(2)}) collective-permute-start(bf16[832,256]{1,0:T(8,128)(2,1)S(1)} %bitcast.9), channel_id=1, source_target_pairs={{24,0},{0,8},{8,16},{16,24},{25,1},{1,9},{9,17},{17,25},{26,2},{2,... | collective-permute-start | bytes 1277960 | tf_op jit(solution)/shard_map/ppermute | solution.py:479
  164.8 12.9 %all_to_all.29.refs_3_ = f32[32,1,256]{2,1,0:T(1,128)S(1)} all-to-all(f32[32,1,256]{2,1,0:T(1,128)S(1)} %shard_map.60), channel_id=1, replica_groups=mesh['z'=8,'y'=4,'c'=2,'x'=4] {'y','c','x'}, dimensions={0} | all-to-all | bytes 65536 | tf_op jit(solution)/shard_map/all_to_all | solution.py:495
  178.7 2.3 %collective-permute-start.27 = (bf16[416,256]{1,0:T(8,128)(2,1)S(1)}, bf16[416,256]{1,0:T(8,128)(2,1)S(1)}, u32[]{:S(2)}, u32[]{:S(2)}) collective-permute-start(bf16[416,256]{1,0:T(8,128)(2,1)S(1)} %slice.7), channel_id=1, source_target_pairs={{8,0},{16,8},{24,16},{0,24},{9,1},{17,9},{25,17},{1,25},{10,2},{18... | collective-permute-start | bytes 638984 | tf_op jit(solution)/shard_map/ppermute | solution.py:479
  181.5 6.2 %shard_map.61 = (bf16[256,6656]{1,0:T(8,128)(2,1)}, bf16[256,6656]{1,0:T(8,128)(2,1)}, f32[4,6656]{1,0:T(4,128)}) custom-call(s32[4]{0:T(128)S(1)} %pad_add_fusion.at_ref.refs_0_, bf16[256,6656]{1,0:T(8,128)(2,1)S(1)} %copy-done, f32[256,256]{1,0:T(8,128)S(1)} %shard_map.56.refs_2_, f32[32,1,256]{2,1,0:T(1,128)S(1)} %all_to_all.29.refs_3_, ...), custom_call_target="tpu_custom_call" | custom-call | flops 1308622848 | bytes 10223616 | tf_op jit(solution)/shard_map/pallas_call | solution.py:439
  187.7 1.0 collective-permute-start.28
  188.9 1.0 collective-permute-done.28.refs_12_
  190.2 3.2 %shard_map.62 = (bf16[256,6656]{1,0:T(8,128)(2,1)}, bf16[256,6656]{1,0:T(8,128)(2,1)}, f32[4,6656]{1,0:T(4,128)}) custom-call(s32[4]{0:T(128)S(1)} %pad_add_fusion.at_ref.refs_0_, bf16[256,6656]{1,0:T(8,128)(2,1)S(1)} %copy-done, f32[256,256]{1,0:T(8,128)S(1)} %shard_map.56.refs_2_, ...), custom_call_target="tpu_custom_call", output_to_operand_aliasing={{0}: (14, {}), {1}: (15, {}), {2}: (16, {})} | custom-call | flops 436207616 | bytes 3407872 | tf_op jit(solution)/shard_map/pallas_call | solution.py:457
  (43 shorter events, 5.0 us)
Async XLA Ops:
  1.6 4.2 %collective-permute-start = (bf16[4,3328]{1,0:T(4,128)(2,1)S(1)}, bf16[4,3328]{1,0:T(4,128)(2,1)S(1)}, u32[]{:S(2)}, u32[]{:S(2)}) collective-permute-start(bf16[4,3328]{1,0:T(4,128)(2,1)S(1)} %constant_dynamic-slice_fusion.2), channel_id=1, source_target_pairs={{0,4},{4,0},{1,5},{5,1},{2,6},{6,2},{3,7},{7,3},{8,12},{12,8},{9,1... | collective-permute-start | bytes 79880 | tf_op jit(solution)/shard_map/ppermute | solution.py:475
  8.0 44.9 %collective-permute-start.1 = (bf16[256,3328]{1,0:T(8,128)(2,1)S(1)}, bf16[256,3328]{1,0:T(8,128)(2,1)S(1)}, u32[]{:S(2)}, u32[]{:S(2)}) collective-permute-start(bf16[256,3328]{1,0:T(8,128)(2,1)S(1)} %get-tuple-element.51), channel_id=1, source_target_pairs={{0,4},{4,0},{1,5},{5,1},{2,6},{6,2},{3,7},{7,3},{8,12},{12,8},{9,1... | collective-permute-start | bytes 5111816 | tf_op jit(solution)/shard_map/ppermute | solution.py:475
  30.5 12.1 %collective-permute-start.4 = (bf16[64,3328]{1,0:T(8,128)(2,1)S(1)}, bf16[64,3328]{1,0:T(8,128)(2,1)S(1)}, u32[]{:S(2)}, u32[]{:S(2)}) collective-permute-start(bf16[64,3328]{1,0:T(8,128)(2,1)S(1)} %bitcast.14), channel_id=1, source_target_pairs={{24,0},{0,8},{8,16},{16,24},{25,1},{1,9},{9,17},{17,25},{26,2},{2,... | collective-permute-start | bytes 1277960 | tf_op jit(solution)/shard_map/ppermute | solution.py:479
  31.8 21.1 %collective-permute-start.3 = (bf16[64,3328]{1,0:T(8,128)(2,1)S(1)}, bf16[64,3328]{1,0:T(8,128)(2,1)S(1)}, u32[]{:S(2)}, u32[]{:S(2)}) collective-permute-start(bf16[64,3328]{1,0:T(8,128)(2,1)S(1)} %bitcast.15), channel_id=1, source_target_pairs={{16,0},{24,8},{0,16},{8,24},{17,1},{25,9},{1,17},{9,25},{18,2},{26... | collective-permute-start | bytes 1277960 | tf_op jit(solution)/shard_map/ppermute | solution.py:479
  34.4 18.5 %collective-permute-start.2 = (bf16[64,3328]{1,0:T(8,128)(2,1)S(1)}, bf16[64,3328]{1,0:T(8,128)(2,1)S(1)}, u32[]{:S(2)}, u32[]{:S(2)}) collective-permute-start(bf16[64,3328]{1,0:T(8,128)(2,1)S(1)} %bitcast.16), channel_id=1, source_target_pairs={{8,0},{16,8},{24,16},{0,24},{9,1},{17,9},{25,17},{1,25},{10,2},{18... | collective-permute-start | bytes 1277960 | tf_op jit(solution)/shard_map/ppermute | solution.py:479
  55.0 2.6 %collective-permute-start.5 = (f32[256,256]{1,0:T(8,128)S(1)}, f32[256,256]{1,0:T(8,128)S(1)}, u32[]{:S(2)}, u32[]{:S(2)}) collective-permute-start(f32[256,256]{1,0:T(8,128)S(1)} %get-tuple-element.31), channel_id=1, source_target_pairs={{0,4},{4,0},{1,5},{5,1},{2,6},{6,2},{3,7},{7,3},{8,12},{12,8},{9,1... | collective-permute-start | bytes 786440 | tf_op jit(solution)/shard_map/ppermute | solution.py:475
  57.7 8.8 %collective-permute-start.8 = (f32[256,256]{1,0:T(8,128)S(1)}, f32[256,256]{1,0:T(8,128)S(1)}, u32[]{:S(2)}, u32[]{:S(2)}) collective-permute-start(f32[256,256]{1,0:T(8,128)S(1)} %shard_map.50.own_ref), channel_id=1, source_target_pairs={{3,0},{0,1},{1,2},{2,3},{7,4},{4,5},{5,6},{6,7},{11,8},{8,9},{9,10... | collective-permute-start | bytes 786440 | tf_op jit(solution)/shard_map/ppermute | solution.py:479
  59.0 14.1 %collective-permute-start.7 = (f32[256,256]{1,0:T(8,128)S(1)}, f32[256,256]{1,0:T(8,128)S(1)}, u32[]{:S(2)}, u32[]{:S(2)}) collective-permute-start(f32[256,256]{1,0:T(8,128)S(1)} %shard_map.50.own_ref), channel_id=1, source_target_pairs={{2,0},{3,1},{0,2},{1,3},{6,4},{7,5},{4,6},{5,7},{10,8},{11,9},{8,1... | collective-permute-start | bytes 786440 | tf_op jit(solution)/shard_map/ppermute | solution.py:479
  61.4 11.7 %collective-permute-start.6 = (f32[256,256]{1,0:T(8,128)S(1)}, f32[256,256]{1,0:T(8,128)S(1)}, u32[]{:S(2)}, u32[]{:S(2)}) collective-permute-start(f32[256,256]{1,0:T(8,128)S(1)} %shard_map.50.own_ref), channel_id=1, source_target_pairs={{1,0},{2,1},{3,2},{0,3},{5,4},{6,5},{7,6},{4,7},{9,8},{10,9},{11,1... | collective-permute-start | bytes 786440 | tf_op jit(solution)/shard_map/ppermute | solution.py:479
  74.1 2.5 %collective-permute-start.10 = (f32[256,256]{1,0:T(8,128)S(1)}, f32[256,256]{1,0:T(8,128)S(1)}, u32[]{:S(2)}, u32[]{:S(2)}) collective-permute-start(f32[256,256]{1,0:T(8,128)S(1)} %get-tuple-element.34.refs_0_.left_mine_ref), channel_id=1, source_target_pairs={{0,4},{4,0},{1,5},{5,1},{2,6},{6,2},{3,7},{7,3},{8,12},{12,8},{9,1... | collective-permute-start | bytes 786440 | tf_op jit(solution)/shard_map/ppermute | solution.py:475
  75.3 1.2 collective-permute-start.9
  76.6 9.7 %collective-permute-start.13 = (f32[32,256]{1,0:T(8,128)S(1)}, f32[32,256]{1,0:T(8,128)S(1)}, u32[]{:S(2)}, u32[]{:S(2)}) collective-permute-start(f32[32,256]{1,0:T(8,128)S(1)} %shard_map.52.own_ref), channel_id=1, source_target_pairs={{24,0},{0,8},{8,16},{16,24},{25,1},{1,9},{9,17},{17,25},{26,2},{2,... | collective-permute-start | bytes 98312 | tf_op jit(solution)/shard_map/ppermute | solution.py:479
  77.5 10.3 %collective-permute-start.12 = (f32[32,256]{1,0:T(8,128)S(1)}, f32[32,256]{1,0:T(8,128)S(1)}, u32[]{:S(2)}, u32[]{:S(2)}) collective-permute-start(f32[32,256]{1,0:T(8,128)S(1)} %shard_map.52.own_ref), channel_id=1, source_target_pairs={{16,0},{24,8},{0,16},{8,24},{17,1},{25,9},{1,17},{9,25},{18,2},{26... | collective-permute-start | bytes 98312 | tf_op jit(solution)/shard_map/ppermute | solution.py:479
  79.6 8.2 %collective-permute-start.11 = (f32[32,256]{1,0:T(8,128)S(1)}, f32[32,256]{1,0:T(8,128)S(1)}, u32[]{:S(2)}, u32[]{:S(2)}) collective-permute-start(f32[32,256]{1,0:T(8,128)S(1)} %shard_map.52.own_ref), channel_id=1, source_target_pairs={{8,0},{16,8},{24,16},{0,24},{9,1},{17,9},{25,17},{1,25},{10,2},{18... | collective-permute-start | bytes 98312 | tf_op jit(solution)/shard_map/ppermute | solution.py:479
  85.0 37.1 %collective-permute-start.18 = (f32[832,256]{1,0:T(8,128)S(1)}, f32[832,256]{1,0:T(8,128)S(1)}, u32[]{:S(2)}, u32[]{:S(2)}) collective-permute-start(f32[832,256]{1,0:T(8,128)S(1)} %get-tuple-element.38), channel_id=1, source_target_pairs={{24,0},{0,8},{8,16},{16,24},{25,1},{1,9},{9,17},{17,25},{26,2},{2,... | collective-permute-start | bytes 2555912 | tf_op jit(solution)/shard_map/ppermute | solution.py:479
  85.1 37.4 %collective-permute-start.19 = (f32[832,256]{1,0:T(8,128)S(1)}, f32[832,256]{1,0:T(8,128)S(1)}, u32[]{:S(2)}, u32[]{:S(2)}) collective-permute-start(f32[832,256]{1,0:T(8,128)S(1)} %get-tuple-element.39), channel_id=1, source_target_pairs={{16,0},{24,8},{0,16},{8,24},{17,1},{25,9},{1,17},{9,25},{18,2},{26... | collective-permute-start | bytes 2555912 | tf_op jit(solution)/shard_map/ppermute | solution.py:479
  86.3 38.3 %collective-permute-start.20 = (f32[832,256]{1,0:T(8,128)S(1)}, f32[832,256]{1,0:T(8,128)S(1)}, u32[]{:S(2)}, u32[]{:S(2)}) collective-permute-start(f32[832,256]{1,0:T(8,128)S(1)} %get-tuple-element.40), channel_id=1, source_target_pairs={{8,0},{16,8},{24,16},{0,24},{9,1},{17,9},{25,17},{1,25},{10,2},{18... | collective-permute-start | bytes 2555912 | tf_op jit(solution)/shard_map/ppermute | solution.py:479
  99.5 4.6 %collective-permute-start.14 = (f32[32,256]{1,0:T(8,128)S(1)}, f32[32,256]{1,0:T(8,128)S(1)}, u32[]{:S(2)}, u32[]{:S(2)}) collective-permute-start(f32[32,256]{1,0:T(8,128)S(1)} %bitcast.19), channel_id=1, source_target_pairs={{0,4},{4,0},{1,5},{5,1},{2,6},{6,2},{3,7},{7,3},{8,12},{12,8},{9,1... | collective-permute-start | bytes 98312 | tf_op jit(solution)/shard_map/ppermute | solution.py:475
  104.1 4.6 %collective-permute-start.17 = (f32[64,256]{1,0:T(8,128)S(1)}, f32[64,256]{1,0:T(8,128)S(1)}, u32[]{:S(2)}, u32[]{:S(2)}) collective-permute-start(f32[64,256]{1,0:T(8,128)S(1)} %pad_maximum_fusion.own_ref), channel_id=1, source_target_pairs={{3,0},{0,1},{1,2},{2,3},{7,4},{4,5},{5,6},{6,7},{11,8},{8,9},{9,10... | collective-permute-start | bytes 196616 | tf_op jit(solution)/shard_map/ppermute | solution.py:479
  105.1 5.6 %collective-permute-start.16 = (f32[64,256]{1,0:T(8,128)S(1)}, f32[64,256]{1,0:T(8,128)S(1)}, u32[]{:S(2)}, u32[]{:S(2)}) collective-permute-start(f32[64,256]{1,0:T(8,128)S(1)} %pad_maximum_fusion.own_ref), channel_id=1, source_target_pairs={{2,0},{3,1},{0,2},{1,3},{6,4},{7,5},{4,6},{5,7},{10,8},{11,9},{8,1... | collective-permute-start | bytes 196616 | tf_op jit(solution)/shard_map/ppermute | solution.py:479
  108.7 3.4 %collective-permute-start.15 = (f32[64,256]{1,0:T(8,128)S(1)}, f32[64,256]{1,0:T(8,128)S(1)}, u32[]{:S(2)}, u32[]{:S(2)}) collective-permute-start(f32[64,256]{1,0:T(8,128)S(1)} %pad_maximum_fusion.own_ref), channel_id=1, source_target_pairs={{1,0},{2,1},{3,2},{0,3},{5,4},{6,5},{7,6},{4,7},{9,8},{10,9},{11,1... | collective-permute-start | bytes 196616 | tf_op jit(solution)/shard_map/ppermute | solution.py:479
  124.5 57.0 %copy-start = (bf16[256,6656]{1,0:T(8,128)(2,1)S(1)}, bf16[256,6656]{1,0:T(8,128)(2,1)}, u32[]{:S(2)}) copy-start(bf16[256,6656]{1,0:T(8,128)(2,1)} %refs_1_.3) | copy-start | bytes 10223620
  156.3 21.4 %collective-permute-start.23 = (bf16[832,256]{1,0:T(8,128)(2,1)S(1)}, bf16[832,256]{1,0:T(8,128)(2,1)S(1)}, u32[]{:S(2)}, u32[]{:S(2)}) collective-permute-start(bf16[832,256]{1,0:T(8,128)(2,1)S(1)} %bitcast.8), channel_id=1, source_target_pairs={{0,4},{4,0},{1,5},{5,1},{2,6},{6,2},{3,7},{7,3},{8,12},{12,8},{9,1... | collective-permute-start | bytes 1277960 | tf_op jit(solution)/shard_map/ppermute | solution.py:475
  160.6 17.1 %collective-permute-start.22 = (bf16[832,256]{1,0:T(8,128)(2,1)S(1)}, bf16[832,256]{1,0:T(8,128)(2,1)S(1)}, u32[]{:S(2)}, u32[]{:S(2)}) collective-permute-start(bf16[832,256]{1,0:T(8,128)(2,1)S(1)} %bitcast.9), channel_id=1, source_target_pairs={{24,0},{0,8},{8,16},{16,24},{25,1},{1,9},{9,17},{17,25},{26,2},{2,... | collective-permute-start | bytes 1277960 | tf_op jit(solution)/shard_map/ppermute | solution.py:479
  164.0 13.6 %collective-permute-start.21 = (bf16[832,256]{1,0:T(8,128)(2,1)S(1)}, bf16[832,256]{1,0:T(8,128)(2,1)S(1)}, u32[]{:S(2)}, u32[]{:S(2)}) collective-permute-start(bf16[832,256]{1,0:T(8,128)(2,1)S(1)} %bitcast.10), channel_id=1, source_target_pairs={{8,0},{16,8},{24,16},{0,24},{9,1},{17,9},{25,17},{1,25},{10,2},{18... | collective-permute-start | bytes 1277960 | tf_op jit(solution)/shard_map/ppermute | solution.py:479
  177.7 3.8 %collective-permute-start.24 = (bf16[832,256]{1,0:T(8,128)(2,1)S(1)}, bf16[832,256]{1,0:T(8,128)(2,1)S(1)}, u32[]{:S(2)}, u32[]{:S(2)}) collective-permute-start(bf16[832,256]{1,0:T(8,128)(2,1)S(1)} %collective-permute-done.21.refs_5_), channel_id=1, source_target_pairs={{0,4},{4,0},{1,5},{5,1},{2,6},{6,2},{3,7},{7,3},{8,12},{12,8},{9,1... | collective-permute-start | bytes 1277960 | tf_op jit(solution)/shard_map/ppermute | solution.py:475
  178.1 3.3 %collective-permute-start.25 = (bf16[832,256]{1,0:T(8,128)(2,1)S(1)}, bf16[832,256]{1,0:T(8,128)(2,1)S(1)}, u32[]{:S(2)}, u32[]{:S(2)}) collective-permute-start(bf16[832,256]{1,0:T(8,128)(2,1)S(1)} %collective-permute-done.22.refs_6_), channel_id=1, source_target_pairs={{0,4},{4,0},{1,5},{5,1},{2,6},{6,2},{3,7},{7,3},{8,12},{12,8},{9,1... | collective-permute-start | bytes 1277960 | tf_op jit(solution)/shard_map/ppermute | solution.py:475
  178.3 9.4 %collective-permute-start.26 = (bf16[416,256]{1,0:T(8,128)(2,1)S(1)}, bf16[416,256]{1,0:T(8,128)(2,1)S(1)}, u32[]{:S(2)}, u32[]{:S(2)}) collective-permute-start(bf16[416,256]{1,0:T(8,128)(2,1)S(1)} %slice.6), channel_id=1, source_target_pairs={{24,0},{0,8},{8,16},{16,24},{25,1},{1,9},{9,17},{17,25},{26,2},{2,... | collective-permute-start | bytes 638984 | tf_op jit(solution)/shard_map/ppermute | solution.py:479
  178.7 9.0 %collective-permute-start.27 = (bf16[416,256]{1,0:T(8,128)(2,1)S(1)}, bf16[416,256]{1,0:T(8,128)(2,1)S(1)}, u32[]{:S(2)}, u32[]{:S(2)}) collective-permute-start(bf16[416,256]{1,0:T(8,128)(2,1)S(1)} %slice.7), channel_id=1, source_target_pairs={{8,0},{16,8},{24,16},{0,24},{9,1},{17,9},{25,17},{1,25},{10,2},{18... | collective-permute-start | bytes 638984 | tf_op jit(solution)/shard_map/ppermute | solution.py:479
  187.7 2.1 %collective-permute-start.28 = (bf16[416,256]{1,0:T(8,128)(2,1)S(1)}, bf16[416,256]{1,0:T(8,128)(2,1)S(1)}, u32[]{:S(2)}, u32[]{:S(2)}) collective-permute-start(bf16[416,256]{1,0:T(8,128)(2,1)S(1)} %collective-permute-done.26.refs_7_), channel_id=1, source_target_pairs={{0,4},{4,0},{1,5},{5,1},{2,6},{6,2},{3,7},{7,3},{8,12},{12,8},{9,1... | collective-permute-start | bytes 638984 | tf_op jit(solution)/shard_map/ppermute | solution.py:475
  188.8 1.5 collective-permute-start.29

commit v5 on v4

--- a/solution.py
+++ b/solution.py
@@ -236,8 +236,11 @@
 
 
 def gram_kernel(at_ref, own_ref, one_ref, two_ref, three_ref, projected_ref, keep_ref, send_ref, gram_ref):
-    projected = (own_ref[...] + two_ref[...]) + (one_ref[...] + three_ref[...])
-    projected_ref[...] = projected
+    for by, ref in enumerate((own_ref, one_ref, two_ref, three_ref)):
+        size = ref.shape[0]
+        start = pl.multiple_of(ahead(at_ref[AT_X], by, NX) * size, size)
+        projected_ref[pl.ds(start, size), :] = ref[...]
+    projected = projected_ref[...]
     gram_ref[...] = lax.dot_general(
         projected, projected, BOTH_FIRST, preferred_element_type=f32, precision=HIGHEST
     )
@@ -248,17 +251,36 @@
 
 
 def gram_rows_of(at, pieces):
-    rows, rank = pieces[0].shape
+    size, rank = pieces[0].shape
     part = jax.ShapeDtypeStruct((rank // (NX * 2), rank), f32)
     return pl.pallas_call(
         gram_kernel,
-        out_shape=[jax.ShapeDtypeStruct((rows, rank), f32), part, part],
+        out_shape=[jax.ShapeDtypeStruct((size * NX, rank), f32), part, part],
         in_specs=[SMEM] + [VMEM] * 4,
         out_specs=[VMEM] * 3,
         scratch_shapes=[pltpu.VMEM((rank, rank), f32)],
         compiler_params=pltpu.CompilerParams(vmem_limit_bytes=8 * MIB),
         cost_estimate=pl.CostEstimate(flops=2**28, bytes_accessed=2**20, transcendentals=0),
     )(at, *pieces)
+
+
+def add_in_blocks(at, one, two):
+    rows, rank = one.shape
+    size = rows // NX
+
+    def kernel(at_ref, one_ref, two_ref, *outs):
+        for by, ref in enumerate(outs):
+            start = pl.multiple_of(ahead(at_ref[AT_X], by, NX) * size, size)
+            ref[...] = one_ref[pl.ds(start, size), :] + two_ref[pl.ds(start, size), :]
+
+    return pl.pallas_call(
+        kernel,
+        out_shape=[jax.ShapeDtypeStruct((size, rank), f32)] * NX,
+        in_specs=[SMEM, VMEM, VMEM],
+        out_specs=[VMEM] * NX,
+        compiler_params=pltpu.CompilerParams(vmem_limit_bytes=8 * MIB),
+        cost_estimate=pl.CostEstimate(flops=2**20, bytes_accessed=2**20, transcendentals=0),
+    )(at, one, two)
 
 
 def cross_kernel(at_ref, mine_ref, other_ref, left_mine_ref, left_other_ref, *refs):
@@ -510,19 +532,22 @@
 
     basis_half = q_basis.astype(bf16)
     basis_own = columns(basis_half, core)
-    basis_other = swap_cores(columns(basis_half, 1 - core))
+    sent = columns(basis_half, 1 - core)
+    later, sent, at = lax.optimization_barrier((momentum, sent, at))
+    mine, theirs = columns(later, core), columns(later, 1 - core)
+    basis_other = swap_cores(sent)
+    mine, theirs, basis_other = lax.optimization_barrier((mine, theirs, basis_other))
+    other = swap_cores(theirs)
     basis_chip = jnp.concatenate(
         [jnp.where(core == 0, basis_own, basis_other), jnp.where(core == 0, basis_other, basis_own)]
     )
-    later, basis_chip, at = lax.optimization_barrier((momentum, basis_chip, at))
-    mine = columns(later, core)
-    other = swap_cores(columns(later, 1 - core))
-
     basis = exchange(jnp.broadcast_to(basis_chip[None], (NZ,) + basis_chip.shape), "z")
     basis = basis.reshape(rank // NY, half)
     proj_mine, proj_other = project(at, mine, other, all_of_four(basis, "y"))
-    proj_chip = add(proj_mine, swap_cores(proj_other))
-    projected, gram_keep, gram_send = gram_rows_of(at, all_of_four(proj_chip, "x"))
+    blocks = add_in_blocks(at, proj_mine, swap_cores(proj_other))
+    block = [blocks[0]] + [from_ahead(blocks[by], "x", NX - by) for by in (1, 2, 3)]
+    block = sum_four_copies(block, 1)[0]
+    projected, gram_keep, gram_send = gram_rows_of(at, all_of_four(block, "x"))
 
     gram_rows = add(gram_keep, swap_cores(gram_send))
     gram_rows, proj_swapped = lax.optimization_barrier((gram_rows, swap_cores(projected)))

time: 194 us -> 191 us (0.985)
  waiting for transfers between devices: 39.8 us -> 34.5 us
  starting transfers between devices: 44.4 us -> 49.1 us
  blocking collectives: 77.2 us -> 74.6 us
    ppermute x19 -> x22, waiting for transfers between devices: 34.5 us -> 30 us  [from_ahead(): lax.ppermute(block, axis, [((i + by) % parts, i) for i in range(parts)])]
    ppermute x11, starting transfers between devices: 16.4 us -> 19 us  [swap_cores(): return lax.ppermute(block, 'c', [(0, 1), (1, 0)])]
    all_to_all x5, blocking collectives: 77.2 us -> 74.6 us  [exchange(): return lax.all_to_all(pieces, axes, 0, 0)]
    ppermute x19 -> x22, starting transfers between devices: 28 us -> 30 us  [from_ahead(): lax.ppermute(block, axis, [((i + by) % parts, i) for i in range(parts)])]
  transfers between devices with their start and end apart: 30 -> 33, of which waited for: 15 -> 18; matrix products, arithmetic and copies ran while one was open for 0% -> 1% of each run, Pallas kernels for 11% -> 11%
where the time goes in v5:
time: 191 us
  blocking collectives  74.6 us (39%)
  starting transfers between devices  49.1 us (26%)
  waiting for transfers between devices  34.5 us (18%)
  Pallas kernels  28.5 us (15%)
  local copies, waits for them, and re-layouts  2.27 us (1%)
    all_to_all x5, blocking collectives, exchange(): return lax.all_to_all(pieces, axes, 0, 0)  74.6 us
    ppermute x22, waiting for transfers between devices, from_ahead(): lax.ppermute(block, axis, [((i + by) % parts, i) for i in range(parts)])  30 us
    ppermute x22, starting transfers between devices, from_ahead(): lax.ppermute(block, axis, [((i + by) % parts, i) for i in range(parts)])  30 us
    ppermute x11, starting transfers between devices, swap_cores(): return lax.ppermute(block, 'c', [(0, 1), (1, 0)])  19 us
    pallas_call x1, Pallas kernels, inverse_factor(): pl.pallas_call(inverse_factor_kernel, out_shape=jax.ShapeDtypeStruct((ran...  9.93 us
    pallas_call x1, Pallas kernels, finish(): pl.pallas_call(lambda *refs: first_kernel(scaling, *refs), out_shape=outs...  6.2 us
    ppermute x11, waiting for transfers between devices, swap_cores(): return lax.ppermute(block, 'c', [(0, 1), (1, 0)])  4.51 us
    pallas_call x1, Pallas kernels, cross(): pl.pallas_call(cross_kernel, out_shape=[jax.ShapeDtypeStruct((cols // NY,...  3.98 us
  transfers between devices with their start and end apart: 33, of which 18 were waited for; matrix products, arithmetic and copies ran while one was open for 1% of the time, Pallas kernels for 11%

profile of v5, /device:TPU:1, one launch (start us, length us, event | category | flops | bytes accessed | tf_op | source)
XLA Modules:
  0.0 191.1 jit_solution(10044226978470629236)
XLA Ops:
  0.6 0.9 convert_element_type.3
  1.7 3.3 %collective-permute-start = (bf16[4,3328]{1,0:T(4,128)(2,1)S(1)}, bf16[4,3328]{1,0:T(4,128)(2,1)S(1)}, u32[]{:S(2)}, u32[]{:S(2)}) collective-permute-start(bf16[4,3328]{1,0:T(4,128)(2,1)S(1)} %constant_dynamic-slice_fusion.2), channel_id=1, source_target_pairs={{0,4},{4,0},{1,5},{5,1},{2,6},{6,2},{3,7},{7,3},{8,12},{12,8},{9,1... | collective-permute-start | bytes 79880 | tf_op jit(solution)/shard_map/ppermute | solution.py:497
  4.9 2.2 %constant_dynamic-slice_fusion = (bf16[256,3328]{1,0:T(8,128)(2,1)S(1)}, bf16[256,3328]{1,0:T(8,128)(2,1)S(1)}) fusion(bf16[256,6656]{1,0:T(8,128)(2,1)} %refs_1_.3, s32[]{:T(128)S(6)} %select_n.20, s32[]{:T(128)S(6)} %select_n.21), kind=kLoop, calls=%fused_computation.4 | loop fusion | bytes 6815752 | tf_op jit(solution)/shard_map/dynamic_slice | solution.py:531
  7.4 20.6 %all_to_all.25 = bf16[8,8,3328]{2,1,0:T(8,128)(2,1)S(1)} all-to-all(bf16[8,8,3328]{2,1,0:T(8,128)(2,1)S(1)} %broadcast_in_dim.2), channel_id=1, replica_groups=mesh['z'=8,'y'=4,'c'=2,'x'=4] {'z'}, dimensions={0} | all-to-all | bytes 851968 | tf_op jit(solution)/shard_map/all_to_all | solution.py:517
  28.0 1.3 collective-permute-start.4
  29.3 2.6 %collective-permute-start.3 = (bf16[64,3328]{1,0:T(8,128)(2,1)S(1)}, bf16[64,3328]{1,0:T(8,128)(2,1)S(1)}, u32[]{:S(2)}, u32[]{:S(2)}) collective-permute-start(bf16[64,3328]{1,0:T(8,128)(2,1)S(1)} %bitcast.16), channel_id=1, source_target_pairs={{16,0},{24,8},{0,16},{8,24},{17,1},{25,9},{1,17},{9,25},{18,2},{26... | collective-permute-start | bytes 1277960 | tf_op jit(solution)/shard_map/ppermute | solution.py:501
  31.9 1.1 collective-permute-start.2
  33.0 5.7 %collective-permute-done.4.refs_3_ = bf16[64,3328]{1,0:T(8,128)(2,1)S(1)} collective-permute-done((bf16[64,3328]{1,0:T(8,128)(2,1)S(1)}, bf16[64,3328]{1,0:T(8,128)(2,1)S(1)}, u32[]{:S(2)}, u32[]{:S(2)}) %collective-permute-start.4) | collective-permute-done | bytes 426016 | tf_op jit(solution)/shard_map/ppermute | solution.py:501
  38.6 10.2 %collective-permute-done.3.refs_2_ = bf16[64,3328]{1,0:T(8,128)(2,1)S(1)} collective-permute-done((bf16[64,3328]{1,0:T(8,128)(2,1)S(1)}, bf16[64,3328]{1,0:T(8,128)(2,1)S(1)}, u32[]{:S(2)}, u32[]{:S(2)}) %collective-permute-start.3) | collective-permute-done | bytes 426016 | tf_op jit(solution)/shard_map/ppermute | solution.py:501
  49.7 2.0 %shard_map.49 = (f32[256,256]{1,0:T(8,128)S(1)}, f32[256,256]{1,0:T(8,128)S(1)}) custom-call(s32[4]{0:T(128)S(1)} %pad_add_fusion.at_ref.refs_0_, bf16[256,3328]{1,0:T(8,128)(2,1)S(1)} %get-tuple-element.37.mine_ref, bf16[256,3328]{1,0:T(8,128)(2,1)S(1)} %collective-permute-done.1.other_ref, bf16[64,3328]{1,0:T(8,128)(2,1)S(1)} %bitcast.18, ...), custom_call_target="tpu_custom_call" | custom-call | flops 872415232 | bytes 5111808 | tf_op jit(solution)/shard_map/pallas_call | solution.py:163
  51.7 2.2 %collective-permute-start.5 = (f32[256,256]{1,0:T(8,128)S(1)}, f32[256,256]{1,0:T(8,128)S(1)}, u32[]{:S(2)}, u32[]{:S(2)}) collective-permute-start(f32[256,256]{1,0:T(8,128)S(1)} %get-tuple-element.41), channel_id=1, source_target_pairs={{0,4},{4,0},{1,5},{5,1},{2,6},{6,2},{3,7},{7,3},{8,12},{12,8},{9,1... | collective-permute-start | bytes 786440 | tf_op jit(solution)/shard_map/ppermute | solution.py:497
  53.9 1.2 collective-permute-done.5.two_ref
  55.7 1.3 collective-permute-start.6
  56.9 2.5 %collective-permute-start.7 = (f32[64,256]{1,0:T(8,128)S(1)}, f32[64,256]{1,0:T(8,128)S(1)}, u32[]{:S(2)}, u32[]{:S(2)}) collective-permute-start(f32[64,256]{1,0:T(8,128)S(1)} %get-tuple-element.44), channel_id=1, source_target_pairs={{2,0},{3,1},{0,2},{1,3},{6,4},{7,5},{4,6},{5,7},{10,8},{11,9},{8,1... | collective-permute-start | bytes 196616 | tf_op jit(solution)/shard_map/ppermute | solution.py:501
  59.4 1.1 collective-permute-start.8
  60.5 1.8 collective-permute-done.7.two_ref
  62.9 3.2 %collective-permute-start.10 = (f32[64,256]{1,0:T(8,128)S(1)}, f32[64,256]{1,0:T(8,128)S(1)}, u32[]{:S(2)}, u32[]{:S(2)}) collective-permute-start(f32[64,256]{1,0:T(8,128)S(1)} %bitcast.23), channel_id=1, source_target_pairs={{2,0},{3,1},{0,2},{1,3},{6,4},{7,5},{4,6},{5,7},{10,8},{11,9},{8,1... | collective-permute-start | bytes 196616 | tf_op jit(solution)/shard_map/ppermute | solution.py:501
  67.2 1.3 collective-permute-done.10.two_ref
  68.5 1.1 collective-permute-done.9.one_ref
  69.6 1.0 shard_map.52
  70.6 3.6 %collective-permute-start.13 = (f32[256,256]{1,0:T(8,128)S(1)}, f32[256,256]{1,0:T(8,128)S(1)}, u32[]{:S(2)}, u32[]{:S(2)}) collective-permute-start(f32[256,256]{1,0:T(8,128)S(1)} %get-tuple-element.48.refs_0_.left_mine_ref), channel_id=1, source_target_pairs={{0,4},{4,0},{1,5},{5,1},{2,6},{6,2},{3,7},{7,3},{8,12},{12,8},{9,1... | collective-permute-start | bytes 786440 | tf_op jit(solution)/shard_map/ppermute | solution.py:497
  74.3 1.1 collective-permute-done.12.two_ref
  75.4 1.0 collective-permute-start.16
  76.3 2.1 %collective-permute-start.15 = (f32[32,256]{1,0:T(8,128)S(1)}, f32[32,256]{1,0:T(8,128)S(1)}, u32[]{:S(2)}, u32[]{:S(2)}) collective-permute-start(f32[32,256]{1,0:T(8,128)S(1)} %shard_map.53.own_ref), channel_id=1, source_target_pairs={{16,0},{24,8},{0,16},{8,24},{17,1},{25,9},{1,17},{9,25},{18,2},{26... | collective-permute-start | bytes 98312 | tf_op jit(solution)/shard_map/ppermute | solution.py:501
  78.4 1.4 collective-permute-start.14
  79.8 4.0 %shard_map.58 = (f32[832,256]{1,0:T(8,128)S(1)}, f32[832,256]{1,0:T(8,128)S(1)}, f32[832,256]{1,0:T(8,128)S(1)}, f32[832,256]{1,0:T(8,128)S(1)}) custom-call(s32[4]{0:T(128)S(1)} %pad_add_fusion.at_ref.refs_0_, bf16[256,3328]{1,0:T(8,128)(2,1)S(1)} %get-tuple-element.37.mine_ref, bf16[256,3328]{1,0:T(8,128)(2,1)S(1)} %collective-permute-done.1.other_ref, ...), custom_call_target="tpu_custom_call" | custom-call | flops 2617245696 | bytes 10223616 | tf_op jit(solution)/shard_map/pallas_call | solution.py:315
  84.0 1.1 collective-permute-start.22
  85.1 1.6 collective-permute-start.23
  86.7 11.9 %all_to_all.26.pieces_ref = f32[8,32,256]{2,1,0:T(8,128)S(1)} all-to-all(f32[8,32,256]{2,1,0:T(8,128)S(1)} %shard_map.54), channel_id=1, replica_groups=mesh['z'=8,'y'=4,'c'=2,'x'=4] {'z'}, dimensions={0} | all-to-all | bytes 524288 | tf_op jit(solution)/shard_map/all_to_all | solution.py:517
  98.6 3.4 %collective-permute-start.17 = (f32[32,256]{1,0:T(8,128)S(1)}, f32[32,256]{1,0:T(8,128)S(1)}, u32[]{:S(2)}, u32[]{:S(2)}) collective-permute-start(f32[32,256]{1,0:T(8,128)S(1)} %bitcast.20), channel_id=1, source_target_pairs={{0,4},{4,0},{1,5},{5,1},{2,6},{6,2},{3,7},{7,3},{8,12},{12,8},{9,1... | collective-permute-start | bytes 98312 | tf_op jit(solution)/shard_map/ppermute | solution.py:497
  102.9 2.5 %collective-permute-start.19 = (f32[64,256]{1,0:T(8,128)S(1)}, f32[64,256]{1,0:T(8,128)S(1)}, u32[]{:S(2)}, u32[]{:S(2)}) collective-permute-start(f32[64,256]{1,0:T(8,128)S(1)} %pad_maximum_fusion.own_ref), channel_id=1, source_target_pairs={{2,0},{3,1},{0,2},{1,3},{6,4},{7,5},{4,6},{5,7},{10,8},{11,9},{8,1... | collective-permute-start | bytes 196616 | tf_op jit(solution)/shard_map/ppermute | solution.py:501
  105.4 2.6 %collective-permute-done.20.last_ref = f32[64,256]{1,0:T(8,128)S(1)} collective-permute-done((f32[64,256]{1,0:T(8,128)S(1)}, f32[64,256]{1,0:T(8,128)S(1)}, u32[]{:S(2)}, u32[]{:S(2)}) %collective-permute-start.20) | collective-permute-done | bytes 65568 | tf_op jit(solution)/shard_map/ppermute | solution.py:501
  108.6 2.7 %collective-permute-done.18.next_ref = f32[64,256]{1,0:T(8,128)S(1)} collective-permute-done((f32[64,256]{1,0:T(8,128)S(1)}, f32[64,256]{1,0:T(8,128)S(1)}, u32[]{:S(2)}, u32[]{:S(2)}) %collective-permute-start.18) | collective-permute-done | bytes 65568 | tf_op jit(solution)/shard_map/ppermute | solution.py:501
  111.4 9.9 %shard_map.56.inverse_ref = f32[256,256]{1,0:T(8,128)S(1)} custom-call(s32[4]{0:T(128)S(1)} %pad_add_fusion.at_ref.refs_0_, f32[64,256]{1,0:T(8,128)S(1)} %pad_maximum_fusion.own_ref, f32[64,256]{1,0:T(8,128)S(1)} %collective-permute-done.18.next_ref, f32[64,256]{1,0:T(8,128)S(1)} %collective-permute-done.19.across_ref, ...), custom_call_target="tpu_custom_call" | custom-call | flops 1000000000 | bytes 1048576 | tf_op jit(solution)/shard_map/pallas_call | solution.py:127
  121.4 2.0 %collective-permute-done.23.refs_3_ = f32[832,256]{1,0:T(8,128)S(1)} collective-permute-done((f32[832,256]{1,0:T(8,128)S(1)}, f32[832,256]{1,0:T(8,128)S(1)}, u32[]{:S(2)}, u32[]{:S(2)}) %collective-permute-start.23) | collective-permute-done | bytes 852000 | tf_op jit(solution)/shard_map/ppermute | solution.py:501
  123.3 0.9 shard_map.59
  124.3 14.6 %all_to_all.27.pieces_ref = bf16[8,104,256]{2,1,0:T(8,128)(2,1)S(1)} all-to-all(bf16[8,104,256]{2,1,0:T(8,128)(2,1)S(1)} %bitcast.19), channel_id=1, replica_groups=mesh['z'=8,'y'=4,'c'=2,'x'=4] {'z'}, dimensions={0} | all-to-all | bytes 851968 | tf_op jit(solution)/shard_map/all_to_all | solution.py:517
  139.0 15.7 %all_to_all.28 = bf16[8,104,256]{2,1,0:T(8,128)(2,1)S(1)} all-to-all(bf16[8,104,256]{2,1,0:T(8,128)(2,1)S(1)} %shard_map.60), channel_id=1, replica_groups=mesh['z'=8,'y'=4,'c'=2,'x'=4] {'z'}, dimensions={0} | all-to-all | bytes 851968 | tf_op jit(solution)/shard_map/all_to_all | solution.py:517
  154.7 4.6 %collective-permute-start.26 = (bf16[832,256]{1,0:T(8,128)(2,1)S(1)}, bf16[832,256]{1,0:T(8,128)(2,1)S(1)}, u32[]{:S(2)}, u32[]{:S(2)}) collective-permute-start(bf16[832,256]{1,0:T(8,128)(2,1)S(1)} %bitcast.9), channel_id=1, source_target_pairs={{0,4},{4,0},{1,5},{5,1},{2,6},{6,2},{3,7},{7,3},{8,12},{12,8},{9,1... | collective-permute-start | bytes 1277960 | tf_op jit(solution)/shard_map/ppermute | solution.py:497
  159.3 2.7 %collective-permute-start.25 = (bf16[832,256]{1,0:T(8,128)(2,1)S(1)}, bf16[832,256]{1,0:T(8,128)(2,1)S(1)}, u32[]{:S(2)}, u32[]{:S(2)}) collective-permute-start(bf16[832,256]{1,0:T(8,128)(2,1)S(1)} %bitcast.10), channel_id=1, source_target_pairs={{24,0},{0,8},{8,16},{16,24},{25,1},{1,9},{9,17},{17,25},{26,2},{2,... | collective-permute-start | bytes 1277960 | tf_op jit(solution)/shard_map/ppermute | solution.py:501
  161.9 1.3 collective-permute-start.24
  163.3 11.8 %all_to_all.29.refs_3_ = f32[32,1,256]{2,1,0:T(1,128)S(1)} all-to-all(f32[32,1,256]{2,1,0:T(1,128)S(1)} %shard_map.61), channel_id=1, replica_groups=mesh['z'=8,'y'=4,'c'=2,'x'=4] {'y','c','x'}, dimensions={0} | all-to-all | bytes 65536 | tf_op jit(solution)/shard_map/all_to_all | solution.py:517
  175.7 0.9 collective-permute-start.29
  176.7 1.8 collective-permute-start.30
  178.9 6.2 %shard_map.62 = (bf16[256,6656]{1,0:T(8,128)(2,1)}, bf16[256,6656]{1,0:T(8,128)(2,1)}, f32[4,6656]{1,0:T(4,128)}) custom-call(s32[4]{0:T(128)S(1)} %pad_add_fusion.at_ref.refs_0_, bf16[256,6656]{1,0:T(8,128)(2,1)S(1)} %copy-done, f32[256,256]{1,0:T(8,128)S(1)} %shard_map.57.refs_2_, f32[32,1,256]{2,1,0:T(1,128)S(1)} %all_to_all.29.refs_3_, ...), custom_call_target="tpu_custom_call" | custom-call | flops 1308622848 | bytes 10223616 | tf_op jit(solution)/shard_map/pallas_call | solution.py:461
  185.2 1.0 collective-permute-start.31
  186.3 1.0 collective-permute-done.31.refs_12_
  187.7 3.2 %shard_map.63 = (bf16[256,6656]{1,0:T(8,128)(2,1)}, bf16[256,6656]{1,0:T(8,128)(2,1)}, f32[4,6656]{1,0:T(4,128)}) custom-call(s32[4]{0:T(128)S(1)} %pad_add_fusion.at_ref.refs_0_, bf16[256,6656]{1,0:T(8,128)(2,1)S(1)} %copy-done, f32[256,256]{1,0:T(8,128)S(1)} %shard_map.57.refs_2_, ...), custom_call_target="tpu_custom_call", output_to_operand_aliasing={{0}: (14, {}), {1}: (15, {}), {2}: (16, {})} | custom-call | flops 436207616 | bytes 3407872 | tf_op jit(solution)/shard_map/pallas_call | solution.py:479
  (50 shorter events, 7.0 us)
Async XLA Ops:
  1.7 5.5 %collective-permute-start = (bf16[4,3328]{1,0:T(4,128)(2,1)S(1)}, bf16[4,3328]{1,0:T(4,128)(2,1)S(1)}, u32[]{:S(2)}, u32[]{:S(2)}) collective-permute-start(bf16[4,3328]{1,0:T(4,128)(2,1)S(1)} %constant_dynamic-slice_fusion.2), channel_id=1, source_target_pairs={{0,4},{4,0},{1,5},{5,1},{2,6},{6,2},{3,7},{7,3},{8,12},{12,8},{9,1... | collective-permute-start | bytes 79880 | tf_op jit(solution)/shard_map/ppermute | solution.py:497
  7.1 42.5 %collective-permute-start.1 = (bf16[256,3328]{1,0:T(8,128)(2,1)S(1)}, bf16[256,3328]{1,0:T(8,128)(2,1)S(1)}, u32[]{:S(2)}, u32[]{:S(2)}) collective-permute-start(bf16[256,3328]{1,0:T(8,128)(2,1)S(1)} %get-tuple-element.38), channel_id=1, source_target_pairs={{0,4},{4,0},{1,5},{5,1},{2,6},{6,2},{3,7},{7,3},{8,12},{12,8},{9,1... | collective-permute-start | bytes 5111816 | tf_op jit(solution)/shard_map/ppermute | solution.py:497
  28.0 10.7 %collective-permute-start.4 = (bf16[64,3328]{1,0:T(8,128)(2,1)S(1)}, bf16[64,3328]{1,0:T(8,128)(2,1)S(1)}, u32[]{:S(2)}, u32[]{:S(2)}) collective-permute-start(bf16[64,3328]{1,0:T(8,128)(2,1)S(1)} %bitcast.15), channel_id=1, source_target_pairs={{24,0},{0,8},{8,16},{16,24},{25,1},{1,9},{9,17},{17,25},{26,2},{2,... | collective-permute-start | bytes 1277960 | tf_op jit(solution)/shard_map/ppermute | solution.py:501
  29.3 19.6 %collective-permute-start.3 = (bf16[64,3328]{1,0:T(8,128)(2,1)S(1)}, bf16[64,3328]{1,0:T(8,128)(2,1)S(1)}, u32[]{:S(2)}, u32[]{:S(2)}) collective-permute-start(bf16[64,3328]{1,0:T(8,128)(2,1)S(1)} %bitcast.16), channel_id=1, source_target_pairs={{16,0},{24,8},{0,16},{8,24},{17,1},{25,9},{1,17},{9,25},{18,2},{26... | collective-permute-start | bytes 1277960 | tf_op jit(solution)/shard_map/ppermute | solution.py:501
  31.9 17.8 %collective-permute-start.2 = (bf16[64,3328]{1,0:T(8,128)(2,1)S(1)}, bf16[64,3328]{1,0:T(8,128)(2,1)S(1)}, u32[]{:S(2)}, u32[]{:S(2)}) collective-permute-start(bf16[64,3328]{1,0:T(8,128)(2,1)S(1)} %bitcast.17), channel_id=1, source_target_pairs={{8,0},{16,8},{24,16},{0,24},{9,1},{17,9},{25,17},{1,25},{10,2},{18... | collective-permute-start | bytes 1277960 | tf_op jit(solution)/shard_map/ppermute | solution.py:501
  51.7 3.4 %collective-permute-start.5 = (f32[256,256]{1,0:T(8,128)S(1)}, f32[256,256]{1,0:T(8,128)S(1)}, u32[]{:S(2)}, u32[]{:S(2)}) collective-permute-start(f32[256,256]{1,0:T(8,128)S(1)} %get-tuple-element.41), channel_id=1, source_target_pairs={{0,4},{4,0},{1,5},{5,1},{2,6},{6,2},{3,7},{7,3},{8,12},{12,8},{9,1... | collective-permute-start | bytes 786440 | tf_op jit(solution)/shard_map/ppermute | solution.py:497
  55.7 4.9 %collective-permute-start.6 = (f32[64,256]{1,0:T(8,128)S(1)}, f32[64,256]{1,0:T(8,128)S(1)}, u32[]{:S(2)}, u32[]{:S(2)}) collective-permute-start(f32[64,256]{1,0:T(8,128)S(1)} %get-tuple-element.43), channel_id=1, source_target_pairs={{3,0},{0,1},{1,2},{2,3},{7,4},{4,5},{5,6},{6,7},{11,8},{8,9},{9,10... | collective-permute-start | bytes 196616 | tf_op jit(solution)/shard_map/ppermute | solution.py:501
  56.9 5.4 %collective-permute-start.7 = (f32[64,256]{1,0:T(8,128)S(1)}, f32[64,256]{1,0:T(8,128)S(1)}, u32[]{:S(2)}, u32[]{:S(2)}) collective-permute-start(f32[64,256]{1,0:T(8,128)S(1)} %get-tuple-element.44), channel_id=1, source_target_pairs={{2,0},{3,1},{0,2},{1,3},{6,4},{7,5},{4,6},{5,7},{10,8},{11,9},{8,1... | collective-permute-start | bytes 196616 | tf_op jit(solution)/shard_map/ppermute | solution.py:501
  59.4 3.4 %collective-permute-start.8 = (f32[64,256]{1,0:T(8,128)S(1)}, f32[64,256]{1,0:T(8,128)S(1)}, u32[]{:S(2)}, u32[]{:S(2)}) collective-permute-start(f32[64,256]{1,0:T(8,128)S(1)} %get-tuple-element.45), channel_id=1, source_target_pairs={{1,0},{2,1},{3,2},{0,3},{5,4},{6,5},{7,6},{4,7},{9,8},{10,9},{11,1... | collective-permute-start | bytes 196616 | tf_op jit(solution)/shard_map/ppermute | solution.py:501
  62.8 4.4 %collective-permute-start.11 = (f32[64,256]{1,0:T(8,128)S(1)}, f32[64,256]{1,0:T(8,128)S(1)}, u32[]{:S(2)}, u32[]{:S(2)}) collective-permute-start(f32[64,256]{1,0:T(8,128)S(1)} %bitcast.22), channel_id=1, source_target_pairs={{3,0},{0,1},{1,2},{2,3},{7,4},{4,5},{5,6},{6,7},{11,8},{8,9},{9,10... | collective-permute-start | bytes 196616 | tf_op jit(solution)/shard_map/ppermute | solution.py:501
  62.9 5.6 %collective-permute-start.10 = (f32[64,256]{1,0:T(8,128)S(1)}, f32[64,256]{1,0:T(8,128)S(1)}, u32[]{:S(2)}, u32[]{:S(2)}) collective-permute-start(f32[64,256]{1,0:T(8,128)S(1)} %bitcast.23), channel_id=1, source_target_pairs={{2,0},{3,1},{0,2},{1,3},{6,4},{7,5},{4,6},{5,7},{10,8},{11,9},{8,1... | collective-permute-start | bytes 196616 | tf_op jit(solution)/shard_map/ppermute | solution.py:501
  66.1 3.4 %collective-permute-start.9 = (f32[64,256]{1,0:T(8,128)S(1)}, f32[64,256]{1,0:T(8,128)S(1)}, u32[]{:S(2)}, u32[]{:S(2)}) collective-permute-start(f32[64,256]{1,0:T(8,128)S(1)} %bitcast.24), channel_id=1, source_target_pairs={{1,0},{2,1},{3,2},{0,3},{5,4},{6,5},{7,6},{4,7},{9,8},{10,9},{11,1... | collective-permute-start | bytes 196616 | tf_op jit(solution)/shard_map/ppermute | solution.py:501
  70.6 4.8 %collective-permute-start.13 = (f32[256,256]{1,0:T(8,128)S(1)}, f32[256,256]{1,0:T(8,128)S(1)}, u32[]{:S(2)}, u32[]{:S(2)}) collective-permute-start(f32[256,256]{1,0:T(8,128)S(1)} %get-tuple-element.48.refs_0_.left_mine_ref), channel_id=1, source_target_pairs={{0,4},{4,0},{1,5},{5,1},{2,6},{6,2},{3,7},{7,3},{8,12},{12,8},{9,1... | collective-permute-start | bytes 786440 | tf_op jit(solution)/shard_map/ppermute | solution.py:497
  74.2 1.2 collective-permute-start.12
  75.4 9.7 %collective-permute-start.16 = (f32[32,256]{1,0:T(8,128)S(1)}, f32[32,256]{1,0:T(8,128)S(1)}, u32[]{:S(2)}, u32[]{:S(2)}) collective-permute-start(f32[32,256]{1,0:T(8,128)S(1)} %shard_map.53.own_ref), channel_id=1, source_target_pairs={{24,0},{0,8},{8,16},{16,24},{25,1},{1,9},{9,17},{17,25},{26,2},{2,... | collective-permute-start | bytes 98312 | tf_op jit(solution)/shard_map/ppermute | solution.py:501
  76.3 10.3 %collective-permute-start.15 = (f32[32,256]{1,0:T(8,128)S(1)}, f32[32,256]{1,0:T(8,128)S(1)}, u32[]{:S(2)}, u32[]{:S(2)}) collective-permute-start(f32[32,256]{1,0:T(8,128)S(1)} %shard_map.53.own_ref), channel_id=1, source_target_pairs={{16,0},{24,8},{0,16},{8,24},{17,1},{25,9},{1,17},{9,25},{18,2},{26... | collective-permute-start | bytes 98312 | tf_op jit(solution)/shard_map/ppermute | solution.py:501
  78.4 8.2 %collective-permute-start.14 = (f32[32,256]{1,0:T(8,128)S(1)}, f32[32,256]{1,0:T(8,128)S(1)}, u32[]{:S(2)}, u32[]{:S(2)}) collective-permute-start(f32[32,256]{1,0:T(8,128)S(1)} %shard_map.53.own_ref), channel_id=1, source_target_pairs={{8,0},{16,8},{24,16},{0,24},{9,1},{17,9},{25,17},{1,25},{10,2},{18... | collective-permute-start | bytes 98312 | tf_op jit(solution)/shard_map/ppermute | solution.py:501
  83.8 37.5 %collective-permute-start.21 = (f32[832,256]{1,0:T(8,128)S(1)}, f32[832,256]{1,0:T(8,128)S(1)}, u32[]{:S(2)}, u32[]{:S(2)}) collective-permute-start(f32[832,256]{1,0:T(8,128)S(1)} %get-tuple-element.52), channel_id=1, source_target_pairs={{24,0},{0,8},{8,16},{16,24},{25,1},{1,9},{9,17},{17,25},{26,2},{2,... | collective-permute-start | bytes 2555912 | tf_op jit(solution)/shard_map/ppermute | solution.py:501
  84.0 37.4 %collective-permute-start.22 = (f32[832,256]{1,0:T(8,128)S(1)}, f32[832,256]{1,0:T(8,128)S(1)}, u32[]{:S(2)}, u32[]{:S(2)}) collective-permute-start(f32[832,256]{1,0:T(8,128)S(1)} %get-tuple-element.53), channel_id=1, source_target_pairs={{16,0},{24,8},{0,16},{8,24},{17,1},{25,9},{1,17},{9,25},{18,2},{26... | collective-permute-start | bytes 2555912 | tf_op jit(solution)/shard_map/ppermute | solution.py:501
  85.1 38.3 %collective-permute-start.23 = (f32[832,256]{1,0:T(8,128)S(1)}, f32[832,256]{1,0:T(8,128)S(1)}, u32[]{:S(2)}, u32[]{:S(2)}) collective-permute-start(f32[832,256]{1,0:T(8,128)S(1)} %get-tuple-element.54), channel_id=1, source_target_pairs={{8,0},{16,8},{24,16},{0,24},{9,1},{17,9},{25,17},{1,25},{10,2},{18... | collective-permute-start | bytes 2555912 | tf_op jit(solution)/shard_map/ppermute | solution.py:501
  98.6 4.3 %collective-permute-start.17 = (f32[32,256]{1,0:T(8,128)S(1)}, f32[32,256]{1,0:T(8,128)S(1)}, u32[]{:S(2)}, u32[]{:S(2)}) collective-permute-start(f32[32,256]{1,0:T(8,128)S(1)} %bitcast.20), channel_id=1, source_target_pairs={{0,4},{4,0},{1,5},{5,1},{2,6},{6,2},{3,7},{7,3},{8,12},{12,8},{9,1... | collective-permute-start | bytes 98312 | tf_op jit(solution)/shard_map/ppermute | solution.py:497
  102.9 5.1 %collective-permute-start.20 = (f32[64,256]{1,0:T(8,128)S(1)}, f32[64,256]{1,0:T(8,128)S(1)}, u32[]{:S(2)}, u32[]{:S(2)}) collective-permute-start(f32[64,256]{1,0:T(8,128)S(1)} %pad_maximum_fusion.own_ref), channel_id=1, source_target_pairs={{3,0},{0,1},{1,2},{2,3},{7,4},{4,5},{5,6},{6,7},{11,8},{8,9},{9,10... | collective-permute-start | bytes 196616 | tf_op jit(solution)/shard_map/ppermute | solution.py:501
  102.9 5.8 %collective-permute-start.19 = (f32[64,256]{1,0:T(8,128)S(1)}, f32[64,256]{1,0:T(8,128)S(1)}, u32[]{:S(2)}, u32[]{:S(2)}) collective-permute-start(f32[64,256]{1,0:T(8,128)S(1)} %pad_maximum_fusion.own_ref), channel_id=1, source_target_pairs={{2,0},{3,1},{0,2},{1,3},{6,4},{7,5},{4,6},{5,7},{10,8},{11,9},{8,1... | collective-permute-start | bytes 196616 | tf_op jit(solution)/shard_map/ppermute | solution.py:501
  107.9 3.4 %collective-permute-start.18 = (f32[64,256]{1,0:T(8,128)S(1)}, f32[64,256]{1,0:T(8,128)S(1)}, u32[]{:S(2)}, u32[]{:S(2)}) collective-permute-start(f32[64,256]{1,0:T(8,128)S(1)} %pad_maximum_fusion.own_ref), channel_id=1, source_target_pairs={{1,0},{2,1},{3,2},{0,3},{5,4},{6,5},{7,6},{4,7},{9,8},{10,9},{11,1... | collective-permute-start | bytes 196616 | tf_op jit(solution)/shard_map/ppermute | solution.py:501
  123.3 55.6 %copy-start = (bf16[256,6656]{1,0:T(8,128)(2,1)S(1)}, bf16[256,6656]{1,0:T(8,128)(2,1)}, u32[]{:S(2)}) copy-start(bf16[256,6656]{1,0:T(8,128)(2,1)} %refs_1_.3) | copy-start | bytes 10223620
  154.7 20.4 %collective-permute-start.26 = (bf16[832,256]{1,0:T(8,128)(2,1)S(1)}, bf16[832,256]{1,0:T(8,128)(2,1)S(1)}, u32[]{:S(2)}, u32[]{:S(2)}) collective-permute-start(bf16[832,256]{1,0:T(8,128)(2,1)S(1)} %bitcast.9), channel_id=1, source_target_pairs={{0,4},{4,0},{1,5},{5,1},{2,6},{6,2},{3,7},{7,3},{8,12},{12,8},{9,1... | collective-permute-start | bytes 1277960 | tf_op jit(solution)/shard_map/ppermute | solution.py:497
  159.3 15.8 %collective-permute-start.25 = (bf16[832,256]{1,0:T(8,128)(2,1)S(1)}, bf16[832,256]{1,0:T(8,128)(2,1)S(1)}, u32[]{:S(2)}, u32[]{:S(2)}) collective-permute-start(bf16[832,256]{1,0:T(8,128)(2,1)S(1)} %bitcast.10), channel_id=1, source_target_pairs={{24,0},{0,8},{8,16},{16,24},{25,1},{1,9},{9,17},{17,25},{26,2},{2,... | collective-permute-start | bytes 1277960 | tf_op jit(solution)/shard_map/ppermute | solution.py:501
  161.9 13.2 %collective-permute-start.24 = (bf16[832,256]{1,0:T(8,128)(2,1)S(1)}, bf16[832,256]{1,0:T(8,128)(2,1)S(1)}, u32[]{:S(2)}, u32[]{:S(2)}) collective-permute-start(bf16[832,256]{1,0:T(8,128)(2,1)S(1)} %bitcast.11), channel_id=1, source_target_pairs={{8,0},{16,8},{24,16},{0,24},{9,1},{17,9},{25,17},{1,25},{10,2},{18... | collective-permute-start | bytes 1277960 | tf_op jit(solution)/shard_map/ppermute | solution.py:501
  175.1 3.8 %collective-permute-start.27 = (bf16[832,256]{1,0:T(8,128)(2,1)S(1)}, bf16[832,256]{1,0:T(8,128)(2,1)S(1)}, u32[]{:S(2)}, u32[]{:S(2)}) collective-permute-start(bf16[832,256]{1,0:T(8,128)(2,1)S(1)} %collective-permute-done.24.refs_5_), channel_id=1, source_target_pairs={{0,4},{4,0},{1,5},{5,1},{2,6},{6,2},{3,7},{7,3},{8,12},{12,8},{9,1... | collective-permute-start | bytes 1277960 | tf_op jit(solution)/shard_map/ppermute | solution.py:497
  175.6 3.3 %collective-permute-start.28 = (bf16[832,256]{1,0:T(8,128)(2,1)S(1)}, bf16[832,256]{1,0:T(8,128)(2,1)S(1)}, u32[]{:S(2)}, u32[]{:S(2)}) collective-permute-start(bf16[832,256]{1,0:T(8,128)(2,1)S(1)} %collective-permute-done.25.refs_6_), channel_id=1, source_target_pairs={{0,4},{4,0},{1,5},{5,1},{2,6},{6,2},{3,7},{7,3},{8,12},{12,8},{9,1... | collective-permute-start | bytes 1277960 | tf_op jit(solution)/shard_map/ppermute | solution.py:497
  175.7 9.4 %collective-permute-start.29 = (bf16[416,256]{1,0:T(8,128)(2,1)S(1)}, bf16[416,256]{1,0:T(8,128)(2,1)S(1)}, u32[]{:S(2)}, u32[]{:S(2)}) collective-permute-start(bf16[416,256]{1,0:T(8,128)(2,1)S(1)} %slice.6), channel_id=1, source_target_pairs={{24,0},{0,8},{8,16},{16,24},{25,1},{1,9},{9,17},{17,25},{26,2},{2,... | collective-permute-start | bytes 638984 | tf_op jit(solution)/shard_map/ppermute | solution.py:501
  176.7 8.5 %collective-permute-start.30 = (bf16[416,256]{1,0:T(8,128)(2,1)S(1)}, bf16[416,256]{1,0:T(8,128)(2,1)S(1)}, u32[]{:S(2)}, u32[]{:S(2)}) collective-permute-start(bf16[416,256]{1,0:T(8,128)(2,1)S(1)} %slice.7), channel_id=1, source_target_pairs={{8,0},{16,8},{24,16},{0,24},{9,1},{17,9},{25,17},{1,25},{10,2},{18... | collective-permute-start | bytes 638984 | tf_op jit(solution)/shard_map/ppermute | solution.py:501
  185.2 2.1 %collective-permute-start.31 = (bf16[416,256]{1,0:T(8,128)(2,1)S(1)}, bf16[416,256]{1,0:T(8,128)(2,1)S(1)}, u32[]{:S(2)}, u32[]{:S(2)}) collective-permute-start(bf16[416,256]{1,0:T(8,128)(2,1)S(1)} %collective-permute-done.29.refs_7_), channel_id=1, source_target_pairs={{0,4},{4,0},{1,5},{5,1},{2,6},{6,2},{3,7},{7,3},{8,12},{12,8},{9,1... | collective-permute-start | bytes 638984 | tf_op jit(solution)/shard_map/ppermute | solution.py:497
  186.2 1.5 collective-permute-start.32

commit v6 on v5

--- a/solution.py
+++ b/solution.py
@@ -27,16 +27,9 @@
     return lax.rem(index + by, parts)
 
 
-def inverse_factor_kernel(at_ref, own_ref, next_ref, across_ref, last_ref, inverse_ref, work_ref, half_ref, done_ref):
+def inverse_factor_kernel(gram_ref, inverse_ref, work_ref, half_ref, done_ref):
     rank = work_ref.shape[0]
-    part = rank // (NX * 2)
-    for by, ref in enumerate((own_ref, next_ref, across_ref, last_ref)):
-        base = ahead(at_ref[AT_X], by, NX) * 2
-        for other in range(2):
-            at_core = (at_ref[AT_CORE] + other) % 2
-            start = pl.multiple_of((base + at_core) * part, part)
-            work_ref[pl.ds(start, part), :] = ref[other * part : (other + 1) * part, :]
-    gram = work_ref[...]
+    gram = gram_ref[...]
     diagonal = lax.broadcasted_iota(jnp.int32, gram.shape, 0) == lax.broadcasted_iota(
         jnp.int32, gram.shape, 1
     )
@@ -122,17 +115,16 @@
     lax.fori_loop(0, 2, eliminate, 0)
 
 
-def inverse_factor(at, pieces):
-    rank = pieces[0].shape[1]
+def inverse_factor(gram_matrix):
+    rank = gram_matrix.shape[0]
     return pl.pallas_call(
         inverse_factor_kernel,
         out_shape=jax.ShapeDtypeStruct((rank, rank), f32),
-        in_specs=[SMEM] + [VMEM] * 4,
+        in_specs=[VMEM],
         out_specs=VMEM,
         scratch_shapes=[pltpu.VMEM((rows, rank), f32) for rows in (rank, rank // 2, rank // 2)],
         compiler_params=pltpu.CompilerParams(vmem_limit_bytes=8 * MIB),
-        cost_estimate=pl.CostEstimate(flops=10**9, bytes_accessed=2**20, transcendentals=0),
-    )(at, *pieces)
+    )(gram_matrix)
 
 
 def project_kernel(at_ref, mine_ref, other_ref, *refs):
@@ -552,9 +544,8 @@
     gram_rows = add(gram_keep, swap_cores(gram_send))
     gram_rows, proj_swapped = lax.optimization_barrier((gram_rows, swap_cores(projected)))
     gram_rows = all_of_four(gram_rows, "y")
-    gram_rows = sum_copies(exchange(sum_four_copies(gram_rows, NZ), "z"), 1)[0]
-    gram_chip = jnp.concatenate([gram_rows, swap_cores(gram_rows)])
-    inverse = inverse_factor(at, all_of_four(gram_chip, "x"))
+    gram_rows = sum_copies(exchange(sum_four_copies(gram_rows, NZ), "z"), NX * 2)
+    inverse = inverse_factor(exchange(gram_rows, ("x", "c")).reshape(rank, rank))
 
     crossed = cross(at, mine, other, projected, proj_swapped)
     right = [crossed[0]] + [from_ahead(crossed[by], "y", NY - by) for by in (1, 2, 3)]

time: 191 us -> 223 us (1.17)
  waiting for transfers between devices: 34.5 us -> 58.9 us
  blocking collectives: 74.6 us -> 88.5 us
  starting transfers between devices: 49.1 us -> 43.2 us
    ppermute x22 -> x19, waiting for transfers between devices: 30 us -> 55.4 us  [from_ahead(): lax.ppermute(block, axis, [((i + by) % parts, i) for i in range(parts)])]
    all_to_all x5 -> x6, blocking collectives: 74.6 us -> 88.5 us  [exchange(): return lax.all_to_all(pieces, axes, 0, 0)]
    ppermute x11 -> x10, starting transfers between devices: 19 us -> 15.4 us  [swap_cores(): return lax.ppermute(block, 'c', [(0, 1), (1, 0)])]
    ppermute x22 -> x19, starting transfers between devices: 30 us -> 27.7 us  [from_ahead(): lax.ppermute(block, axis, [((i + by) % parts, i) for i in range(parts)])]
    ppermute x11 -> x10, waiting for transfers between devices: 4.51 us -> 3.47 us  [swap_cores(): return lax.ppermute(block, 'c', [(0, 1), (1, 0)])]
  transfers between devices with their start and end apart: 33 -> 29, of which waited for: 18 -> 15; matrix products, arithmetic and copies ran while one was open for 1% -> 1% of each run, Pallas kernels for 11% -> 7%
where the time goes in v6:
time: 223 us
  blocking collectives  88.5 us (40%)
  waiting for transfers between devices  58.9 us (26%)
  starting transfers between devices  43.2 us (19%)
  Pallas kernels  28 us (13%)
  local copies, waits for them, and re-layouts  2.27 us (1%)
    all_to_all x6, blocking collectives, exchange(): return lax.all_to_all(pieces, axes, 0, 0)  88.5 us
    ppermute x19, waiting for transfers between devices, from_ahead(): lax.ppermute(block, axis, [((i + by) % parts, i) for i in range(parts)])  55.4 us
    ppermute x19, starting transfers between devices, from_ahead(): lax.ppermute(block, axis, [((i + by) % parts, i) for i in range(parts)])  27.7 us
    ppermute x10, starting transfers between devices, swap_cores(): return lax.ppermute(block, 'c', [(0, 1), (1, 0)])  15.4 us
    pallas_call x1, Pallas kernels, inverse_factor(): pl.pallas_call(inverse_factor_kernel, out_shape=jax.ShapeDtypeStruct((ran...  9.36 us
    pallas_call x1, Pallas kernels, finish(): pl.pallas_call(lambda *refs: first_kernel(scaling, *refs), out_shape=outs...  6.22 us
  transfers between devices with their start and end apart: 29, of which 15 were waited for; matrix products, arithmetic and copies ran while one was open for 1% of the time, Pallas kernels for 7%

profile of v6, /device:TPU:1, one launch (start us, length us, event | category | flops | bytes accessed | tf_op | source)
XLA Modules:
  0.0 222.9 jit_solution(7269156188687716650)
XLA Ops:
  0.6 0.9 convert_element_type.3
  1.7 3.3 %collective-permute-start = (bf16[4,3328]{1,0:T(4,128)(2,1)S(1)}, bf16[4,3328]{1,0:T(4,128)(2,1)S(1)}, u32[]{:S(2)}, u32[]{:S(2)}) collective-permute-start(bf16[4,3328]{1,0:T(4,128)(2,1)S(1)} %constant_dynamic-slice_fusion.2), channel_id=1, source_target_pairs={{0,4},{4,0},{1,5},{5,1},{2,6},{6,2},{3,7},{7,3},{8,12},{12,8},{9,1... | collective-permute-start | bytes 79880 | tf_op jit(solution)/shard_map/ppermute | solution.py:489
  4.9 2.2 constant_dynamic-slice_fusion
  7.4 20.6 %all_to_all.30 = bf16[8,8,3328]{2,1,0:T(8,128)(2,1)S(1)} all-to-all(bf16[8,8,3328]{2,1,0:T(8,128)(2,1)S(1)} %broadcast_in_dim.2), channel_id=1, replica_groups=mesh['z'=8,'y'=4,'c'=2,'x'=4] {'z'}, dimensions={0} | all-to-all | bytes 851968 | tf_op jit(solution)/shard_map/all_to_all | solution.py:509
  28.0 1.3 collective-permute-start.4
  29.3 2.6 %collective-permute-start.3 = (bf16[64,3328]{1,0:T(8,128)(2,1)S(1)}, bf16[64,3328]{1,0:T(8,128)(2,1)S(1)}, u32[]{:S(2)}, u32[]{:S(2)}) collective-permute-start(bf16[64,3328]{1,0:T(8,128)(2,1)S(1)} %bitcast.16), channel_id=1, source_target_pairs={{16,0},{24,8},{0,16},{8,24},{17,1},{25,9},{1,17},{9,25},{18,2},{26... | collective-permute-start | bytes 1277960 | tf_op jit(solution)/shard_map/ppermute | solution.py:493
  31.9 1.1 collective-permute-start.2
  33.0 5.7 %collective-permute-done.4.refs_3_ = bf16[64,3328]{1,0:T(8,128)(2,1)S(1)} collective-permute-done((bf16[64,3328]{1,0:T(8,128)(2,1)S(1)}, bf16[64,3328]{1,0:T(8,128)(2,1)S(1)}, u32[]{:S(2)}, u32[]{:S(2)}) %collective-permute-start.4) | collective-permute-done | bytes 426016 | tf_op jit(solution)/shard_map/ppermute | solution.py:493
  38.6 10.2 %collective-permute-done.3.refs_2_ = bf16[64,3328]{1,0:T(8,128)(2,1)S(1)} collective-permute-done((bf16[64,3328]{1,0:T(8,128)(2,1)S(1)}, bf16[64,3328]{1,0:T(8,128)(2,1)S(1)}, u32[]{:S(2)}, u32[]{:S(2)}) %collective-permute-start.3) | collective-permute-done | bytes 426016 | tf_op jit(solution)/shard_map/ppermute | solution.py:493
  48.9 0.8 collective-permute-done.2.refs_1_
  49.7 2.0 shard_map.49
  51.7 2.2 collective-permute-start.5
  53.9 1.2 collective-permute-done.5.two_ref
  55.1 0.6 shard_map.50
  55.7 1.3 collective-permute-start.6
  56.9 2.5 %collective-permute-start.7 = (f32[64,256]{1,0:T(8,128)S(1)}, f32[64,256]{1,0:T(8,128)S(1)}, u32[]{:S(2)}, u32[]{:S(2)}) collective-permute-start(f32[64,256]{1,0:T(8,128)S(1)} %get-tuple-element.44), channel_id=1, source_target_pairs={{2,0},{3,1},{0,2},{1,3},{6,4},{7,5},{4,6},{5,7},{10,8},{11,9},{8,1... | collective-permute-start | bytes 196616 | tf_op jit(solution)/shard_map/ppermute | solution.py:493
  59.4 1.1 collective-permute-start.8
  60.5 1.8 collective-permute-done.7.two_ref
  62.9 3.2 %collective-permute-start.10 = (f32[64,256]{1,0:T(8,128)S(1)}, f32[64,256]{1,0:T(8,128)S(1)}, u32[]{:S(2)}, u32[]{:S(2)}) collective-permute-start(f32[64,256]{1,0:T(8,128)S(1)} %bitcast.22), channel_id=1, source_target_pairs={{2,0},{3,1},{0,2},{1,3},{6,4},{7,5},{4,6},{5,7},{10,8},{11,9},{8,1... | collective-permute-start | bytes 196616 | tf_op jit(solution)/shard_map/ppermute | solution.py:493
  66.5 0.7 collective-permute-done.11.three_ref
  67.2 1.3 collective-permute-done.10.two_ref
  68.5 1.1 collective-permute-done.9.one_ref
  69.6 1.0 shard_map.52
  70.6 3.6 %collective-permute-start.13 = (f32[256,256]{1,0:T(8,128)S(1)}, f32[256,256]{1,0:T(8,128)S(1)}, u32[]{:S(2)}, u32[]{:S(2)}) collective-permute-start(f32[256,256]{1,0:T(8,128)S(1)} %get-tuple-element.48.refs_0_.left_mine_ref), channel_id=1, source_target_pairs={{0,4},{4,0},{1,5},{5,1},{2,6},{6,2},{3,7},{7,3},{8,12},{12,8},{9,1... | collective-permute-start | bytes 786440 | tf_op jit(solution)/shard_map/ppermute | solution.py:489
  74.4 0.9 collective-permute-done.12.two_ref
  75.4 4.0 %shard_map.58 = (f32[832,256]{1,0:T(8,128)S(1)}, f32[832,256]{1,0:T(8,128)S(1)}, f32[832,256]{1,0:T(8,128)S(1)}, f32[832,256]{1,0:T(8,128)S(1)}) custom-call(s32[4]{0:T(128)S(1)} %pad_add_fusion.at_ref.refs_0_, bf16[256,3328]{1,0:T(8,128)(2,1)S(1)} %get-tuple-element.37.mine_ref, bf16[256,3328]{1,0:T(8,128)(2,1)S(1)} %collective-permute-done.1.other_ref, ...), custom_call_target="tpu_custom_call" | custom-call | flops 2617245696 | bytes 10223616 | tf_op jit(solution)/shard_map/pallas_call | solution.py:307
  79.4 1.0 collective-permute-start.17
  80.3 2.1 collective-permute-start.18
  82.4 1.4 collective-permute-start.19
  83.9 1.1 collective-permute-start.15
  85.0 32.3 %collective-permute-done.16.three_ref = f32[32,256]{1,0:T(8,128)S(1)} collective-permute-done((f32[32,256]{1,0:T(8,128)S(1)}, f32[32,256]{1,0:T(8,128)S(1)}, u32[]{:S(2)}, u32[]{:S(2)}) %collective-permute-start.16) | collective-permute-done | bytes 32800 | tf_op jit(solution)/shard_map/ppermute | solution.py:493
  117.3 3.1 %collective-permute-start.14 = (f32[32,256]{1,0:T(8,128)S(1)}, f32[32,256]{1,0:T(8,128)S(1)}, u32[]{:S(2)}, u32[]{:S(2)}) collective-permute-start(f32[32,256]{1,0:T(8,128)S(1)} %shard_map.53.own_ref), channel_id=1, source_target_pairs={{8,0},{16,8},{24,16},{0,24},{9,1},{17,9},{25,17},{1,25},{10,2},{18... | collective-permute-start | bytes 98312 | tf_op jit(solution)/shard_map/ppermute | solution.py:493
  120.8 0.7 collective-permute-done.14.one_ref
  121.5 11.8 %all_to_all.31.pieces_ref = f32[8,32,256]{2,1,0:T(8,128)S(1)} all-to-all(f32[8,32,256]{2,1,0:T(8,128)S(1)} %shard_map.54), channel_id=1, replica_groups=mesh['z'=8,'y'=4,'c'=2,'x'=4] {'z'}, dimensions={0} | all-to-all | bytes 524288 | tf_op jit(solution)/shard_map/all_to_all | solution.py:509
  133.4 13.4 %all_to_all.32 = f32[8,32,256]{2,1,0:T(8,128)S(1)} all-to-all(f32[8,32,256]{2,1,0:T(8,128)S(1)} %shard_map.55), channel_id=1, replica_groups=mesh['z'=8,'y'=4,'c'=2,'x'=4] {'x','c'}, dimensions={0} | all-to-all | bytes 524288 | tf_op jit(solution)/shard_map/all_to_all | solution.py:509
  146.8 9.4 %shard_map.56.inverse_ref = f32[256,256]{1,0:T(8,128)S(1)} custom-call(f32[256,256]{1,0:T(8,128)S(1)} %bitcast.20), custom_call_target="tpu_custom_call" | custom-call | tf_op jit(solution)/shard_map/pallas_call | solution.py:120
  156.2 0.9 shard_map.59
  157.1 16.5 %all_to_all.33.pieces_ref = bf16[8,104,256]{2,1,0:T(8,128)(2,1)S(1)} all-to-all(bf16[8,104,256]{2,1,0:T(8,128)(2,1)S(1)} %bitcast.19), channel_id=1, replica_groups=mesh['z'=8,'y'=4,'c'=2,'x'=4] {'z'}, dimensions={0} | all-to-all | bytes 851968 | tf_op jit(solution)/shard_map/all_to_all | solution.py:509
  173.7 14.5 %all_to_all.34 = bf16[8,104,256]{2,1,0:T(8,128)(2,1)S(1)} all-to-all(bf16[8,104,256]{2,1,0:T(8,128)(2,1)S(1)} %shard_map.60), channel_id=1, replica_groups=mesh['z'=8,'y'=4,'c'=2,'x'=4] {'z'}, dimensions={0} | all-to-all | bytes 851968 | tf_op jit(solution)/shard_map/all_to_all | solution.py:509
  188.2 4.3 %collective-permute-start.22 = (bf16[832,256]{1,0:T(8,128)(2,1)S(1)}, bf16[832,256]{1,0:T(8,128)(2,1)S(1)}, u32[]{:S(2)}, u32[]{:S(2)}) collective-permute-start(bf16[832,256]{1,0:T(8,128)(2,1)S(1)} %bitcast.9), channel_id=1, source_target_pairs={{0,4},{4,0},{1,5},{5,1},{2,6},{6,2},{3,7},{7,3},{8,12},{12,8},{9,1... | collective-permute-start | bytes 1277960 | tf_op jit(solution)/shard_map/ppermute | solution.py:489
  192.9 2.2 collective-permute-start.20
  195.2 11.7 %all_to_all.35.refs_3_ = f32[32,1,256]{2,1,0:T(1,128)S(1)} all-to-all(f32[32,1,256]{2,1,0:T(1,128)S(1)} %shard_map.61), channel_id=1, replica_groups=mesh['z'=8,'y'=4,'c'=2,'x'=4] {'y','c','x'}, dimensions={0} | all-to-all | bytes 65536 | tf_op jit(solution)/shard_map/all_to_all | solution.py:509
  207.6 1.0 collective-permute-start.25
  208.5 1.8 collective-permute-start.26
  210.8 6.2 %shard_map.62 = (bf16[256,6656]{1,0:T(8,128)(2,1)}, bf16[256,6656]{1,0:T(8,128)(2,1)}, f32[4,6656]{1,0:T(4,128)}) custom-call(s32[4]{0:T(128)S(1)} %pad_add_fusion.at_ref.refs_0_, bf16[256,6656]{1,0:T(8,128)(2,1)S(1)} %copy-done, f32[256,256]{1,0:T(8,128)S(1)} %shard_map.57.refs_2_, f32[32,1,256]{2,1,0:T(1,128)S(1)} %all_to_all.35.refs_3_, ...), custom_call_target="tpu_custom_call" | custom-call | flops 1308622848 | bytes 10223616 | tf_op jit(solution)/shard_map/pallas_call | solution.py:453
  217.0 1.0 collective-permute-start.27
  218.1 1.0 collective-permute-done.27.refs_12_
  219.5 3.2 %shard_map.63 = (bf16[256,6656]{1,0:T(8,128)(2,1)}, bf16[256,6656]{1,0:T(8,128)(2,1)}, f32[4,6656]{1,0:T(4,128)}) custom-call(s32[4]{0:T(128)S(1)} %pad_add_fusion.at_ref.refs_0_, bf16[256,6656]{1,0:T(8,128)(2,1)S(1)} %copy-done, f32[256,256]{1,0:T(8,128)S(1)} %shard_map.57.refs_2_, ...), custom_call_target="tpu_custom_call", output_to_operand_aliasing={{0}: (14, {}), {1}: (15, {}), {2}: (16, {})} | custom-call | flops 436207616 | bytes 3407872 | tf_op jit(solution)/shard_map/pallas_call | solution.py:471
  (42 shorter events, 4.2 us)
Async XLA Ops:
  1.7 5.5 %collective-permute-start = (bf16[4,3328]{1,0:T(4,128)(2,1)S(1)}, bf16[4,3328]{1,0:T(4,128)(2,1)S(1)}, u32[]{:S(2)}, u32[]{:S(2)}) collective-permute-start(bf16[4,3328]{1,0:T(4,128)(2,1)S(1)} %constant_dynamic-slice_fusion.2), channel_id=1, source_target_pairs={{0,4},{4,0},{1,5},{5,1},{2,6},{6,2},{3,7},{7,3},{8,12},{12,8},{9,1... | collective-permute-start | bytes 79880 | tf_op jit(solution)/shard_map/ppermute | solution.py:489
  7.1 42.5 %collective-permute-start.1 = (bf16[256,3328]{1,0:T(8,128)(2,1)S(1)}, bf16[256,3328]{1,0:T(8,128)(2,1)S(1)}, u32[]{:S(2)}, u32[]{:S(2)}) collective-permute-start(bf16[256,3328]{1,0:T(8,128)(2,1)S(1)} %get-tuple-element.38), channel_id=1, source_target_pairs={{0,4},{4,0},{1,5},{5,1},{2,6},{6,2},{3,7},{7,3},{8,12},{12,8},{9,1... | collective-permute-start | bytes 5111816 | tf_op jit(solution)/shard_map/ppermute | solution.py:489
  28.0 10.7 %collective-permute-start.4 = (bf16[64,3328]{1,0:T(8,128)(2,1)S(1)}, bf16[64,3328]{1,0:T(8,128)(2,1)S(1)}, u32[]{:S(2)}, u32[]{:S(2)}) collective-permute-start(bf16[64,3328]{1,0:T(8,128)(2,1)S(1)} %bitcast.15), channel_id=1, source_target_pairs={{24,0},{0,8},{8,16},{16,24},{25,1},{1,9},{9,17},{17,25},{26,2},{2,... | collective-permute-start | bytes 1277960 | tf_op jit(solution)/shard_map/ppermute | solution.py:493
  29.3 19.6 %collective-permute-start.3 = (bf16[64,3328]{1,0:T(8,128)(2,1)S(1)}, bf16[64,3328]{1,0:T(8,128)(2,1)S(1)}, u32[]{:S(2)}, u32[]{:S(2)}) collective-permute-start(bf16[64,3328]{1,0:T(8,128)(2,1)S(1)} %bitcast.16), channel_id=1, source_target_pairs={{16,0},{24,8},{0,16},{8,24},{17,1},{25,9},{1,17},{9,25},{18,2},{26... | collective-permute-start | bytes 1277960 | tf_op jit(solution)/shard_map/ppermute | solution.py:493
  31.9 17.8 %collective-permute-start.2 = (bf16[64,3328]{1,0:T(8,128)(2,1)S(1)}, bf16[64,3328]{1,0:T(8,128)(2,1)S(1)}, u32[]{:S(2)}, u32[]{:S(2)}) collective-permute-start(bf16[64,3328]{1,0:T(8,128)(2,1)S(1)} %bitcast.17), channel_id=1, source_target_pairs={{8,0},{16,8},{24,16},{0,24},{9,1},{17,9},{25,17},{1,25},{10,2},{18... | collective-permute-start | bytes 1277960 | tf_op jit(solution)/shard_map/ppermute | solution.py:493
  51.7 3.4 %collective-permute-start.5 = (f32[256,256]{1,0:T(8,128)S(1)}, f32[256,256]{1,0:T(8,128)S(1)}, u32[]{:S(2)}, u32[]{:S(2)}) collective-permute-start(f32[256,256]{1,0:T(8,128)S(1)} %get-tuple-element.41), channel_id=1, source_target_pairs={{0,4},{4,0},{1,5},{5,1},{2,6},{6,2},{3,7},{7,3},{8,12},{12,8},{9,1... | collective-permute-start | bytes 786440 | tf_op jit(solution)/shard_map/ppermute | solution.py:489
  55.7 4.9 %collective-permute-start.6 = (f32[64,256]{1,0:T(8,128)S(1)}, f32[64,256]{1,0:T(8,128)S(1)}, u32[]{:S(2)}, u32[]{:S(2)}) collective-permute-start(f32[64,256]{1,0:T(8,128)S(1)} %get-tuple-element.43), channel_id=1, source_target_pairs={{3,0},{0,1},{1,2},{2,3},{7,4},{4,5},{5,6},{6,7},{11,8},{8,9},{9,10... | collective-permute-start | bytes 196616 | tf_op jit(solution)/shard_map/ppermute | solution.py:493
  56.9 5.4 %collective-permute-start.7 = (f32[64,256]{1,0:T(8,128)S(1)}, f32[64,256]{1,0:T(8,128)S(1)}, u32[]{:S(2)}, u32[]{:S(2)}) collective-permute-start(f32[64,256]{1,0:T(8,128)S(1)} %get-tuple-element.44), channel_id=1, source_target_pairs={{2,0},{3,1},{0,2},{1,3},{6,4},{7,5},{4,6},{5,7},{10,8},{11,9},{8,1... | collective-permute-start | bytes 196616 | tf_op jit(solution)/shard_map/ppermute | solution.py:493
  59.4 3.4 %collective-permute-start.8 = (f32[64,256]{1,0:T(8,128)S(1)}, f32[64,256]{1,0:T(8,128)S(1)}, u32[]{:S(2)}, u32[]{:S(2)}) collective-permute-start(f32[64,256]{1,0:T(8,128)S(1)} %get-tuple-element.45), channel_id=1, source_target_pairs={{1,0},{2,1},{3,2},{0,3},{5,4},{6,5},{7,6},{4,7},{9,8},{10,9},{11,1... | collective-permute-start | bytes 196616 | tf_op jit(solution)/shard_map/ppermute | solution.py:493
  62.8 4.4 %collective-permute-start.11 = (f32[64,256]{1,0:T(8,128)S(1)}, f32[64,256]{1,0:T(8,128)S(1)}, u32[]{:S(2)}, u32[]{:S(2)}) collective-permute-start(f32[64,256]{1,0:T(8,128)S(1)} %bitcast.21), channel_id=1, source_target_pairs={{3,0},{0,1},{1,2},{2,3},{7,4},{4,5},{5,6},{6,7},{11,8},{8,9},{9,10... | collective-permute-start | bytes 196616 | tf_op jit(solution)/shard_map/ppermute | solution.py:493
  62.9 5.6 %collective-permute-start.10 = (f32[64,256]{1,0:T(8,128)S(1)}, f32[64,256]{1,0:T(8,128)S(1)}, u32[]{:S(2)}, u32[]{:S(2)}) collective-permute-start(f32[64,256]{1,0:T(8,128)S(1)} %bitcast.22), channel_id=1, source_target_pairs={{2,0},{3,1},{0,2},{1,3},{6,4},{7,5},{4,6},{5,7},{10,8},{11,9},{8,1... | collective-permute-start | bytes 196616 | tf_op jit(solution)/shard_map/ppermute | solution.py:493
  66.1 3.4 %collective-permute-start.9 = (f32[64,256]{1,0:T(8,128)S(1)}, f32[64,256]{1,0:T(8,128)S(1)}, u32[]{:S(2)}, u32[]{:S(2)}) collective-permute-start(f32[64,256]{1,0:T(8,128)S(1)} %bitcast.23), channel_id=1, source_target_pairs={{1,0},{2,1},{3,2},{0,3},{5,4},{6,5},{7,6},{4,7},{9,8},{10,9},{11,1... | collective-permute-start | bytes 196616 | tf_op jit(solution)/shard_map/ppermute | solution.py:493
  70.6 4.8 %collective-permute-start.13 = (f32[256,256]{1,0:T(8,128)S(1)}, f32[256,256]{1,0:T(8,128)S(1)}, u32[]{:S(2)}, u32[]{:S(2)}) collective-permute-start(f32[256,256]{1,0:T(8,128)S(1)} %get-tuple-element.48.refs_0_.left_mine_ref), channel_id=1, source_target_pairs={{0,4},{4,0},{1,5},{5,1},{2,6},{6,2},{3,7},{7,3},{8,12},{12,8},{9,1... | collective-permute-start | bytes 786440 | tf_op jit(solution)/shard_map/ppermute | solution.py:489
  74.2 1.2 collective-permute-start.12
  79.4 76.8 %collective-permute-start.17 = (f32[832,256]{1,0:T(8,128)S(1)}, f32[832,256]{1,0:T(8,128)S(1)}, u32[]{:S(2)}, u32[]{:S(2)}) collective-permute-start(f32[832,256]{1,0:T(8,128)S(1)} %get-tuple-element.52), channel_id=1, source_target_pairs={{24,0},{0,8},{8,16},{16,24},{25,1},{1,9},{9,17},{17,25},{26,2},{2,... | collective-permute-start | bytes 2555912 | tf_op jit(solution)/shard_map/ppermute | solution.py:493
  80.3 75.8 %collective-permute-start.18 = (f32[832,256]{1,0:T(8,128)S(1)}, f32[832,256]{1,0:T(8,128)S(1)}, u32[]{:S(2)}, u32[]{:S(2)}) collective-permute-start(f32[832,256]{1,0:T(8,128)S(1)} %get-tuple-element.53), channel_id=1, source_target_pairs={{16,0},{24,8},{0,16},{8,24},{17,1},{25,9},{1,17},{9,25},{18,2},{26... | collective-permute-start | bytes 2555912 | tf_op jit(solution)/shard_map/ppermute | solution.py:493
  82.4 73.7 %collective-permute-start.19 = (f32[832,256]{1,0:T(8,128)S(1)}, f32[832,256]{1,0:T(8,128)S(1)}, u32[]{:S(2)}, u32[]{:S(2)}) collective-permute-start(f32[832,256]{1,0:T(8,128)S(1)} %get-tuple-element.54), channel_id=1, source_target_pairs={{8,0},{16,8},{24,16},{0,24},{9,1},{17,9},{25,17},{1,25},{10,2},{18... | collective-permute-start | bytes 2555912 | tf_op jit(solution)/shard_map/ppermute | solution.py:493
  83.8 33.5 %collective-permute-start.16 = (f32[32,256]{1,0:T(8,128)S(1)}, f32[32,256]{1,0:T(8,128)S(1)}, u32[]{:S(2)}, u32[]{:S(2)}) collective-permute-start(f32[32,256]{1,0:T(8,128)S(1)} %shard_map.53.own_ref), channel_id=1, source_target_pairs={{24,0},{0,8},{8,16},{16,24},{25,1},{1,9},{9,17},{17,25},{26,2},{2,... | collective-permute-start | bytes 98312 | tf_op jit(solution)/shard_map/ppermute | solution.py:493
  83.9 36.9 %collective-permute-start.15 = (f32[32,256]{1,0:T(8,128)S(1)}, f32[32,256]{1,0:T(8,128)S(1)}, u32[]{:S(2)}, u32[]{:S(2)}) collective-permute-start(f32[32,256]{1,0:T(8,128)S(1)} %shard_map.53.own_ref), channel_id=1, source_target_pairs={{16,0},{24,8},{0,16},{8,24},{17,1},{25,9},{1,17},{9,25},{18,2},{26... | collective-permute-start | bytes 98312 | tf_op jit(solution)/shard_map/ppermute | solution.py:493
  117.3 4.2 %collective-permute-start.14 = (f32[32,256]{1,0:T(8,128)S(1)}, f32[32,256]{1,0:T(8,128)S(1)}, u32[]{:S(2)}, u32[]{:S(2)}) collective-permute-start(f32[32,256]{1,0:T(8,128)S(1)} %shard_map.53.own_ref), channel_id=1, source_target_pairs={{8,0},{16,8},{24,16},{0,24},{9,1},{17,9},{25,17},{1,25},{10,2},{18... | collective-permute-start | bytes 98312 | tf_op jit(solution)/shard_map/ppermute | solution.py:493
  156.2 54.6 %copy-start = (bf16[256,6656]{1,0:T(8,128)(2,1)S(1)}, bf16[256,6656]{1,0:T(8,128)(2,1)}, u32[]{:S(2)}) copy-start(bf16[256,6656]{1,0:T(8,128)(2,1)} %refs_1_.3) | copy-start | bytes 10223620
  188.2 18.7 %collective-permute-start.22 = (bf16[832,256]{1,0:T(8,128)(2,1)S(1)}, bf16[832,256]{1,0:T(8,128)(2,1)S(1)}, u32[]{:S(2)}, u32[]{:S(2)}) collective-permute-start(bf16[832,256]{1,0:T(8,128)(2,1)S(1)} %bitcast.9), channel_id=1, source_target_pairs={{0,4},{4,0},{1,5},{5,1},{2,6},{6,2},{3,7},{7,3},{8,12},{12,8},{9,1... | collective-permute-start | bytes 1277960 | tf_op jit(solution)/shard_map/ppermute | solution.py:489
  192.4 14.5 %collective-permute-start.21 = (bf16[832,256]{1,0:T(8,128)(2,1)S(1)}, bf16[832,256]{1,0:T(8,128)(2,1)S(1)}, u32[]{:S(2)}, u32[]{:S(2)}) collective-permute-start(bf16[832,256]{1,0:T(8,128)(2,1)S(1)} %bitcast.10), channel_id=1, source_target_pairs={{24,0},{0,8},{8,16},{16,24},{25,1},{1,9},{9,17},{17,25},{26,2},{2,... | collective-permute-start | bytes 1277960 | tf_op jit(solution)/shard_map/ppermute | solution.py:493
  192.9 14.0 %collective-permute-start.20 = (bf16[832,256]{1,0:T(8,128)(2,1)S(1)}, bf16[832,256]{1,0:T(8,128)(2,1)S(1)}, u32[]{:S(2)}, u32[]{:S(2)}) collective-permute-start(bf16[832,256]{1,0:T(8,128)(2,1)S(1)} %bitcast.11), channel_id=1, source_target_pairs={{8,0},{16,8},{24,16},{0,24},{9,1},{17,9},{25,17},{1,25},{10,2},{18... | collective-permute-start | bytes 1277960 | tf_op jit(solution)/shard_map/ppermute | solution.py:493
  206.9 3.8 %collective-permute-start.23 = (bf16[832,256]{1,0:T(8,128)(2,1)S(1)}, bf16[832,256]{1,0:T(8,128)(2,1)S(1)}, u32[]{:S(2)}, u32[]{:S(2)}) collective-permute-start(bf16[832,256]{1,0:T(8,128)(2,1)S(1)} %collective-permute-done.20.refs_5_), channel_id=1, source_target_pairs={{0,4},{4,0},{1,5},{5,1},{2,6},{6,2},{3,7},{7,3},{8,12},{12,8},{9,1... | collective-permute-start | bytes 1277960 | tf_op jit(solution)/shard_map/ppermute | solution.py:489
  207.4 3.3 %collective-permute-start.24 = (bf16[832,256]{1,0:T(8,128)(2,1)S(1)}, bf16[832,256]{1,0:T(8,128)(2,1)S(1)}, u32[]{:S(2)}, u32[]{:S(2)}) collective-permute-start(bf16[832,256]{1,0:T(8,128)(2,1)S(1)} %collective-permute-done.21.refs_6_), channel_id=1, source_target_pairs={{0,4},{4,0},{1,5},{5,1},{2,6},{6,2},{3,7},{7,3},{8,12},{12,8},{9,1... | collective-permute-start | bytes 1277960 | tf_op jit(solution)/shard_map/ppermute | solution.py:489
  207.6 9.4 %collective-permute-start.25 = (bf16[416,256]{1,0:T(8,128)(2,1)S(1)}, bf16[416,256]{1,0:T(8,128)(2,1)S(1)}, u32[]{:S(2)}, u32[]{:S(2)}) collective-permute-start(bf16[416,256]{1,0:T(8,128)(2,1)S(1)} %slice.6), channel_id=1, source_target_pairs={{24,0},{0,8},{8,16},{16,24},{25,1},{1,9},{9,17},{17,25},{26,2},{2,... | collective-permute-start | bytes 638984 | tf_op jit(solution)/shard_map/ppermute | solution.py:493
  208.5 8.5 %collective-permute-start.26 = (bf16[416,256]{1,0:T(8,128)(2,1)S(1)}, bf16[416,256]{1,0:T(8,128)(2,1)S(1)}, u32[]{:S(2)}, u32[]{:S(2)}) collective-permute-start(bf16[416,256]{1,0:T(8,128)(2,1)S(1)} %slice.7), channel_id=1, source_target_pairs={{8,0},{16,8},{24,16},{0,24},{9,1},{17,9},{25,17},{1,25},{10,2},{18... | collective-permute-start | bytes 638984 | tf_op jit(solution)/shard_map/ppermute | solution.py:493
  217.0 2.1 collective-permute-start.27
  218.0 1.5 collective-permute-start.28

commit v7 on v5

--- a/solution.py
+++ b/solution.py
@@ -508,7 +508,7 @@
 def ring_of_four(block, axis, beside):
     middle = block.shape[0] // 2
     one, three = from_ahead(block, axis, 1), from_ahead(block, axis, 3)
-    one, three, beside = lax.optimization_barrier((one, three, beside))
+    block, one, three, beside = lax.optimization_barrier((block, one, three, beside))
     across = (from_ahead(three[:middle], axis, 3), from_ahead(one[middle:], axis, 1))
     return (block, one, three), across, beside
 
@@ -564,8 +564,8 @@
 
     parts = NY * 2 * NX
     squares = exchange(square_copies(right, parts), ("y", "c", "x"))
-    near, far, (squares, swapped) = ring_of_four(right, "y", (squares, swap_cores(right)))
-    near = near + (swapped,) + tuple(swap_cores(block) for block in near[1:])
+    near, far, squares = ring_of_four(right, "y", squares)
+    near = near + tuple(swap_cores(block) for block in near)
 
     total_rows = rows * NZ * NY * 2
     total_cols = cols * NX

time: 191 us -> 191 us (level)
  blocking collectives: 74.6 us -> 78.9 us
  starting transfers between devices: 49.1 us -> 44.9 us
    ppermute x11, starting transfers between devices: 19 us -> 14.5 us  [swap_cores(): return lax.ppermute(block, 'c', [(0, 1), (1, 0)])]
    all_to_all x5, blocking collectives: 74.6 us -> 78.9 us  [exchange(): return lax.all_to_all(pieces, axes, 0, 0)]
where the time goes in v7:
time: 191 us
  blocking collectives  78.9 us (41%)
  starting transfers between devices  44.9 us (24%)
  waiting for transfers between devices  34.5 us (18%)
  Pallas kernels  28.5 us (15%)
  local copies, waits for them, and re-layouts  2.27 us (1%)
    all_to_all x5, blocking collectives, exchange(): return lax.all_to_all(pieces, axes, 0, 0)  78.9 us
    ppermute x22, starting transfers between devices, from_ahead(): lax.ppermute(block, axis, [((i + by) % parts, i) for i in range(parts)])  30.4 us
    ppermute x22, waiting for transfers between devices, from_ahead(): lax.ppermute(block, axis, [((i + by) % parts, i) for i in range(parts)])  30 us
    ppermute x11, starting transfers between devices, swap_cores(): return lax.ppermute(block, 'c', [(0, 1), (1, 0)])  14.5 us
    pallas_call x1, Pallas kernels, inverse_factor(): pl.pallas_call(inverse_factor_kernel, out_shape=jax.ShapeDtypeStruct((ran...  9.93 us
    pallas_call x1, Pallas kernels, finish(): pl.pallas_call(lambda *refs: first_kernel(scaling, *refs), out_shape=outs...  6.22 us
    ppermute x11, waiting for transfers between devices, swap_cores(): return lax.ppermute(block, 'c', [(0, 1), (1, 0)])  4.51 us
    pallas_call x1, Pallas kernels, cross(): pl.pallas_call(cross_kernel, out_shape=[jax.ShapeDtypeStruct((cols // NY,...  3.98 us
  transfers between devices with their start and end apart: 33, of which 18 were waited for; matrix products, arithmetic and copies ran while one was open for 1% of the time, Pallas kernels for 11%

profile of v7, /device:TPU:1, one launch (start us, length us, event | category | flops | bytes accessed | tf_op | source)
XLA Modules:
  0.0 191.2 jit_solution(10698825557266068199)
XLA Ops:
  0.6 0.9 convert_element_type.3
  1.7 3.3 %collective-permute-start = (bf16[4,3328]{1,0:T(4,128)(2,1)S(1)}, bf16[4,3328]{1,0:T(4,128)(2,1)S(1)}, u32[]{:S(2)}, u32[]{:S(2)}) collective-permute-start(bf16[4,3328]{1,0:T(4,128)(2,1)S(1)} %constant_dynamic-slice_fusion.2), channel_id=1, source_target_pairs={{0,4},{4,0},{1,5},{5,1},{2,6},{6,2},{3,7},{7,3},{8,12},{12,8},{9,1... | collective-permute-start | bytes 79880 | tf_op jit(solution)/shard_map/ppermute | solution.py:497
  4.9 2.2 %constant_dynamic-slice_fusion = (bf16[256,3328]{1,0:T(8,128)(2,1)S(1)}, bf16[256,3328]{1,0:T(8,128)(2,1)S(1)}) fusion(bf16[256,6656]{1,0:T(8,128)(2,1)} %refs_1_.3, s32[]{:T(128)S(6)} %select_n.20, s32[]{:T(128)S(6)} %select_n.21), kind=kLoop, calls=%fused_computation.4 | loop fusion | bytes 6815752 | tf_op jit(solution)/shard_map/dynamic_slice | solution.py:531
  7.4 20.6 %all_to_all.25 = bf16[8,8,3328]{2,1,0:T(8,128)(2,1)S(1)} all-to-all(bf16[8,8,3328]{2,1,0:T(8,128)(2,1)S(1)} %broadcast_in_dim.2), channel_id=1, replica_groups=mesh['z'=8,'y'=4,'c'=2,'x'=4] {'z'}, dimensions={0} | all-to-all | bytes 851968 | tf_op jit(solution)/shard_map/all_to_all | solution.py:517
  28.0 1.3 collective-permute-start.4
  29.3 2.6 %collective-permute-start.3 = (bf16[64,3328]{1,0:T(8,128)(2,1)S(1)}, bf16[64,3328]{1,0:T(8,128)(2,1)S(1)}, u32[]{:S(2)}, u32[]{:S(2)}) collective-permute-start(bf16[64,3328]{1,0:T(8,128)(2,1)S(1)} %bitcast.16), channel_id=1, source_target_pairs={{16,0},{24,8},{0,16},{8,24},{17,1},{25,9},{1,17},{9,25},{18,2},{26... | collective-permute-start | bytes 1277960 | tf_op jit(solution)/shard_map/ppermute | solution.py:501
  31.9 1.1 collective-permute-start.2
  33.0 5.7 %collective-permute-done.4.refs_3_ = bf16[64,3328]{1,0:T(8,128)(2,1)S(1)} collective-permute-done((bf16[64,3328]{1,0:T(8,128)(2,1)S(1)}, bf16[64,3328]{1,0:T(8,128)(2,1)S(1)}, u32[]{:S(2)}, u32[]{:S(2)}) %collective-permute-start.4) | collective-permute-done | bytes 426016 | tf_op jit(solution)/shard_map/ppermute | solution.py:501
  38.6 10.2 %collective-permute-done.3.refs_2_ = bf16[64,3328]{1,0:T(8,128)(2,1)S(1)} collective-permute-done((bf16[64,3328]{1,0:T(8,128)(2,1)S(1)}, bf16[64,3328]{1,0:T(8,128)(2,1)S(1)}, u32[]{:S(2)}, u32[]{:S(2)}) %collective-permute-start.3) | collective-permute-done | bytes 426016 | tf_op jit(solution)/shard_map/ppermute | solution.py:501
  48.9 0.8 collective-permute-done.2.refs_1_
  49.7 2.0 %shard_map.49 = (f32[256,256]{1,0:T(8,128)S(1)}, f32[256,256]{1,0:T(8,128)S(1)}) custom-call(s32[4]{0:T(128)S(1)} %pad_add_fusion.at_ref.refs_0_, bf16[256,3328]{1,0:T(8,128)(2,1)S(1)} %get-tuple-element.37.mine_ref, bf16[256,3328]{1,0:T(8,128)(2,1)S(1)} %collective-permute-done.1.other_ref, bf16[64,3328]{1,0:T(8,128)(2,1)S(1)} %bitcast.18, ...), custom_call_target="tpu_custom_call" | custom-call | flops 872415232 | bytes 5111808 | tf_op jit(solution)/shard_map/pallas_call | solution.py:163
  51.7 2.2 %collective-permute-start.5 = (f32[256,256]{1,0:T(8,128)S(1)}, f32[256,256]{1,0:T(8,128)S(1)}, u32[]{:S(2)}, u32[]{:S(2)}) collective-permute-start(f32[256,256]{1,0:T(8,128)S(1)} %get-tuple-element.41), channel_id=1, source_target_pairs={{0,4},{4,0},{1,5},{5,1},{2,6},{6,2},{3,7},{7,3},{8,12},{12,8},{9,1... | collective-permute-start | bytes 786440 | tf_op jit(solution)/shard_map/ppermute | solution.py:497
  53.9 1.2 collective-permute-done.5.two_ref
  55.7 1.3 collective-permute-start.6
  56.9 2.5 %collective-permute-start.7 = (f32[64,256]{1,0:T(8,128)S(1)}, f32[64,256]{1,0:T(8,128)S(1)}, u32[]{:S(2)}, u32[]{:S(2)}) collective-permute-start(f32[64,256]{1,0:T(8,128)S(1)} %get-tuple-element.44), channel_id=1, source_target_pairs={{2,0},{3,1},{0,2},{1,3},{6,4},{7,5},{4,6},{5,7},{10,8},{11,9},{8,1... | collective-permute-start | bytes 196616 | tf_op jit(solution)/shard_map/ppermute | solution.py:501
  59.4 1.1 collective-permute-start.8
  60.5 1.8 collective-permute-done.7.two_ref
  62.9 3.2 %collective-permute-start.10 = (f32[64,256]{1,0:T(8,128)S(1)}, f32[64,256]{1,0:T(8,128)S(1)}, u32[]{:S(2)}, u32[]{:S(2)}) collective-permute-start(f32[64,256]{1,0:T(8,128)S(1)} %bitcast.23), channel_id=1, source_target_pairs={{2,0},{3,1},{0,2},{1,3},{6,4},{7,5},{4,6},{5,7},{10,8},{11,9},{8,1... | collective-permute-start | bytes 196616 | tf_op jit(solution)/shard_map/ppermute | solution.py:501
  66.5 0.7 collective-permute-done.11.three_ref
  67.2 1.3 collective-permute-done.10.two_ref
  68.5 1.1 collective-permute-done.9.one_ref
  69.6 1.0 shard_map.52
  70.6 3.6 %collective-permute-start.13 = (f32[256,256]{1,0:T(8,128)S(1)}, f32[256,256]{1,0:T(8,128)S(1)}, u32[]{:S(2)}, u32[]{:S(2)}) collective-permute-start(f32[256,256]{1,0:T(8,128)S(1)} %get-tuple-element.48.refs_0_.left_mine_ref), channel_id=1, source_target_pairs={{0,4},{4,0},{1,5},{5,1},{2,6},{6,2},{3,7},{7,3},{8,12},{12,8},{9,1... | collective-permute-start | bytes 786440 | tf_op jit(solution)/shard_map/ppermute | solution.py:497
  74.3 1.1 collective-permute-done.12.two_ref
  75.4 1.0 collective-permute-start.16
  76.3 2.1 %collective-permute-start.15 = (f32[32,256]{1,0:T(8,128)S(1)}, f32[32,256]{1,0:T(8,128)S(1)}, u32[]{:S(2)}, u32[]{:S(2)}) collective-permute-start(f32[32,256]{1,0:T(8,128)S(1)} %shard_map.53.own_ref), channel_id=1, source_target_pairs={{16,0},{24,8},{0,16},{8,24},{17,1},{25,9},{1,17},{9,25},{18,2},{26... | collective-permute-start | bytes 98312 | tf_op jit(solution)/shard_map/ppermute | solution.py:501
  78.4 1.4 collective-permute-start.14
  79.8 4.0 %shard_map.58 = (f32[832,256]{1,0:T(8,128)S(1)}, f32[832,256]{1,0:T(8,128)S(1)}, f32[832,256]{1,0:T(8,128)S(1)}, f32[832,256]{1,0:T(8,128)S(1)}) custom-call(s32[4]{0:T(128)S(1)} %pad_add_fusion.at_ref.refs_0_, bf16[256,3328]{1,0:T(8,128)(2,1)S(1)} %get-tuple-element.37.mine_ref, bf16[256,3328]{1,0:T(8,128)(2,1)S(1)} %collective-permute-done.1.other_ref, ...), custom_call_target="tpu_custom_call" | custom-call | flops 2617245696 | bytes 10223616 | tf_op jit(solution)/shard_map/pallas_call | solution.py:315
  84.0 1.1 collective-permute-start.22
  85.1 1.6 collective-permute-start.23
  86.7 11.9 %all_to_all.26.pieces_ref = f32[8,32,256]{2,1,0:T(8,128)S(1)} all-to-all(f32[8,32,256]{2,1,0:T(8,128)S(1)} %shard_map.54), channel_id=1, replica_groups=mesh['z'=8,'y'=4,'c'=2,'x'=4] {'z'}, dimensions={0} | all-to-all | bytes 524288 | tf_op jit(solution)/shard_map/all_to_all | solution.py:517
  98.6 3.4 %collective-permute-start.17 = (f32[32,256]{1,0:T(8,128)S(1)}, f32[32,256]{1,0:T(8,128)S(1)}, u32[]{:S(2)}, u32[]{:S(2)}) collective-permute-start(f32[32,256]{1,0:T(8,128)S(1)} %bitcast.20), channel_id=1, source_target_pairs={{0,4},{4,0},{1,5},{5,1},{2,6},{6,2},{3,7},{7,3},{8,12},{12,8},{9,1... | collective-permute-start | bytes 98312 | tf_op jit(solution)/shard_map/ppermute | solution.py:497
  102.0 0.9 collective-permute-done.17
  102.9 2.5 %collective-permute-start.19 = (f32[64,256]{1,0:T(8,128)S(1)}, f32[64,256]{1,0:T(8,128)S(1)}, u32[]{:S(2)}, u32[]{:S(2)}) collective-permute-start(f32[64,256]{1,0:T(8,128)S(1)} %pad_maximum_fusion.own_ref), channel_id=1, source_target_pairs={{2,0},{3,1},{0,2},{1,3},{6,4},{7,5},{4,6},{5,7},{10,8},{11,9},{8,1... | collective-permute-start | bytes 196616 | tf_op jit(solution)/shard_map/ppermute | solution.py:501
  105.4 2.6 %collective-permute-done.20.last_ref = f32[64,256]{1,0:T(8,128)S(1)} collective-permute-done((f32[64,256]{1,0:T(8,128)S(1)}, f32[64,256]{1,0:T(8,128)S(1)}, u32[]{:S(2)}, u32[]{:S(2)}) %collective-permute-start.20) | collective-permute-done | bytes 65568 | tf_op jit(solution)/shard_map/ppermute | solution.py:501
  108.6 2.7 %collective-permute-done.18.next_ref = f32[64,256]{1,0:T(8,128)S(1)} collective-permute-done((f32[64,256]{1,0:T(8,128)S(1)}, f32[64,256]{1,0:T(8,128)S(1)}, u32[]{:S(2)}, u32[]{:S(2)}) %collective-permute-start.18) | collective-permute-done | bytes 65568 | tf_op jit(solution)/shard_map/ppermute | solution.py:501
  111.4 9.9 %shard_map.56.inverse_ref = f32[256,256]{1,0:T(8,128)S(1)} custom-call(s32[4]{0:T(128)S(1)} %pad_add_fusion.at_ref.refs_0_, f32[64,256]{1,0:T(8,128)S(1)} %pad_maximum_fusion.own_ref, f32[64,256]{1,0:T(8,128)S(1)} %collective-permute-done.18.next_ref, f32[64,256]{1,0:T(8,128)S(1)} %collective-permute-done.19.across_ref, ...), custom_call_target="tpu_custom_call" | custom-call | flops 1000000000 | bytes 1048576 | tf_op jit(solution)/shard_map/pallas_call | solution.py:127
  121.4 2.0 %collective-permute-done.23.refs_3_ = f32[832,256]{1,0:T(8,128)S(1)} collective-permute-done((f32[832,256]{1,0:T(8,128)S(1)}, f32[832,256]{1,0:T(8,128)S(1)}, u32[]{:S(2)}, u32[]{:S(2)}) %collective-permute-start.23) | collective-permute-done | bytes 852000 | tf_op jit(solution)/shard_map/ppermute | solution.py:501
  123.3 0.9 shard_map.59
  124.3 14.6 %all_to_all.27.pieces_ref = bf16[8,104,256]{2,1,0:T(8,128)(2,1)S(1)} all-to-all(bf16[8,104,256]{2,1,0:T(8,128)(2,1)S(1)} %bitcast.19), channel_id=1, replica_groups=mesh['z'=8,'y'=4,'c'=2,'x'=4] {'z'}, dimensions={0} | all-to-all | bytes 851968 | tf_op jit(solution)/shard_map/all_to_all | solution.py:517
  139.0 15.7 %all_to_all.28 = bf16[8,104,256]{2,1,0:T(8,128)(2,1)S(1)} all-to-all(bf16[8,104,256]{2,1,0:T(8,128)(2,1)S(1)} %shard_map.60), channel_id=1, replica_groups=mesh['z'=8,'y'=4,'c'=2,'x'=4] {'z'}, dimensions={0} | all-to-all | bytes 851968 | tf_op jit(solution)/shard_map/all_to_all | solution.py:517
  154.7 3.9 %collective-permute-start.25 = (bf16[832,256]{1,0:T(8,128)(2,1)S(1)}, bf16[832,256]{1,0:T(8,128)(2,1)S(1)}, u32[]{:S(2)}, u32[]{:S(2)}) collective-permute-start(bf16[832,256]{1,0:T(8,128)(2,1)S(1)} %bitcast.9), channel_id=1, source_target_pairs={{24,0},{0,8},{8,16},{16,24},{25,1},{1,9},{9,17},{17,25},{26,2},{2,... | collective-permute-start | bytes 1277960 | tf_op jit(solution)/shard_map/ppermute | solution.py:501
  159.0 16.0 %all_to_all.29.refs_3_ = f32[32,1,256]{2,1,0:T(1,128)S(1)} all-to-all(f32[32,1,256]{2,1,0:T(1,128)S(1)} %shard_map.61), channel_id=1, replica_groups=mesh['z'=8,'y'=4,'c'=2,'x'=4] {'y','c','x'}, dimensions={0} | all-to-all | bytes 65536 | tf_op jit(solution)/shard_map/all_to_all | solution.py:517
  176.5 2.3 %collective-permute-start.30 = (bf16[416,256]{1,0:T(8,128)(2,1)S(1)}, bf16[416,256]{1,0:T(8,128)(2,1)S(1)}, u32[]{:S(2)}, u32[]{:S(2)}) collective-permute-start(bf16[416,256]{1,0:T(8,128)(2,1)S(1)} %slice.7), channel_id=1, source_target_pairs={{8,0},{16,8},{24,16},{0,24},{9,1},{17,9},{25,17},{1,25},{10,2},{18... | collective-permute-start | bytes 638984 | tf_op jit(solution)/shard_map/ppermute | solution.py:501
  179.3 6.2 %shard_map.62 = (bf16[256,6656]{1,0:T(8,128)(2,1)}, bf16[256,6656]{1,0:T(8,128)(2,1)}, f32[4,6656]{1,0:T(4,128)}) custom-call(s32[4]{0:T(128)S(1)} %pad_add_fusion.at_ref.refs_0_, bf16[256,6656]{1,0:T(8,128)(2,1)S(1)} %copy-done, f32[256,256]{1,0:T(8,128)S(1)} %shard_map.57.refs_2_, f32[32,1,256]{2,1,0:T(1,128)S(1)} %all_to_all.29.refs_3_, ...), custom_call_target="tpu_custom_call" | custom-call | flops 1308622848 | bytes 10223616 | tf_op jit(solution)/shard_map/pallas_call | solution.py:461
  185.5 0.8 collective-permute-start.31
  186.4 1.0 collective-permute-done.31.refs_12_
  187.7 3.2 %shard_map.63 = (bf16[256,6656]{1,0:T(8,128)(2,1)}, bf16[256,6656]{1,0:T(8,128)(2,1)}, f32[4,6656]{1,0:T(4,128)}) custom-call(s32[4]{0:T(128)S(1)} %pad_add_fusion.at_ref.refs_0_, bf16[256,6656]{1,0:T(8,128)(2,1)S(1)} %copy-done, f32[256,256]{1,0:T(8,128)S(1)} %shard_map.57.refs_2_, ...), custom_call_target="tpu_custom_call", output_to_operand_aliasing={{0}: (14, {}), {1}: (15, {}), {2}: (16, {})} | custom-call | flops 436207616 | bytes 3407872 | tf_op jit(solution)/shard_map/pallas_call | solution.py:479
  (50 shorter events, 5.7 us)
Async XLA Ops:
  1.7 5.5 %collective-permute-start = (bf16[4,3328]{1,0:T(4,128)(2,1)S(1)}, bf16[4,3328]{1,0:T(4,128)(2,1)S(1)}, u32[]{:S(2)}, u32[]{:S(2)}) collective-permute-start(bf16[4,3328]{1,0:T(4,128)(2,1)S(1)} %constant_dynamic-slice_fusion.2), channel_id=1, source_target_pairs={{0,4},{4,0},{1,5},{5,1},{2,6},{6,2},{3,7},{7,3},{8,12},{12,8},{9,1... | collective-permute-start | bytes 79880 | tf_op jit(solution)/shard_map/ppermute | solution.py:497
  7.1 42.5 %collective-permute-start.1 = (bf16[256,3328]{1,0:T(8,128)(2,1)S(1)}, bf16[256,3328]{1,0:T(8,128)(2,1)S(1)}, u32[]{:S(2)}, u32[]{:S(2)}) collective-permute-start(bf16[256,3328]{1,0:T(8,128)(2,1)S(1)} %get-tuple-element.38), channel_id=1, source_target_pairs={{0,4},{4,0},{1,5},{5,1},{2,6},{6,2},{3,7},{7,3},{8,12},{12,8},{9,1... | collective-permute-start | bytes 5111816 | tf_op jit(solution)/shard_map/ppermute | solution.py:497
  28.0 10.7 %collective-permute-start.4 = (bf16[64,3328]{1,0:T(8,128)(2,1)S(1)}, bf16[64,3328]{1,0:T(8,128)(2,1)S(1)}, u32[]{:S(2)}, u32[]{:S(2)}) collective-permute-start(bf16[64,3328]{1,0:T(8,128)(2,1)S(1)} %bitcast.15), channel_id=1, source_target_pairs={{24,0},{0,8},{8,16},{16,24},{25,1},{1,9},{9,17},{17,25},{26,2},{2,... | collective-permute-start | bytes 1277960 | tf_op jit(solution)/shard_map/ppermute | solution.py:501
  29.3 19.6 %collective-permute-start.3 = (bf16[64,3328]{1,0:T(8,128)(2,1)S(1)}, bf16[64,3328]{1,0:T(8,128)(2,1)S(1)}, u32[]{:S(2)}, u32[]{:S(2)}) collective-permute-start(bf16[64,3328]{1,0:T(8,128)(2,1)S(1)} %bitcast.16), channel_id=1, source_target_pairs={{16,0},{24,8},{0,16},{8,24},{17,1},{25,9},{1,17},{9,25},{18,2},{26... | collective-permute-start | bytes 1277960 | tf_op jit(solution)/shard_map/ppermute | solution.py:501
  31.9 17.8 %collective-permute-start.2 = (bf16[64,3328]{1,0:T(8,128)(2,1)S(1)}, bf16[64,3328]{1,0:T(8,128)(2,1)S(1)}, u32[]{:S(2)}, u32[]{:S(2)}) collective-permute-start(bf16[64,3328]{1,0:T(8,128)(2,1)S(1)} %bitcast.17), channel_id=1, source_target_pairs={{8,0},{16,8},{24,16},{0,24},{9,1},{17,9},{25,17},{1,25},{10,2},{18... | collective-permute-start | bytes 1277960 | tf_op jit(solution)/shard_map/ppermute | solution.py:501
  51.7 3.4 %collective-permute-start.5 = (f32[256,256]{1,0:T(8,128)S(1)}, f32[256,256]{1,0:T(8,128)S(1)}, u32[]{:S(2)}, u32[]{:S(2)}) collective-permute-start(f32[256,256]{1,0:T(8,128)S(1)} %get-tuple-element.41), channel_id=1, source_target_pairs={{0,4},{4,0},{1,5},{5,1},{2,6},{6,2},{3,7},{7,3},{8,12},{12,8},{9,1... | collective-permute-start | bytes 786440 | tf_op jit(solution)/shard_map/ppermute | solution.py:497
  55.7 4.9 %collective-permute-start.6 = (f32[64,256]{1,0:T(8,128)S(1)}, f32[64,256]{1,0:T(8,128)S(1)}, u32[]{:S(2)}, u32[]{:S(2)}) collective-permute-start(f32[64,256]{1,0:T(8,128)S(1)} %get-tuple-element.43), channel_id=1, source_target_pairs={{3,0},{0,1},{1,2},{2,3},{7,4},{4,5},{5,6},{6,7},{11,8},{8,9},{9,10... | collective-permute-start | bytes 196616 | tf_op jit(solution)/shard_map/ppermute | solution.py:501
  56.9 5.4 %collective-permute-start.7 = (f32[64,256]{1,0:T(8,128)S(1)}, f32[64,256]{1,0:T(8,128)S(1)}, u32[]{:S(2)}, u32[]{:S(2)}) collective-permute-start(f32[64,256]{1,0:T(8,128)S(1)} %get-tuple-element.44), channel_id=1, source_target_pairs={{2,0},{3,1},{0,2},{1,3},{6,4},{7,5},{4,6},{5,7},{10,8},{11,9},{8,1... | collective-permute-start | bytes 196616 | tf_op jit(solution)/shard_map/ppermute | solution.py:501
  59.4 3.4 %collective-permute-start.8 = (f32[64,256]{1,0:T(8,128)S(1)}, f32[64,256]{1,0:T(8,128)S(1)}, u32[]{:S(2)}, u32[]{:S(2)}) collective-permute-start(f32[64,256]{1,0:T(8,128)S(1)} %get-tuple-element.45), channel_id=1, source_target_pairs={{1,0},{2,1},{3,2},{0,3},{5,4},{6,5},{7,6},{4,7},{9,8},{10,9},{11,1... | collective-permute-start | bytes 196616 | tf_op jit(solution)/shard_map/ppermute | solution.py:501
  62.8 4.4 %collective-permute-start.11 = (f32[64,256]{1,0:T(8,128)S(1)}, f32[64,256]{1,0:T(8,128)S(1)}, u32[]{:S(2)}, u32[]{:S(2)}) collective-permute-start(f32[64,256]{1,0:T(8,128)S(1)} %bitcast.22), channel_id=1, source_target_pairs={{3,0},{0,1},{1,2},{2,3},{7,4},{4,5},{5,6},{6,7},{11,8},{8,9},{9,10... | collective-permute-start | bytes 196616 | tf_op jit(solution)/shard_map/ppermute | solution.py:501
  62.9 5.6 %collective-permute-start.10 = (f32[64,256]{1,0:T(8,128)S(1)}, f32[64,256]{1,0:T(8,128)S(1)}, u32[]{:S(2)}, u32[]{:S(2)}) collective-permute-start(f32[64,256]{1,0:T(8,128)S(1)} %bitcast.23), channel_id=1, source_target_pairs={{2,0},{3,1},{0,2},{1,3},{6,4},{7,5},{4,6},{5,7},{10,8},{11,9},{8,1... | collective-permute-start | bytes 196616 | tf_op jit(solution)/shard_map/ppermute | solution.py:501
  66.1 3.4 %collective-permute-start.9 = (f32[64,256]{1,0:T(8,128)S(1)}, f32[64,256]{1,0:T(8,128)S(1)}, u32[]{:S(2)}, u32[]{:S(2)}) collective-permute-start(f32[64,256]{1,0:T(8,128)S(1)} %bitcast.24), channel_id=1, source_target_pairs={{1,0},{2,1},{3,2},{0,3},{5,4},{6,5},{7,6},{4,7},{9,8},{10,9},{11,1... | collective-permute-start | bytes 196616 | tf_op jit(solution)/shard_map/ppermute | solution.py:501
  70.6 4.8 %collective-permute-start.13 = (f32[256,256]{1,0:T(8,128)S(1)}, f32[256,256]{1,0:T(8,128)S(1)}, u32[]{:S(2)}, u32[]{:S(2)}) collective-permute-start(f32[256,256]{1,0:T(8,128)S(1)} %get-tuple-element.48.refs_0_.left_mine_ref), channel_id=1, source_target_pairs={{0,4},{4,0},{1,5},{5,1},{2,6},{6,2},{3,7},{7,3},{8,12},{12,8},{9,1... | collective-permute-start | bytes 786440 | tf_op jit(solution)/shard_map/ppermute | solution.py:497
  74.2 1.2 collective-permute-start.12
  75.4 9.7 %collective-permute-start.16 = (f32[32,256]{1,0:T(8,128)S(1)}, f32[32,256]{1,0:T(8,128)S(1)}, u32[]{:S(2)}, u32[]{:S(2)}) collective-permute-start(f32[32,256]{1,0:T(8,128)S(1)} %shard_map.53.own_ref), channel_id=1, source_target_pairs={{24,0},{0,8},{8,16},{16,24},{25,1},{1,9},{9,17},{17,25},{26,2},{2,... | collective-permute-start | bytes 98312 | tf_op jit(solution)/shard_map/ppermute | solution.py:501
  76.3 10.3 %collective-permute-start.15 = (f32[32,256]{1,0:T(8,128)S(1)}, f32[32,256]{1,0:T(8,128)S(1)}, u32[]{:S(2)}, u32[]{:S(2)}) collective-permute-start(f32[32,256]{1,0:T(8,128)S(1)} %shard_map.53.own_ref), channel_id=1, source_target_pairs={{16,0},{24,8},{0,16},{8,24},{17,1},{25,9},{1,17},{9,25},{18,2},{26... | collective-permute-start | bytes 98312 | tf_op jit(solution)/shard_map/ppermute | solution.py:501
  78.4 8.2 %collective-permute-start.14 = (f32[32,256]{1,0:T(8,128)S(1)}, f32[32,256]{1,0:T(8,128)S(1)}, u32[]{:S(2)}, u32[]{:S(2)}) collective-permute-start(f32[32,256]{1,0:T(8,128)S(1)} %shard_map.53.own_ref), channel_id=1, source_target_pairs={{8,0},{16,8},{24,16},{0,24},{9,1},{17,9},{25,17},{1,25},{10,2},{18... | collective-permute-start | bytes 98312 | tf_op jit(solution)/shard_map/ppermute | solution.py:501
  83.8 37.5 %collective-permute-start.21 = (f32[832,256]{1,0:T(8,128)S(1)}, f32[832,256]{1,0:T(8,128)S(1)}, u32[]{:S(2)}, u32[]{:S(2)}) collective-permute-start(f32[832,256]{1,0:T(8,128)S(1)} %get-tuple-element.52), channel_id=1, source_target_pairs={{24,0},{0,8},{8,16},{16,24},{25,1},{1,9},{9,17},{17,25},{26,2},{2,... | collective-permute-start | bytes 2555912 | tf_op jit(solution)/shard_map/ppermute | solution.py:501
  84.0 37.4 %collective-permute-start.22 = (f32[832,256]{1,0:T(8,128)S(1)}, f32[832,256]{1,0:T(8,128)S(1)}, u32[]{:S(2)}, u32[]{:S(2)}) collective-permute-start(f32[832,256]{1,0:T(8,128)S(1)} %get-tuple-element.53), channel_id=1, source_target_pairs={{16,0},{24,8},{0,16},{8,24},{17,1},{25,9},{1,17},{9,25},{18,2},{26... | collective-permute-start | bytes 2555912 | tf_op jit(solution)/shard_map/ppermute | solution.py:501
  85.1 38.3 %collective-permute-start.23 = (f32[832,256]{1,0:T(8,128)S(1)}, f32[832,256]{1,0:T(8,128)S(1)}, u32[]{:S(2)}, u32[]{:S(2)}) collective-permute-start(f32[832,256]{1,0:T(8,128)S(1)} %get-tuple-element.54), channel_id=1, source_target_pairs={{8,0},{16,8},{24,16},{0,24},{9,1},{17,9},{25,17},{1,25},{10,2},{18... | collective-permute-start | bytes 2555912 | tf_op jit(solution)/shard_map/ppermute | solution.py:501
  98.6 4.3 %collective-permute-start.17 = (f32[32,256]{1,0:T(8,128)S(1)}, f32[32,256]{1,0:T(8,128)S(1)}, u32[]{:S(2)}, u32[]{:S(2)}) collective-permute-start(f32[32,256]{1,0:T(8,128)S(1)} %bitcast.20), channel_id=1, source_target_pairs={{0,4},{4,0},{1,5},{5,1},{2,6},{6,2},{3,7},{7,3},{8,12},{12,8},{9,1... | collective-permute-start | bytes 98312 | tf_op jit(solution)/shard_map/ppermute | solution.py:497
  102.9 5.1 %collective-permute-start.20 = (f32[64,256]{1,0:T(8,128)S(1)}, f32[64,256]{1,0:T(8,128)S(1)}, u32[]{:S(2)}, u32[]{:S(2)}) collective-permute-start(f32[64,256]{1,0:T(8,128)S(1)} %pad_maximum_fusion.own_ref), channel_id=1, source_target_pairs={{3,0},{0,1},{1,2},{2,3},{7,4},{4,5},{5,6},{6,7},{11,8},{8,9},{9,10... | collective-permute-start | bytes 196616 | tf_op jit(solution)/shard_map/ppermute | solution.py:501
  102.9 5.8 %collective-permute-start.19 = (f32[64,256]{1,0:T(8,128)S(1)}, f32[64,256]{1,0:T(8,128)S(1)}, u32[]{:S(2)}, u32[]{:S(2)}) collective-permute-start(f32[64,256]{1,0:T(8,128)S(1)} %pad_maximum_fusion.own_ref), channel_id=1, source_target_pairs={{2,0},{3,1},{0,2},{1,3},{6,4},{7,5},{4,6},{5,7},{10,8},{11,9},{8,1... | collective-permute-start | bytes 196616 | tf_op jit(solution)/shard_map/ppermute | solution.py:501
  107.9 3.4 %collective-permute-start.18 = (f32[64,256]{1,0:T(8,128)S(1)}, f32[64,256]{1,0:T(8,128)S(1)}, u32[]{:S(2)}, u32[]{:S(2)}) collective-permute-start(f32[64,256]{1,0:T(8,128)S(1)} %pad_maximum_fusion.own_ref), channel_id=1, source_target_pairs={{1,0},{2,1},{3,2},{0,3},{5,4},{6,5},{7,6},{4,7},{9,8},{10,9},{11,1... | collective-permute-start | bytes 196616 | tf_op jit(solution)/shard_map/ppermute | solution.py:501
  123.3 55.9 %copy-start = (bf16[256,6656]{1,0:T(8,128)(2,1)S(1)}, bf16[256,6656]{1,0:T(8,128)(2,1)}, u32[]{:S(2)}) copy-start(bf16[256,6656]{1,0:T(8,128)(2,1)} %refs_1_.3) | copy-start | bytes 10223620
  154.7 20.4 %collective-permute-start.25 = (bf16[832,256]{1,0:T(8,128)(2,1)S(1)}, bf16[832,256]{1,0:T(8,128)(2,1)S(1)}, u32[]{:S(2)}, u32[]{:S(2)}) collective-permute-start(bf16[832,256]{1,0:T(8,128)(2,1)S(1)} %bitcast.9), channel_id=1, source_target_pairs={{24,0},{0,8},{8,16},{16,24},{25,1},{1,9},{9,17},{17,25},{26,2},{2,... | collective-permute-start | bytes 1277960 | tf_op jit(solution)/shard_map/ppermute | solution.py:501
  158.6 16.5 %collective-permute-start.24 = (bf16[832,256]{1,0:T(8,128)(2,1)S(1)}, bf16[832,256]{1,0:T(8,128)(2,1)S(1)}, u32[]{:S(2)}, u32[]{:S(2)}) collective-permute-start(bf16[832,256]{1,0:T(8,128)(2,1)S(1)} %bitcast.10), channel_id=1, source_target_pairs={{8,0},{16,8},{24,16},{0,24},{9,1},{17,9},{25,17},{1,25},{10,2},{18... | collective-permute-start | bytes 1277960 | tf_op jit(solution)/shard_map/ppermute | solution.py:501
  175.1 4.1 %collective-permute-start.26 = (bf16[832,256]{1,0:T(8,128)(2,1)S(1)}, bf16[832,256]{1,0:T(8,128)(2,1)S(1)}, u32[]{:S(2)}, u32[]{:S(2)}) collective-permute-start(bf16[832,256]{1,0:T(8,128)(2,1)S(1)} %bitcast.12), channel_id=1, source_target_pairs={{0,4},{4,0},{1,5},{5,1},{2,6},{6,2},{3,7},{7,3},{8,12},{12,8},{9,1... | collective-permute-start | bytes 1277960 | tf_op jit(solution)/shard_map/ppermute | solution.py:497
  175.5 3.7 %collective-permute-start.27 = (bf16[832,256]{1,0:T(8,128)(2,1)S(1)}, bf16[832,256]{1,0:T(8,128)(2,1)S(1)}, u32[]{:S(2)}, u32[]{:S(2)}) collective-permute-start(bf16[832,256]{1,0:T(8,128)(2,1)S(1)} %collective-permute-done.24.refs_5_), channel_id=1, source_target_pairs={{0,4},{4,0},{1,5},{5,1},{2,6},{6,2},{3,7},{7,3},{8,12},{12,8},{9,1... | collective-permute-start | bytes 1277960 | tf_op jit(solution)/shard_map/ppermute | solution.py:497
  175.6 3.6 %collective-permute-start.28 = (bf16[832,256]{1,0:T(8,128)(2,1)S(1)}, bf16[832,256]{1,0:T(8,128)(2,1)S(1)}, u32[]{:S(2)}, u32[]{:S(2)}) collective-permute-start(bf16[832,256]{1,0:T(8,128)(2,1)S(1)} %collective-permute-done.25.refs_6_), channel_id=1, source_target_pairs={{0,4},{4,0},{1,5},{5,1},{2,6},{6,2},{3,7},{7,3},{8,12},{12,8},{9,1... | collective-permute-start | bytes 1277960 | tf_op jit(solution)/shard_map/ppermute | solution.py:497
  176.0 9.4 %collective-permute-start.29 = (bf16[416,256]{1,0:T(8,128)(2,1)S(1)}, bf16[416,256]{1,0:T(8,128)(2,1)S(1)}, u32[]{:S(2)}, u32[]{:S(2)}) collective-permute-start(bf16[416,256]{1,0:T(8,128)(2,1)S(1)} %slice.6), channel_id=1, source_target_pairs={{24,0},{0,8},{8,16},{16,24},{25,1},{1,9},{9,17},{17,25},{26,2},{2,... | collective-permute-start | bytes 638984 | tf_op jit(solution)/shard_map/ppermute | solution.py:501
  176.5 9.0 %collective-permute-start.30 = (bf16[416,256]{1,0:T(8,128)(2,1)S(1)}, bf16[416,256]{1,0:T(8,128)(2,1)S(1)}, u32[]{:S(2)}, u32[]{:S(2)}) collective-permute-start(bf16[416,256]{1,0:T(8,128)(2,1)S(1)} %slice.7), channel_id=1, source_target_pairs={{8,0},{16,8},{24,16},{0,24},{9,1},{17,9},{25,17},{1,25},{10,2},{18... | collective-permute-start | bytes 638984 | tf_op jit(solution)/shard_map/ppermute | solution.py:501
  185.5 1.9 collective-permute-start.31
  186.3 1.5 collective-permute-start.32

commit v8 on v7

--- a/solution.py
+++ b/solution.py
@@ -550,7 +550,8 @@
     projected, gram_keep, gram_send = gram_rows_of(at, all_of_four(block, "x"))
 
     gram_rows = add(gram_keep, swap_cores(gram_send))
-    gram_rows, proj_swapped = lax.optimization_barrier((gram_rows, swap_cores(projected)))
+    gram_rows, projected = lax.optimization_barrier((gram_rows, projected))
+    proj_swapped = swap_cores(projected)
     gram_rows = all_of_four(gram_rows, "y")
     gram_rows = sum_copies(exchange(sum_four_copies(gram_rows, NZ), "z"), 1)[0]
     gram_chip = jnp.concatenate([gram_rows, swap_cores(gram_rows)])

time: 191 us -> 191 us (level)
  no operation moved by 1% of the time
where the time goes in v8:
time: 191 us
  blocking collectives  78.6 us (41%)
  starting transfers between devices  45.4 us (24%)
  waiting for transfers between devices  34.3 us (18%)
  Pallas kernels  28.5 us (15%)
  local copies, waits for them, and re-layouts  2.27 us (1%)
    all_to_all x5, blocking collectives, exchange(): return lax.all_to_all(pieces, axes, 0, 0)  78.6 us
    ppermute x22, starting transfers between devices, from_ahead(): lax.ppermute(block, axis, [((i + by) % parts, i) for i in range(parts)])  30.3 us
    ppermute x22, waiting for transfers between devices, from_ahead(): lax.ppermute(block, axis, [((i + by) % parts, i) for i in range(parts)])  30 us
    ppermute x11, starting transfers between devices, swap_cores(): return lax.ppermute(block, 'c', [(0, 1), (1, 0)])  15.1 us
    pallas_call x1, Pallas kernels, inverse_factor(): pl.pallas_call(inverse_factor_kernel, out_shape=jax.ShapeDtypeStruct((ran...  9.93 us
    pallas_call x1, Pallas kernels, finish(): pl.pallas_call(lambda *refs: first_kernel(scaling, *refs), out_shape=outs...  6.2 us
    ppermute x11, waiting for transfers between devices, swap_cores(): return lax.ppermute(block, 'c', [(0, 1), (1, 0)])  4.26 us
    pallas_call x1, Pallas kernels, cross(): pl.pallas_call(cross_kernel, out_shape=[jax.ShapeDtypeStruct((cols // NY,...  3.98 us
  transfers between devices with their start and end apart: 33, of which 18 were waited for; matrix products, arithmetic and copies ran while one was open for 1% of the time, Pallas kernels for 11%

profile of v8, /device:TPU:1, one launch (start us, length us, event | category | flops | bytes accessed | tf_op | source)
XLA Modules:
  0.0 191.1 jit_solution(11023167600701641054)
XLA Ops:
  0.6 0.9 convert_element_type.3
  1.7 3.3 %collective-permute-start = (bf16[4,3328]{1,0:T(4,128)(2,1)S(1)}, bf16[4,3328]{1,0:T(4,128)(2,1)S(1)}, u32[]{:S(2)}, u32[]{:S(2)}) collective-permute-start(bf16[4,3328]{1,0:T(4,128)(2,1)S(1)} %constant_dynamic-slice_fusion.2), channel_id=1, source_target_pairs={{0,4},{4,0},{1,5},{5,1},{2,6},{6,2},{3,7},{7,3},{8,12},{12,8},{9,1... | collective-permute-start | bytes 79880 | tf_op jit(solution)/shard_map/ppermute | solution.py:497
  4.9 2.2 %constant_dynamic-slice_fusion = (bf16[256,3328]{1,0:T(8,128)(2,1)S(1)}, bf16[256,3328]{1,0:T(8,128)(2,1)S(1)}) fusion(bf16[256,6656]{1,0:T(8,128)(2,1)} %refs_1_.3, s32[]{:T(128)S(6)} %select_n.20, s32[]{:T(128)S(6)} %select_n.21), kind=kLoop, calls=%fused_computation.4 | loop fusion | bytes 6815752 | tf_op jit(solution)/shard_map/dynamic_slice | solution.py:531
  7.4 20.6 %all_to_all.25 = bf16[8,8,3328]{2,1,0:T(8,128)(2,1)S(1)} all-to-all(bf16[8,8,3328]{2,1,0:T(8,128)(2,1)S(1)} %broadcast_in_dim.2), channel_id=1, replica_groups=mesh['z'=8,'y'=4,'c'=2,'x'=4] {'z'}, dimensions={0} | all-to-all | bytes 851968 | tf_op jit(solution)/shard_map/all_to_all | solution.py:517
  28.0 1.3 collective-permute-start.4
  29.3 2.6 %collective-permute-start.3 = (bf16[64,3328]{1,0:T(8,128)(2,1)S(1)}, bf16[64,3328]{1,0:T(8,128)(2,1)S(1)}, u32[]{:S(2)}, u32[]{:S(2)}) collective-permute-start(bf16[64,3328]{1,0:T(8,128)(2,1)S(1)} %bitcast.16), channel_id=1, source_target_pairs={{16,0},{24,8},{0,16},{8,24},{17,1},{25,9},{1,17},{9,25},{18,2},{26... | collective-permute-start | bytes 1277960 | tf_op jit(solution)/shard_map/ppermute | solution.py:501
  31.9 1.1 collective-permute-start.2
  33.0 5.7 %collective-permute-done.4.refs_3_ = bf16[64,3328]{1,0:T(8,128)(2,1)S(1)} collective-permute-done((bf16[64,3328]{1,0:T(8,128)(2,1)S(1)}, bf16[64,3328]{1,0:T(8,128)(2,1)S(1)}, u32[]{:S(2)}, u32[]{:S(2)}) %collective-permute-start.4) | collective-permute-done | bytes 426016 | tf_op jit(solution)/shard_map/ppermute | solution.py:501
  38.6 10.2 %collective-permute-done.3.refs_2_ = bf16[64,3328]{1,0:T(8,128)(2,1)S(1)} collective-permute-done((bf16[64,3328]{1,0:T(8,128)(2,1)S(1)}, bf16[64,3328]{1,0:T(8,128)(2,1)S(1)}, u32[]{:S(2)}, u32[]{:S(2)}) %collective-permute-start.3) | collective-permute-done | bytes 426016 | tf_op jit(solution)/shard_map/ppermute | solution.py:501
  48.9 0.8 collective-permute-done.2.refs_1_
  49.7 2.0 %shard_map.49 = (f32[256,256]{1,0:T(8,128)S(1)}, f32[256,256]{1,0:T(8,128)S(1)}) custom-call(s32[4]{0:T(128)S(1)} %pad_add_fusion.at_ref.refs_0_, bf16[256,3328]{1,0:T(8,128)(2,1)S(1)} %get-tuple-element.37.mine_ref, bf16[256,3328]{1,0:T(8,128)(2,1)S(1)} %collective-permute-done.1.other_ref, bf16[64,3328]{1,0:T(8,128)(2,1)S(1)} %bitcast.18, ...), custom_call_target="tpu_custom_call" | custom-call | flops 872415232 | bytes 5111808 | tf_op jit(solution)/shard_map/pallas_call | solution.py:163
  51.7 2.2 %collective-permute-start.5 = (f32[256,256]{1,0:T(8,128)S(1)}, f32[256,256]{1,0:T(8,128)S(1)}, u32[]{:S(2)}, u32[]{:S(2)}) collective-permute-start(f32[256,256]{1,0:T(8,128)S(1)} %get-tuple-element.41), channel_id=1, source_target_pairs={{0,4},{4,0},{1,5},{5,1},{2,6},{6,2},{3,7},{7,3},{8,12},{12,8},{9,1... | collective-permute-start | bytes 786440 | tf_op jit(solution)/shard_map/ppermute | solution.py:497
  53.9 1.2 collective-permute-done.5.two_ref
  55.7 1.3 collective-permute-start.6
  56.9 2.5 %collective-permute-start.7 = (f32[64,256]{1,0:T(8,128)S(1)}, f32[64,256]{1,0:T(8,128)S(1)}, u32[]{:S(2)}, u32[]{:S(2)}) collective-permute-start(f32[64,256]{1,0:T(8,128)S(1)} %get-tuple-element.44), channel_id=1, source_target_pairs={{2,0},{3,1},{0,2},{1,3},{6,4},{7,5},{4,6},{5,7},{10,8},{11,9},{8,1... | collective-permute-start | bytes 196616 | tf_op jit(solution)/shard_map/ppermute | solution.py:501
  59.4 1.1 collective-permute-start.8
  60.5 1.8 collective-permute-done.7.two_ref
  62.9 3.2 %collective-permute-start.10 = (f32[64,256]{1,0:T(8,128)S(1)}, f32[64,256]{1,0:T(8,128)S(1)}, u32[]{:S(2)}, u32[]{:S(2)}) collective-permute-start(f32[64,256]{1,0:T(8,128)S(1)} %bitcast.23), channel_id=1, source_target_pairs={{2,0},{3,1},{0,2},{1,3},{6,4},{7,5},{4,6},{5,7},{10,8},{11,9},{8,1... | collective-permute-start | bytes 196616 | tf_op jit(solution)/shard_map/ppermute | solution.py:501
  66.5 0.7 collective-permute-done.11.three_ref
  67.2 1.3 collective-permute-done.10.two_ref
  68.5 1.1 collective-permute-done.9.one_ref
  69.6 1.0 shard_map.52
  70.6 3.6 %collective-permute-start.12 = (f32[32,256]{1,0:T(8,128)S(1)}, f32[32,256]{1,0:T(8,128)S(1)}, u32[]{:S(2)}, u32[]{:S(2)}) collective-permute-start(f32[32,256]{1,0:T(8,128)S(1)} %get-tuple-element.47), channel_id=1, source_target_pairs={{0,4},{4,0},{1,5},{5,1},{2,6},{6,2},{3,7},{7,3},{8,12},{12,8},{9,1... | collective-permute-start | bytes 98312 | tf_op jit(solution)/shard_map/ppermute | solution.py:497
  74.2 0.9 collective-permute-done.12.two_ref
  75.4 0.9 collective-permute-start.15
  76.2 2.1 %collective-permute-start.14 = (f32[32,256]{1,0:T(8,128)S(1)}, f32[32,256]{1,0:T(8,128)S(1)}, u32[]{:S(2)}, u32[]{:S(2)}) collective-permute-start(f32[32,256]{1,0:T(8,128)S(1)} %shard_map.53.own_ref), channel_id=1, source_target_pairs={{16,0},{24,8},{0,16},{8,24},{17,1},{25,9},{1,17},{9,25},{18,2},{26... | collective-permute-start | bytes 98312 | tf_op jit(solution)/shard_map/ppermute | solution.py:501
  78.3 1.4 collective-permute-start.13
  79.7 4.0 %shard_map.58 = (f32[832,256]{1,0:T(8,128)S(1)}, f32[832,256]{1,0:T(8,128)S(1)}, f32[832,256]{1,0:T(8,128)S(1)}, f32[832,256]{1,0:T(8,128)S(1)}) custom-call(s32[4]{0:T(128)S(1)} %pad_add_fusion.at_ref.refs_0_, bf16[256,3328]{1,0:T(8,128)(2,1)S(1)} %get-tuple-element.37.mine_ref, bf16[256,3328]{1,0:T(8,128)(2,1)S(1)} %collective-permute-done.1.other_ref, ...), custom_call_target="tpu_custom_call" | custom-call | flops 2617245696 | bytes 10223616 | tf_op jit(solution)/shard_map/pallas_call | solution.py:315
  83.9 1.1 collective-permute-start.22
  85.0 1.6 collective-permute-start.23
  86.6 11.6 %all_to_all.26.pieces_ref = f32[8,32,256]{2,1,0:T(8,128)S(1)} all-to-all(f32[8,32,256]{2,1,0:T(8,128)S(1)} %shard_map.54), channel_id=1, replica_groups=mesh['z'=8,'y'=4,'c'=2,'x'=4] {'z'}, dimensions={0} | all-to-all | bytes 524288 | tf_op jit(solution)/shard_map/all_to_all | solution.py:517
  98.2 3.7 %collective-permute-start.16 = (f32[32,256]{1,0:T(8,128)S(1)}, f32[32,256]{1,0:T(8,128)S(1)}, u32[]{:S(2)}, u32[]{:S(2)}) collective-permute-start(f32[32,256]{1,0:T(8,128)S(1)} %bitcast.20), channel_id=1, source_target_pairs={{0,4},{4,0},{1,5},{5,1},{2,6},{6,2},{3,7},{7,3},{8,12},{12,8},{9,1... | collective-permute-start | bytes 98312 | tf_op jit(solution)/shard_map/ppermute | solution.py:497
  102.0 0.9 collective-permute-done.16
  102.8 2.5 %collective-permute-start.18 = (f32[64,256]{1,0:T(8,128)S(1)}, f32[64,256]{1,0:T(8,128)S(1)}, u32[]{:S(2)}, u32[]{:S(2)}) collective-permute-start(f32[64,256]{1,0:T(8,128)S(1)} %pad_maximum_fusion.own_ref), channel_id=1, source_target_pairs={{2,0},{3,1},{0,2},{1,3},{6,4},{7,5},{4,6},{5,7},{10,8},{11,9},{8,1... | collective-permute-start | bytes 196616 | tf_op jit(solution)/shard_map/ppermute | solution.py:501
  105.3 2.6 %collective-permute-done.19.last_ref = f32[64,256]{1,0:T(8,128)S(1)} collective-permute-done((f32[64,256]{1,0:T(8,128)S(1)}, f32[64,256]{1,0:T(8,128)S(1)}, u32[]{:S(2)}, u32[]{:S(2)}) %collective-permute-start.19) | collective-permute-done | bytes 65568 | tf_op jit(solution)/shard_map/ppermute | solution.py:501
  108.6 2.7 %collective-permute-done.17.next_ref = f32[64,256]{1,0:T(8,128)S(1)} collective-permute-done((f32[64,256]{1,0:T(8,128)S(1)}, f32[64,256]{1,0:T(8,128)S(1)}, u32[]{:S(2)}, u32[]{:S(2)}) %collective-permute-start.17) | collective-permute-done | bytes 65568 | tf_op jit(solution)/shard_map/ppermute | solution.py:501
  111.3 9.9 %shard_map.56.inverse_ref = f32[256,256]{1,0:T(8,128)S(1)} custom-call(s32[4]{0:T(128)S(1)} %pad_add_fusion.at_ref.refs_0_, f32[64,256]{1,0:T(8,128)S(1)} %pad_maximum_fusion.own_ref, f32[64,256]{1,0:T(8,128)S(1)} %collective-permute-done.17.next_ref, f32[64,256]{1,0:T(8,128)S(1)} %collective-permute-done.18.across_ref, ...), custom_call_target="tpu_custom_call" | custom-call | flops 1000000000 | bytes 1048576 | tf_op jit(solution)/shard_map/pallas_call | solution.py:127
  121.5 1.7 collective-permute-done.23.refs_3_
  123.3 0.9 shard_map.59
  124.2 14.6 %all_to_all.27.pieces_ref = bf16[8,104,256]{2,1,0:T(8,128)(2,1)S(1)} all-to-all(bf16[8,104,256]{2,1,0:T(8,128)(2,1)S(1)} %bitcast.19), channel_id=1, replica_groups=mesh['z'=8,'y'=4,'c'=2,'x'=4] {'z'}, dimensions={0} | all-to-all | bytes 851968 | tf_op jit(solution)/shard_map/all_to_all | solution.py:517
  138.9 15.7 %all_to_all.28 = bf16[8,104,256]{2,1,0:T(8,128)(2,1)S(1)} all-to-all(bf16[8,104,256]{2,1,0:T(8,128)(2,1)S(1)} %shard_map.60), channel_id=1, replica_groups=mesh['z'=8,'y'=4,'c'=2,'x'=4] {'z'}, dimensions={0} | all-to-all | bytes 851968 | tf_op jit(solution)/shard_map/all_to_all | solution.py:517
  154.6 3.9 %collective-permute-start.25 = (bf16[832,256]{1,0:T(8,128)(2,1)S(1)}, bf16[832,256]{1,0:T(8,128)(2,1)S(1)}, u32[]{:S(2)}, u32[]{:S(2)}) collective-permute-start(bf16[832,256]{1,0:T(8,128)(2,1)S(1)} %bitcast.9), channel_id=1, source_target_pairs={{24,0},{0,8},{8,16},{16,24},{25,1},{1,9},{9,17},{17,25},{26,2},{2,... | collective-permute-start | bytes 1277960 | tf_op jit(solution)/shard_map/ppermute | solution.py:501
  159.0 16.0 %all_to_all.29.refs_3_ = f32[32,1,256]{2,1,0:T(1,128)S(1)} all-to-all(f32[32,1,256]{2,1,0:T(1,128)S(1)} %shard_map.61), channel_id=1, replica_groups=mesh['z'=8,'y'=4,'c'=2,'x'=4] {'y','c','x'}, dimensions={0} | all-to-all | bytes 65536 | tf_op jit(solution)/shard_map/all_to_all | solution.py:517
  176.4 2.3 %collective-permute-start.30 = (bf16[416,256]{1,0:T(8,128)(2,1)S(1)}, bf16[416,256]{1,0:T(8,128)(2,1)S(1)}, u32[]{:S(2)}, u32[]{:S(2)}) collective-permute-start(bf16[416,256]{1,0:T(8,128)(2,1)S(1)} %slice.7), channel_id=1, source_target_pairs={{8,0},{16,8},{24,16},{0,24},{9,1},{17,9},{25,17},{1,25},{10,2},{18... | collective-permute-start | bytes 638984 | tf_op jit(solution)/shard_map/ppermute | solution.py:501
  179.2 6.2 %shard_map.62 = (bf16[256,6656]{1,0:T(8,128)(2,1)}, bf16[256,6656]{1,0:T(8,128)(2,1)}, f32[4,6656]{1,0:T(4,128)}) custom-call(s32[4]{0:T(128)S(1)} %pad_add_fusion.at_ref.refs_0_, bf16[256,6656]{1,0:T(8,128)(2,1)S(1)} %copy-done, f32[256,256]{1,0:T(8,128)S(1)} %shard_map.57.refs_2_, f32[32,1,256]{2,1,0:T(1,128)S(1)} %all_to_all.29.refs_3_, ...), custom_call_target="tpu_custom_call" | custom-call | flops 1308622848 | bytes 10223616 | tf_op jit(solution)/shard_map/pallas_call | solution.py:461
  185.4 0.8 collective-permute-start.31
  186.3 1.0 collective-permute-done.31.refs_12_
  187.7 3.2 %shard_map.63 = (bf16[256,6656]{1,0:T(8,128)(2,1)}, bf16[256,6656]{1,0:T(8,128)(2,1)}, f32[4,6656]{1,0:T(4,128)}) custom-call(s32[4]{0:T(128)S(1)} %pad_add_fusion.at_ref.refs_0_, bf16[256,6656]{1,0:T(8,128)(2,1)S(1)} %copy-done, f32[256,256]{1,0:T(8,128)S(1)} %shard_map.57.refs_2_, ...), custom_call_target="tpu_custom_call", output_to_operand_aliasing={{0}: (14, {}), {1}: (15, {}), {2}: (16, {})} | custom-call | flops 436207616 | bytes 3407872 | tf_op jit(solution)/shard_map/pallas_call | solution.py:479
  (50 shorter events, 6.2 us)
Async XLA Ops:
  1.7 5.5 %collective-permute-start = (bf16[4,3328]{1,0:T(4,128)(2,1)S(1)}, bf16[4,3328]{1,0:T(4,128)(2,1)S(1)}, u32[]{:S(2)}, u32[]{:S(2)}) collective-permute-start(bf16[4,3328]{1,0:T(4,128)(2,1)S(1)} %constant_dynamic-slice_fusion.2), channel_id=1, source_target_pairs={{0,4},{4,0},{1,5},{5,1},{2,6},{6,2},{3,7},{7,3},{8,12},{12,8},{9,1... | collective-permute-start | bytes 79880 | tf_op jit(solution)/shard_map/ppermute | solution.py:497
  7.1 42.5 %collective-permute-start.1 = (bf16[256,3328]{1,0:T(8,128)(2,1)S(1)}, bf16[256,3328]{1,0:T(8,128)(2,1)S(1)}, u32[]{:S(2)}, u32[]{:S(2)}) collective-permute-start(bf16[256,3328]{1,0:T(8,128)(2,1)S(1)} %get-tuple-element.38), channel_id=1, source_target_pairs={{0,4},{4,0},{1,5},{5,1},{2,6},{6,2},{3,7},{7,3},{8,12},{12,8},{9,1... | collective-permute-start | bytes 5111816 | tf_op jit(solution)/shard_map/ppermute | solution.py:497
  28.0 10.7 %collective-permute-start.4 = (bf16[64,3328]{1,0:T(8,128)(2,1)S(1)}, bf16[64,3328]{1,0:T(8,128)(2,1)S(1)}, u32[]{:S(2)}, u32[]{:S(2)}) collective-permute-start(bf16[64,3328]{1,0:T(8,128)(2,1)S(1)} %bitcast.15), channel_id=1, source_target_pairs={{24,0},{0,8},{8,16},{16,24},{25,1},{1,9},{9,17},{17,25},{26,2},{2,... | collective-permute-start | bytes 1277960 | tf_op jit(solution)/shard_map/ppermute | solution.py:501
  29.3 19.6 %collective-permute-start.3 = (bf16[64,3328]{1,0:T(8,128)(2,1)S(1)}, bf16[64,3328]{1,0:T(8,128)(2,1)S(1)}, u32[]{:S(2)}, u32[]{:S(2)}) collective-permute-start(bf16[64,3328]{1,0:T(8,128)(2,1)S(1)} %bitcast.16), channel_id=1, source_target_pairs={{16,0},{24,8},{0,16},{8,24},{17,1},{25,9},{1,17},{9,25},{18,2},{26... | collective-permute-start | bytes 1277960 | tf_op jit(solution)/shard_map/ppermute | solution.py:501
  31.9 17.8 %collective-permute-start.2 = (bf16[64,3328]{1,0:T(8,128)(2,1)S(1)}, bf16[64,3328]{1,0:T(8,128)(2,1)S(1)}, u32[]{:S(2)}, u32[]{:S(2)}) collective-permute-start(bf16[64,3328]{1,0:T(8,128)(2,1)S(1)} %bitcast.17), channel_id=1, source_target_pairs={{8,0},{16,8},{24,16},{0,24},{9,1},{17,9},{25,17},{1,25},{10,2},{18... | collective-permute-start | bytes 1277960 | tf_op jit(solution)/shard_map/ppermute | solution.py:501
  51.7 3.4 %collective-permute-start.5 = (f32[256,256]{1,0:T(8,128)S(1)}, f32[256,256]{1,0:T(8,128)S(1)}, u32[]{:S(2)}, u32[]{:S(2)}) collective-permute-start(f32[256,256]{1,0:T(8,128)S(1)} %get-tuple-element.41), channel_id=1, source_target_pairs={{0,4},{4,0},{1,5},{5,1},{2,6},{6,2},{3,7},{7,3},{8,12},{12,8},{9,1... | collective-permute-start | bytes 786440 | tf_op jit(solution)/shard_map/ppermute | solution.py:497
  55.7 4.9 %collective-permute-start.6 = (f32[64,256]{1,0:T(8,128)S(1)}, f32[64,256]{1,0:T(8,128)S(1)}, u32[]{:S(2)}, u32[]{:S(2)}) collective-permute-start(f32[64,256]{1,0:T(8,128)S(1)} %get-tuple-element.43), channel_id=1, source_target_pairs={{3,0},{0,1},{1,2},{2,3},{7,4},{4,5},{5,6},{6,7},{11,8},{8,9},{9,10... | collective-permute-start | bytes 196616 | tf_op jit(solution)/shard_map/ppermute | solution.py:501
  56.9 5.4 %collective-permute-start.7 = (f32[64,256]{1,0:T(8,128)S(1)}, f32[64,256]{1,0:T(8,128)S(1)}, u32[]{:S(2)}, u32[]{:S(2)}) collective-permute-start(f32[64,256]{1,0:T(8,128)S(1)} %get-tuple-element.44), channel_id=1, source_target_pairs={{2,0},{3,1},{0,2},{1,3},{6,4},{7,5},{4,6},{5,7},{10,8},{11,9},{8,1... | collective-permute-start | bytes 196616 | tf_op jit(solution)/shard_map/ppermute | solution.py:501
  59.4 3.4 %collective-permute-start.8 = (f32[64,256]{1,0:T(8,128)S(1)}, f32[64,256]{1,0:T(8,128)S(1)}, u32[]{:S(2)}, u32[]{:S(2)}) collective-permute-start(f32[64,256]{1,0:T(8,128)S(1)} %get-tuple-element.45), channel_id=1, source_target_pairs={{1,0},{2,1},{3,2},{0,3},{5,4},{6,5},{7,6},{4,7},{9,8},{10,9},{11,1... | collective-permute-start | bytes 196616 | tf_op jit(solution)/shard_map/ppermute | solution.py:501
  62.8 4.4 %collective-permute-start.11 = (f32[64,256]{1,0:T(8,128)S(1)}, f32[64,256]{1,0:T(8,128)S(1)}, u32[]{:S(2)}, u32[]{:S(2)}) collective-permute-start(f32[64,256]{1,0:T(8,128)S(1)} %bitcast.22), channel_id=1, source_target_pairs={{3,0},{0,1},{1,2},{2,3},{7,4},{4,5},{5,6},{6,7},{11,8},{8,9},{9,10... | collective-permute-start | bytes 196616 | tf_op jit(solution)/shard_map/ppermute | solution.py:501
  62.9 5.6 %collective-permute-start.10 = (f32[64,256]{1,0:T(8,128)S(1)}, f32[64,256]{1,0:T(8,128)S(1)}, u32[]{:S(2)}, u32[]{:S(2)}) collective-permute-start(f32[64,256]{1,0:T(8,128)S(1)} %bitcast.23), channel_id=1, source_target_pairs={{2,0},{3,1},{0,2},{1,3},{6,4},{7,5},{4,6},{5,7},{10,8},{11,9},{8,1... | collective-permute-start | bytes 196616 | tf_op jit(solution)/shard_map/ppermute | solution.py:501
  66.1 3.4 %collective-permute-start.9 = (f32[64,256]{1,0:T(8,128)S(1)}, f32[64,256]{1,0:T(8,128)S(1)}, u32[]{:S(2)}, u32[]{:S(2)}) collective-permute-start(f32[64,256]{1,0:T(8,128)S(1)} %bitcast.24), channel_id=1, source_target_pairs={{1,0},{2,1},{3,2},{0,3},{5,4},{6,5},{7,6},{4,7},{9,8},{10,9},{11,1... | collective-permute-start | bytes 196616 | tf_op jit(solution)/shard_map/ppermute | solution.py:501
  70.6 4.4 %collective-permute-start.12 = (f32[32,256]{1,0:T(8,128)S(1)}, f32[32,256]{1,0:T(8,128)S(1)}, u32[]{:S(2)}, u32[]{:S(2)}) collective-permute-start(f32[32,256]{1,0:T(8,128)S(1)} %get-tuple-element.47), channel_id=1, source_target_pairs={{0,4},{4,0},{1,5},{5,1},{2,6},{6,2},{3,7},{7,3},{8,12},{12,8},{9,1... | collective-permute-start | bytes 98312 | tf_op jit(solution)/shard_map/ppermute | solution.py:497
  75.0 4.7 %collective-permute-start.20 = (f32[256,256]{1,0:T(8,128)S(1)}, f32[256,256]{1,0:T(8,128)S(1)}, u32[]{:S(2)}, u32[]{:S(2)}) collective-permute-start(f32[256,256]{1,0:T(8,128)S(1)} %get-tuple-element.50.refs_0_.left_mine_ref), channel_id=1, source_target_pairs={{0,4},{4,0},{1,5},{5,1},{2,6},{6,2},{3,7},{7,3},{8,12},{12,8},{9,1... | collective-permute-start | bytes 786440 | tf_op jit(solution)/shard_map/ppermute | solution.py:497
  75.4 9.6 %collective-permute-start.15 = (f32[32,256]{1,0:T(8,128)S(1)}, f32[32,256]{1,0:T(8,128)S(1)}, u32[]{:S(2)}, u32[]{:S(2)}) collective-permute-start(f32[32,256]{1,0:T(8,128)S(1)} %shard_map.53.own_ref), channel_id=1, source_target_pairs={{24,0},{0,8},{8,16},{16,24},{25,1},{1,9},{9,17},{17,25},{26,2},{2,... | collective-permute-start | bytes 98312 | tf_op jit(solution)/shard_map/ppermute | solution.py:501
  76.2 10.3 %collective-permute-start.14 = (f32[32,256]{1,0:T(8,128)S(1)}, f32[32,256]{1,0:T(8,128)S(1)}, u32[]{:S(2)}, u32[]{:S(2)}) collective-permute-start(f32[32,256]{1,0:T(8,128)S(1)} %shard_map.53.own_ref), channel_id=1, source_target_pairs={{16,0},{24,8},{0,16},{8,24},{17,1},{25,9},{1,17},{9,25},{18,2},{26... | collective-permute-start | bytes 98312 | tf_op jit(solution)/shard_map/ppermute | solution.py:501
  78.3 8.2 %collective-permute-start.13 = (f32[32,256]{1,0:T(8,128)S(1)}, f32[32,256]{1,0:T(8,128)S(1)}, u32[]{:S(2)}, u32[]{:S(2)}) collective-permute-start(f32[32,256]{1,0:T(8,128)S(1)} %shard_map.53.own_ref), channel_id=1, source_target_pairs={{8,0},{16,8},{24,16},{0,24},{9,1},{17,9},{25,17},{1,25},{10,2},{18... | collective-permute-start | bytes 98312 | tf_op jit(solution)/shard_map/ppermute | solution.py:501
  83.7 37.5 %collective-permute-start.21 = (f32[832,256]{1,0:T(8,128)S(1)}, f32[832,256]{1,0:T(8,128)S(1)}, u32[]{:S(2)}, u32[]{:S(2)}) collective-permute-start(f32[832,256]{1,0:T(8,128)S(1)} %get-tuple-element.52), channel_id=1, source_target_pairs={{24,0},{0,8},{8,16},{16,24},{25,1},{1,9},{9,17},{17,25},{26,2},{2,... | collective-permute-start | bytes 2555912 | tf_op jit(solution)/shard_map/ppermute | solution.py:501
  83.9 37.7 %collective-permute-start.22 = (f32[832,256]{1,0:T(8,128)S(1)}, f32[832,256]{1,0:T(8,128)S(1)}, u32[]{:S(2)}, u32[]{:S(2)}) collective-permute-start(f32[832,256]{1,0:T(8,128)S(1)} %get-tuple-element.53), channel_id=1, source_target_pairs={{16,0},{24,8},{0,16},{8,24},{17,1},{25,9},{1,17},{9,25},{18,2},{26... | collective-permute-start | bytes 2555912 | tf_op jit(solution)/shard_map/ppermute | solution.py:501
  85.0 38.3 %collective-permute-start.23 = (f32[832,256]{1,0:T(8,128)S(1)}, f32[832,256]{1,0:T(8,128)S(1)}, u32[]{:S(2)}, u32[]{:S(2)}) collective-permute-start(f32[832,256]{1,0:T(8,128)S(1)} %get-tuple-element.54), channel_id=1, source_target_pairs={{8,0},{16,8},{24,16},{0,24},{9,1},{17,9},{25,17},{1,25},{10,2},{18... | collective-permute-start | bytes 2555912 | tf_op jit(solution)/shard_map/ppermute | solution.py:501
  98.2 4.6 %collective-permute-start.16 = (f32[32,256]{1,0:T(8,128)S(1)}, f32[32,256]{1,0:T(8,128)S(1)}, u32[]{:S(2)}, u32[]{:S(2)}) collective-permute-start(f32[32,256]{1,0:T(8,128)S(1)} %bitcast.20), channel_id=1, source_target_pairs={{0,4},{4,0},{1,5},{5,1},{2,6},{6,2},{3,7},{7,3},{8,12},{12,8},{9,1... | collective-permute-start | bytes 98312 | tf_op jit(solution)/shard_map/ppermute | solution.py:497
  102.8 5.1 %collective-permute-start.19 = (f32[64,256]{1,0:T(8,128)S(1)}, f32[64,256]{1,0:T(8,128)S(1)}, u32[]{:S(2)}, u32[]{:S(2)}) collective-permute-start(f32[64,256]{1,0:T(8,128)S(1)} %pad_maximum_fusion.own_ref), channel_id=1, source_target_pairs={{3,0},{0,1},{1,2},{2,3},{7,4},{4,5},{5,6},{6,7},{11,8},{8,9},{9,10... | collective-permute-start | bytes 196616 | tf_op jit(solution)/shard_map/ppermute | solution.py:501
  102.8 5.8 %collective-permute-start.18 = (f32[64,256]{1,0:T(8,128)S(1)}, f32[64,256]{1,0:T(8,128)S(1)}, u32[]{:S(2)}, u32[]{:S(2)}) collective-permute-start(f32[64,256]{1,0:T(8,128)S(1)} %pad_maximum_fusion.own_ref), channel_id=1, source_target_pairs={{2,0},{3,1},{0,2},{1,3},{6,4},{7,5},{4,6},{5,7},{10,8},{11,9},{8,1... | collective-permute-start | bytes 196616 | tf_op jit(solution)/shard_map/ppermute | solution.py:501
  107.9 3.4 %collective-permute-start.17 = (f32[64,256]{1,0:T(8,128)S(1)}, f32[64,256]{1,0:T(8,128)S(1)}, u32[]{:S(2)}, u32[]{:S(2)}) collective-permute-start(f32[64,256]{1,0:T(8,128)S(1)} %pad_maximum_fusion.own_ref), channel_id=1, source_target_pairs={{1,0},{2,1},{3,2},{0,3},{5,4},{6,5},{7,6},{4,7},{9,8},{10,9},{11,1... | collective-permute-start | bytes 196616 | tf_op jit(solution)/shard_map/ppermute | solution.py:501
  123.3 55.9 %copy-start = (bf16[256,6656]{1,0:T(8,128)(2,1)S(1)}, bf16[256,6656]{1,0:T(8,128)(2,1)}, u32[]{:S(2)}) copy-start(bf16[256,6656]{1,0:T(8,128)(2,1)} %refs_1_.3) | copy-start | bytes 10223620
  154.6 20.4 %collective-permute-start.25 = (bf16[832,256]{1,0:T(8,128)(2,1)S(1)}, bf16[832,256]{1,0:T(8,128)(2,1)S(1)}, u32[]{:S(2)}, u32[]{:S(2)}) collective-permute-start(bf16[832,256]{1,0:T(8,128)(2,1)S(1)} %bitcast.9), channel_id=1, source_target_pairs={{24,0},{0,8},{8,16},{16,24},{25,1},{1,9},{9,17},{17,25},{26,2},{2,... | collective-permute-start | bytes 1277960 | tf_op jit(solution)/shard_map/ppermute | solution.py:501
  158.5 16.5 %collective-permute-start.24 = (bf16[832,256]{1,0:T(8,128)(2,1)S(1)}, bf16[832,256]{1,0:T(8,128)(2,1)S(1)}, u32[]{:S(2)}, u32[]{:S(2)}) collective-permute-start(bf16[832,256]{1,0:T(8,128)(2,1)S(1)} %bitcast.10), channel_id=1, source_target_pairs={{8,0},{16,8},{24,16},{0,24},{9,1},{17,9},{25,17},{1,25},{10,2},{18... | collective-permute-start | bytes 1277960 | tf_op jit(solution)/shard_map/ppermute | solution.py:501
  175.0 4.1 %collective-permute-start.26 = (bf16[832,256]{1,0:T(8,128)(2,1)S(1)}, bf16[832,256]{1,0:T(8,128)(2,1)S(1)}, u32[]{:S(2)}, u32[]{:S(2)}) collective-permute-start(bf16[832,256]{1,0:T(8,128)(2,1)S(1)} %bitcast.12), channel_id=1, source_target_pairs={{0,4},{4,0},{1,5},{5,1},{2,6},{6,2},{3,7},{7,3},{8,12},{12,8},{9,1... | collective-permute-start | bytes 1277960 | tf_op jit(solution)/shard_map/ppermute | solution.py:497
  175.4 3.7 %collective-permute-start.27 = (bf16[832,256]{1,0:T(8,128)(2,1)S(1)}, bf16[832,256]{1,0:T(8,128)(2,1)S(1)}, u32[]{:S(2)}, u32[]{:S(2)}) collective-permute-start(bf16[832,256]{1,0:T(8,128)(2,1)S(1)} %collective-permute-done.24.refs_5_), channel_id=1, source_target_pairs={{0,4},{4,0},{1,5},{5,1},{2,6},{6,2},{3,7},{7,3},{8,12},{12,8},{9,1... | collective-permute-start | bytes 1277960 | tf_op jit(solution)/shard_map/ppermute | solution.py:497
  175.5 3.6 %collective-permute-start.28 = (bf16[832,256]{1,0:T(8,128)(2,1)S(1)}, bf16[832,256]{1,0:T(8,128)(2,1)S(1)}, u32[]{:S(2)}, u32[]{:S(2)}) collective-permute-start(bf16[832,256]{1,0:T(8,128)(2,1)S(1)} %collective-permute-done.25.refs_6_), channel_id=1, source_target_pairs={{0,4},{4,0},{1,5},{5,1},{2,6},{6,2},{3,7},{7,3},{8,12},{12,8},{9,1... | collective-permute-start | bytes 1277960 | tf_op jit(solution)/shard_map/ppermute | solution.py:497
  176.0 9.4 %collective-permute-start.29 = (bf16[416,256]{1,0:T(8,128)(2,1)S(1)}, bf16[416,256]{1,0:T(8,128)(2,1)S(1)}, u32[]{:S(2)}, u32[]{:S(2)}) collective-permute-start(bf16[416,256]{1,0:T(8,128)(2,1)S(1)} %slice.6), channel_id=1, source_target_pairs={{24,0},{0,8},{8,16},{16,24},{25,1},{1,9},{9,17},{17,25},{26,2},{2,... | collective-permute-start | bytes 638984 | tf_op jit(solution)/shard_map/ppermute | solution.py:501
  176.4 9.0 %collective-permute-start.30 = (bf16[416,256]{1,0:T(8,128)(2,1)S(1)}, bf16[416,256]{1,0:T(8,128)(2,1)S(1)}, u32[]{:S(2)}, u32[]{:S(2)}) collective-permute-start(bf16[416,256]{1,0:T(8,128)(2,1)S(1)} %slice.7), channel_id=1, source_target_pairs={{8,0},{16,8},{24,16},{0,24},{9,1},{17,9},{25,17},{1,25},{10,2},{18... | collective-permute-start | bytes 638984 | tf_op jit(solution)/shard_map/ppermute | solution.py:501
  185.4 1.9 collective-permute-start.31
  186.2 1.5 collective-permute-start.32
